TPU v7x, 32 devices: a whole 2x2x4 slice. The times are simulated.
32 devices in a mesh: gx: 2 (over y), gy: 4 (over z), gz: 4 (over x, core).
Axes of the slice: x: 2, y: 2, z: 4, core: 2. Of those that a mesh axis runs over, the one named last changes fastest.
Arguments:
- divergence: float32 [64, 32, 512], P('gz', 'gx', 'gy'), may hold values from -6 to 6
- pressure_prev: float32 [64, 32, 512], P('gz', 'gx', 'gy'), may hold values from -6 to 6
Outputs:
- pressure: float32 [64, 32, 512], P('gz', 'gx', 'gy')
- residual: float32 [64, 32, 512], P('gz', 'gx', 'gy')
- coarse_correction: float32 [2, 1, 16], replicated
All inputs are finite; a program needn't handle non-finite values.
Results may differ from a plain program's by a relative error of at most 0.0004.
Values sent between devices are 32-bit elements; how exact they have to be, the bound alone decides.
No kernel may reach another device: no remote copies, remote signals or barrier semaphores. Data moves between devices by JAX's collectives and lax.ppermute only.
A program may use at most 64 MiB of HBM per device.

v0:
```python
import jax
import jax.numpy as jnp
from jax import lax
from jax.sharding import PartitionSpec as P

LEVELS = 6


first_scale = 1.0 / 7.5
rho_one = 1.0 / (2.0 * (5.0 / 3.0) - 0.6)
carry_coef = 0.6 * rho_one
fresh_coef = 2.0 * rho_one / (0.75 * 6.0)


def extended(x, sides, width):
    for axis, dim in sides:
        peers, length = (lax.axis_size(axis), x.shape[dim])
        up = [(i, (i + 1) % peers) for i in range(peers - 1)]
        down = [(j, i) for i, j in up]
        last = lax.slice_in_dim(x, length - width, length, axis=dim)
        first = lax.slice_in_dim(x, 0, width, axis=dim)
        before = lax.ppermute(last, axis, up)
        after = lax.ppermute(first, axis, down)
        x = jnp.concatenate([before, x, after], axis=dim)
    return x


def stencil(values):
    padded = jnp.pad(values, 1)
    beside = padded[2:, 1:-1, 1:-1] + padded[:-2, 1:-1, 1:-1]
    beside = beside + padded[1:-1, 2:, 1:-1] + padded[1:-1, :-2, 1:-1]
    beside = beside + padded[1:-1, 1:-1, 2:] + padded[1:-1, 1:-1, :-2]
    return 6.0 * values - beside


def valid_op(padded):
    beside = padded[2:, 1:-1, 1:-1] + padded[:-2, 1:-1, 1:-1]
    beside = beside + padded[1:-1, 2:, 1:-1] + padded[1:-1, :-2, 1:-1]
    beside = beside + padded[1:-1, 1:-1, 2:] + padded[1:-1, 1:-1, :-2]
    return 6.0 * padded[1:-1, 1:-1, 1:-1] - beside


def local_stencil(values):
    padded = extended(values, (("gz", 0), ("gx", 1), ("gy", 2)), 1)
    return valid_op(padded)


def smooth_pass(iterate, source, apply_op, from_zero):
    residue = source if from_zero else source - apply_op(iterate)
    update = residue * first_scale
    iterate = update if from_zero else iterate + update
    residue = source - apply_op(iterate)
    update = carry_coef * update + fresh_coef * residue
    return iterate + update


def restrict(values):
    shape_a, shape_b, shape_c = values.shape
    blocks = values.reshape(shape_a // 2, 2, shape_b // 2, 2, shape_c // 2, 2)
    return 0.5 * jnp.sum(blocks, axis=(1, 3, 5))


def prolong(values):
    shape_a, shape_b, shape_c = values.shape
    spread = jnp.broadcast_to(
        values[:, None, :, None, :, None], (shape_a, 2, shape_b, 2, shape_c, 2)
    )
    return spread.reshape(2 * shape_a, 2 * shape_b, 2 * shape_c)


def vcycle(level_num, iterate, source):
    iterate = smooth_pass(iterate, source, stencil, True)
    coarsest = None
    if level_num < LEVELS - 1:
        residue = source - stencil(iterate)
        coarse, coarsest = vcycle(level_num + 1, None, restrict(residue))
        iterate = iterate + prolong(coarse)
    result = smooth_pass(iterate, source, stencil, False)
    if level_num == LEVELS - 1:
        coarsest = result
    return (result, coarsest)


def collect(values):
    gathered = lax.all_gather(values, "gz", axis=0, tiled=True)
    gathered = lax.all_gather(gathered, "gy", axis=2, tiled=True)
    return lax.all_gather(gathered, "gx", axis=1, tiled=True)


def own_block(whole, block_shape):
    start_z = lax.axis_index("gz") * block_shape[0]
    start_x = lax.axis_index("gx") * block_shape[1]
    start_y = lax.axis_index("gy") * block_shape[2]
    return lax.dynamic_slice(whole, (start_z, start_x, start_y), block_shape)


def body_cycle(level_num, iterate, source, from_zero, gather_at):
    if level_num == gather_at:
        whole_source = collect(source)
        coarse, coarsest = vcycle(level_num, None, whole_source)
        return (own_block(coarse, source.shape), coarsest)
    iterate = smooth_pass(iterate, source, local_stencil, from_zero)
    residue = source - local_stencil(iterate)
    coarse, coarsest = body_cycle(level_num + 1, None, restrict(residue), True, gather_at)
    iterate = iterate + prolong(coarse)
    return (smooth_pass(iterate, source, local_stencil, False), coarsest)


def body(divergence, pressure_prev):
    gather_at = 3
    pressure, coarse_correction = body_cycle(0, pressure_prev, divergence, False, gather_at)
    residual = divergence - local_stencil(pressure)
    return (pressure, residual, coarse_correction)


def solution(mesh):
    in_specs = (P("gz", "gx", "gy"), P("gz", "gx", "gy"))
    out_specs = (P("gz", "gx", "gy"), P("gz", "gx", "gy"), P())
    return jax.shard_map(body, mesh=mesh, in_specs=in_specs, out_specs=out_specs, check_vma=False)
```

profile of v0, /device:TPU:30, one launch (start us, length us, event | category | flops | bytes accessed | tf_op | source)
XLA Modules:
  0.0 386.0 jit_solution(14885988374868531672)
XLA Ops:
  12.1 4.2 %collective-permute-done.3 = f32[18,1,128]{2,1,0:T(1,128)S(1)} collective-permute-done((f32[18,1,128]{2,1,0:T(1,128)S(1)}, f32[18,1,128]{2,1,0:T(1,128)S(1)}, u32[]{:S(2)}, u32[]{:S(2)}) %collective-permute-start.3) | collective-permute-done | bytes 9248 | tf_op jit(solution)/shard_map/ppermute | solution.py:22
  22.2 4.4 %collective-permute-done.5 = f32[18,18,1]{2,1,0:T(8,128)S(1)} collective-permute-done((f32[18,18,1]{2,1,0:T(8,128)S(1)}, f32[18,18,1]{2,1,0:T(8,128)S(1)}, u32[]{:S(2)}, u32[]{:S(2)}) %collective-permute-start.5) | collective-permute-done | bytes 1328 | tf_op jit(solution)/shard_map/ppermute | solution.py:22
  39.6 4.2 %collective-permute-done.9 = f32[18,1,128]{2,1,0:T(1,128)S(1)} collective-permute-done((f32[18,1,128]{2,1,0:T(1,128)S(1)}, f32[18,1,128]{2,1,0:T(1,128)S(1)}, u32[]{:S(2)}, u32[]{:S(2)}) %collective-permute-start.9) | collective-permute-done | bytes 9248 | tf_op jit(solution)/shard_map/ppermute | solution.py:22
  49.8 4.4 %collective-permute-done.11 = f32[18,18,1]{2,1,0:T(8,128)S(1)} collective-permute-done((f32[18,18,1]{2,1,0:T(8,128)S(1)}, f32[18,18,1]{2,1,0:T(8,128)S(1)}, u32[]{:S(2)}, u32[]{:S(2)}) %collective-permute-start.11) | collective-permute-done | bytes 1328 | tf_op jit(solution)/shard_map/ppermute | solution.py:22
  65.2 4.2 %collective-permute-done.15 = f32[18,1,128]{2,1,0:T(1,128)S(1)} collective-permute-done((f32[18,1,128]{2,1,0:T(1,128)S(1)}, f32[18,1,128]{2,1,0:T(1,128)S(1)}, u32[]{:S(2)}, u32[]{:S(2)}) %collective-permute-start.15) | collective-permute-done | bytes 9248 | tf_op jit(solution)/shard_map/ppermute | solution.py:22
  75.4 4.4 %collective-permute-done.17 = f32[18,18,1]{2,1,0:T(8,128)S(1)} collective-permute-done((f32[18,18,1]{2,1,0:T(8,128)S(1)}, f32[18,18,1]{2,1,0:T(8,128)S(1)}, u32[]{:S(2)}, u32[]{:S(2)}) %collective-permute-start.17) | collective-permute-done | bytes 1328 | tf_op jit(solution)/shard_map/ppermute | solution.py:22
  80.9 9.8 %reshape.80 = f32[8,2,8,2,64,2]{5,4,3,2,1,0:T(8,128)} reshape(f32[16,16,128]{2,1,0:T(8,128)S(1)} %fusion.26) | data formatting | bytes 262144 | tf_op jit(solution)/shard_map/reshape | solution.py:59
  112.9 4.3 %collective-permute-done.23 = f32[10,10,1]{2,1,0:T(8,128)S(1)} collective-permute-done((f32[10,10,1]{2,1,0:T(8,128)S(1)}, f32[10,10,1]{2,1,0:T(8,128)S(1)}, u32[]{:S(2)}, u32[]{:S(2)}) %collective-permute-start.23) | collective-permute-done | bytes 432 | tf_op jit(solution)/shard_map/ppermute | solution.py:22
  135.4 4.3 %collective-permute-done.29 = f32[10,10,1]{2,1,0:T(8,128)S(1)} collective-permute-done((f32[10,10,1]{2,1,0:T(8,128)S(1)}, f32[10,10,1]{2,1,0:T(8,128)S(1)}, u32[]{:S(2)}, u32[]{:S(2)}) %collective-permute-start.29) | collective-permute-done | bytes 432 | tf_op jit(solution)/shard_map/ppermute | solution.py:22
  158.6 4.2 %collective-permute-done.35 = f32[6,6,1]{2,1,0:T(8,128)S(1)} collective-permute-done((f32[6,6,1]{2,1,0:T(8,128)S(1)}, f32[6,6,1]{2,1,0:T(8,128)S(1)}, u32[]{:S(2)}, u32[]{:S(2)}) %collective-permute-start.35) | collective-permute-done | bytes 176 | tf_op jit(solution)/shard_map/ppermute | solution.py:22
  180.4 4.2 %collective-permute-done.41 = f32[6,6,1]{2,1,0:T(8,128)S(1)} collective-permute-done((f32[6,6,1]{2,1,0:T(8,128)S(1)}, f32[6,6,1]{2,1,0:T(8,128)S(1)}, u32[]{:S(2)}, u32[]{:S(2)}) %collective-permute-start.41) | collective-permute-done | bytes 176 | tf_op jit(solution)/shard_map/ppermute | solution.py:22
  185.0 5.2 %all_gather.9 = f32[8,2,16]{2,1,0:T(2,128)S(1)} all-gather(f32[2,2,16]{2,1,0:T(2,128)S(1)} %broadcast_multiply_fusion.4), channel_id=1, replica_groups=mesh['gx'=2,'gy'=4,'gz'=4] {'gz'}, dimensions={0}, use_global_device_ids=true | all-gather | bytes 1280 | tf_op jit(solution)/shard_map/all_gather | solution.py:85
  190.2 13.1 %all_gather.10 = f32[8,2,64]{0,1,2:T(2,128)S(1)} all-gather(f32[8,2,16]{0,1,2:T(2,128)S(1)} %copy.8), channel_id=1, replica_groups=mesh['gx'=2,'gy'=4,'gz'=4] {'gy'}, dimensions={2}, use_global_device_ids=true | all-gather | bytes 5120 | tf_op jit(solution)/shard_map/all_gather | solution.py:86
  203.4 4.4 %all_gather.11 = f32[8,4,64]{2,0,1:T(8,128)S(1)} all-gather(f32[8,2,64]{2,0,1:T(8,128)S(1)} %copy.9), channel_id=1, replica_groups=mesh['gx'=2,'gy'=4,'gz'=4] {'gx'}, dimensions={1}, use_global_device_ids=true | all-gather | bytes 12288 | tf_op jit(solution)/shard_map/all_gather | solution.py:87
  227.7 4.2 %collective-permute-done.47 = f32[6,6,1]{2,1,0:T(8,128)S(1)} collective-permute-done((f32[6,6,1]{2,1,0:T(8,128)S(1)}, f32[6,6,1]{2,1,0:T(8,128)S(1)}, u32[]{:S(2)}, u32[]{:S(2)}) %collective-permute-start.47) | collective-permute-done | bytes 176 | tf_op jit(solution)/shard_map/ppermute | solution.py:22
  251.2 4.2 %collective-permute-done.53 = f32[6,6,1]{2,1,0:T(8,128)S(1)} collective-permute-done((f32[6,6,1]{2,1,0:T(8,128)S(1)}, f32[6,6,1]{2,1,0:T(8,128)S(1)}, u32[]{:S(2)}, u32[]{:S(2)}) %collective-permute-start.53) | collective-permute-done | bytes 176 | tf_op jit(solution)/shard_map/ppermute | solution.py:22
  274.6 4.3 %collective-permute-done.59 = f32[10,10,1]{2,1,0:T(8,128)S(1)} collective-permute-done((f32[10,10,1]{2,1,0:T(8,128)S(1)}, f32[10,10,1]{2,1,0:T(8,128)S(1)}, u32[]{:S(2)}, u32[]{:S(2)}) %collective-permute-start.59) | collective-permute-done | bytes 432 | tf_op jit(solution)/shard_map/ppermute | solution.py:22
  297.2 4.3 %collective-permute-done.65 = f32[10,10,1]{2,1,0:T(8,128)S(1)} collective-permute-done((f32[10,10,1]{2,1,0:T(8,128)S(1)}, f32[10,10,1]{2,1,0:T(8,128)S(1)}, u32[]{:S(2)}, u32[]{:S(2)}) %collective-permute-start.65) | collective-permute-done | bytes 432 | tf_op jit(solution)/shard_map/ppermute | solution.py:22
  305.6 6.9 %reshape.87 = f32[16,16,128]{2,1,0:T(8,128)S(1)} reshape(f32[8,2,8,2,64,2]{5,4,3,2,1,0:T(8,128)} %broadcast_in_dim.43) | data formatting | bytes 262144 | tf_op jit(solution)/shard_map/reshape | solution.py:68
  322.4 4.2 %collective-permute-done.69 = f32[18,1,128]{2,1,0:T(1,128)S(1)} collective-permute-done((f32[18,1,128]{2,1,0:T(1,128)S(1)}, f32[18,1,128]{2,1,0:T(1,128)S(1)}, u32[]{:S(2)}, u32[]{:S(2)}) %collective-permute-start.69) | collective-permute-done | bytes 9248 | tf_op jit(solution)/shard_map/ppermute | solution.py:22
  332.2 4.4 %collective-permute-done.71 = f32[18,18,1]{2,1,0:T(8,128)S(1)} collective-permute-done((f32[18,18,1]{2,1,0:T(8,128)S(1)}, f32[18,18,1]{2,1,0:T(8,128)S(1)}, u32[]{:S(2)}, u32[]{:S(2)}) %collective-permute-start.71) | collective-permute-done | bytes 1328 | tf_op jit(solution)/shard_map/ppermute | solution.py:22
  346.7 4.2 %collective-permute-done.75 = f32[18,1,128]{2,1,0:T(1,128)S(1)} collective-permute-done((f32[18,1,128]{2,1,0:T(1,128)S(1)}, f32[18,1,128]{2,1,0:T(1,128)S(1)}, u32[]{:S(2)}, u32[]{:S(2)}) %collective-permute-start.75) | collective-permute-done | bytes 9248 | tf_op jit(solution)/shard_map/ppermute | solution.py:22
  356.4 4.4 %collective-permute-done.77 = f32[18,18,1]{2,1,0:T(8,128)S(1)} collective-permute-done((f32[18,18,1]{2,1,0:T(8,128)S(1)}, f32[18,18,1]{2,1,0:T(8,128)S(1)}, u32[]{:S(2)}, u32[]{:S(2)}) %collective-permute-start.77) | collective-permute-done | bytes 1328 | tf_op jit(solution)/shard_map/ppermute | solution.py:22
  380.7 4.4 %collective-permute-done.83 = f32[18,18,1]{2,1,0:T(8,128)S(1)} collective-permute-done((f32[18,18,1]{2,1,0:T(8,128)S(1)}, f32[18,18,1]{2,1,0:T(8,128)S(1)}, u32[]{:S(2)}, u32[]{:S(2)}) %collective-permute-start.83) | collective-permute-done | bytes 1328 | tf_op jit(solution)/shard_map/ppermute | solution.py:22
  (273 shorter events, 263.2 us)
Async XLA Ops:
  1.3 5.6 %collective-permute-start.1 = (f32[1,16,128]{2,1,0:T(8,128)S(1)}, f32[1,16,128]{2,1,0:T(8,128)S(1)}, u32[]{:S(2)}, u32[]{:S(2)}) collective-permute-start(f32[1,16,128]{2,1,0:T(8,128)S(1)} %get-tuple-element.61), channel_id=1, source_target_pairs={{0,1},{1,2},{2,3},{4,5},{5,6},{6,7},{8,9},{9,10},{10,11},{12,13},{... | collective-permute-start | bytes 24584 | tf_op jit(solution)/shard_map/ppermute | solution.py:22
  10.7 5.6 %collective-permute-start.3 = (f32[18,1,128]{2,1,0:T(1,128)S(1)}, f32[18,1,128]{2,1,0:T(1,128)S(1)}, u32[]{:S(2)}, u32[]{:S(2)}) collective-permute-start(f32[18,1,128]{2,1,0:T(1,128)S(1)} %get-tuple-element.48), channel_id=1, source_target_pairs={{0,16},{1,17},{2,18},{3,19},{4,20},{5,21},{6,22},{7,23},{8,24},{9,... | collective-permute-start | bytes 27656 | tf_op jit(solution)/shard_map/ppermute | solution.py:22
  16.4 5.8 %collective-permute-start.4 = (f32[18,18,1]{2,1,0:T(8,128)S(1)}, f32[18,18,1]{2,1,0:T(8,128)S(1)}, u32[]{:S(2)}, u32[]{:S(2)}) collective-permute-start(f32[18,18,1]{2,1,0:T(8,128)S(1)} %get-tuple-element.36), channel_id=1, source_target_pairs={{4,0},{8,4},{12,8},{5,1},{9,5},{13,9},{6,2},{10,6},{14,10},{7,3},{... | collective-permute-start | bytes 3896 | tf_op jit(solution)/shard_map/ppermute | solution.py:23
  18.8 7.8 %collective-permute-start.5 = (f32[18,18,1]{2,1,0:T(8,128)S(1)}, f32[18,18,1]{2,1,0:T(8,128)S(1)}, u32[]{:S(2)}, u32[]{:S(2)}) collective-permute-start(f32[18,18,1]{2,1,0:T(8,128)S(1)} %get-tuple-element.37), channel_id=1, source_target_pairs={{0,4},{4,8},{8,12},{1,5},{5,9},{9,13},{2,6},{6,10},{10,14},{3,7},{... | collective-permute-start | bytes 3896 | tf_op jit(solution)/shard_map/ppermute | solution.py:22
  38.3 5.6 %collective-permute-start.9 = (f32[18,1,128]{2,1,0:T(1,128)S(1)}, f32[18,1,128]{2,1,0:T(1,128)S(1)}, u32[]{:S(2)}, u32[]{:S(2)}) collective-permute-start(f32[18,1,128]{2,1,0:T(1,128)S(1)} %get-tuple-element.46), channel_id=1, source_target_pairs={{0,16},{1,17},{2,18},{3,19},{4,20},{5,21},{6,22},{7,23},{8,24},{9,... | collective-permute-start | bytes 27656 | tf_op jit(solution)/shard_map/ppermute | solution.py:22
  44.0 5.8 %collective-permute-start.10 = (f32[18,18,1]{2,1,0:T(8,128)S(1)}, f32[18,18,1]{2,1,0:T(8,128)S(1)}, u32[]{:S(2)}, u32[]{:S(2)}) collective-permute-start(f32[18,18,1]{2,1,0:T(8,128)S(1)} %get-tuple-element.34), channel_id=1, source_target_pairs={{4,0},{8,4},{12,8},{5,1},{9,5},{13,9},{6,2},{10,6},{14,10},{7,3},{... | collective-permute-start | bytes 3896 | tf_op jit(solution)/shard_map/ppermute | solution.py:23
  46.4 7.8 %collective-permute-start.11 = (f32[18,18,1]{2,1,0:T(8,128)S(1)}, f32[18,18,1]{2,1,0:T(8,128)S(1)}, u32[]{:S(2)}, u32[]{:S(2)}) collective-permute-start(f32[18,18,1]{2,1,0:T(8,128)S(1)} %get-tuple-element.35), channel_id=1, source_target_pairs={{0,4},{4,8},{8,12},{1,5},{5,9},{9,13},{2,6},{6,10},{10,14},{3,7},{... | collective-permute-start | bytes 3896 | tf_op jit(solution)/shard_map/ppermute | solution.py:22
  63.9 5.6 %collective-permute-start.15 = (f32[18,1,128]{2,1,0:T(1,128)S(1)}, f32[18,1,128]{2,1,0:T(1,128)S(1)}, u32[]{:S(2)}, u32[]{:S(2)}) collective-permute-start(f32[18,1,128]{2,1,0:T(1,128)S(1)} %get-tuple-element.44), channel_id=1, source_target_pairs={{0,16},{1,17},{2,18},{3,19},{4,20},{5,21},{6,22},{7,23},{8,24},{9,... | collective-permute-start | bytes 27656 | tf_op jit(solution)/shard_map/ppermute | solution.py:22
  69.6 5.8 %collective-permute-start.16 = (f32[18,18,1]{2,1,0:T(8,128)S(1)}, f32[18,18,1]{2,1,0:T(8,128)S(1)}, u32[]{:S(2)}, u32[]{:S(2)}) collective-permute-start(f32[18,18,1]{2,1,0:T(8,128)S(1)} %get-tuple-element.32), channel_id=1, source_target_pairs={{4,0},{8,4},{12,8},{5,1},{9,5},{13,9},{6,2},{10,6},{14,10},{7,3},{... | collective-permute-start | bytes 3896 | tf_op jit(solution)/shard_map/ppermute | solution.py:23
  72.0 7.8 %collective-permute-start.17 = (f32[18,18,1]{2,1,0:T(8,128)S(1)}, f32[18,18,1]{2,1,0:T(8,128)S(1)}, u32[]{:S(2)}, u32[]{:S(2)}) collective-permute-start(f32[18,18,1]{2,1,0:T(8,128)S(1)} %get-tuple-element.33), channel_id=1, source_target_pairs={{0,4},{4,8},{8,12},{1,5},{5,9},{9,13},{2,6},{6,10},{10,14},{3,7},{... | collective-permute-start | bytes 3896 | tf_op jit(solution)/shard_map/ppermute | solution.py:22
  110.8 6.3 %collective-permute-start.23 = (f32[10,10,1]{2,1,0:T(8,128)S(1)}, f32[10,10,1]{2,1,0:T(8,128)S(1)}, u32[]{:S(2)}, u32[]{:S(2)}) collective-permute-start(f32[10,10,1]{2,1,0:T(8,128)S(1)} %get-tuple-element.69), channel_id=1, source_target_pairs={{0,4},{4,8},{8,12},{1,5},{5,9},{9,13},{2,6},{6,10},{10,14},{3,7},{... | collective-permute-start | bytes 1208 | tf_op jit(solution)/shard_map/ppermute | solution.py:22
  133.4 6.3 %collective-permute-start.29 = (f32[10,10,1]{2,1,0:T(8,128)S(1)}, f32[10,10,1]{2,1,0:T(8,128)S(1)}, u32[]{:S(2)}, u32[]{:S(2)}) collective-permute-start(f32[10,10,1]{2,1,0:T(8,128)S(1)} %get-tuple-element.67), channel_id=1, source_target_pairs={{0,4},{4,8},{8,12},{1,5},{5,9},{9,13},{2,6},{6,10},{10,14},{3,7},{... | collective-permute-start | bytes 1208 | tf_op jit(solution)/shard_map/ppermute | solution.py:22
  157.1 5.7 %collective-permute-start.35 = (f32[6,6,1]{2,1,0:T(8,128)S(1)}, f32[6,6,1]{2,1,0:T(8,128)S(1)}, u32[]{:S(2)}, u32[]{:S(2)}) collective-permute-start(f32[6,6,1]{2,1,0:T(8,128)S(1)} %get-tuple-element.93), channel_id=1, source_target_pairs={{0,4},{4,8},{8,12},{1,5},{5,9},{9,13},{2,6},{6,10},{10,14},{3,7},{... | collective-permute-start | bytes 440 | tf_op jit(solution)/shard_map/ppermute | solution.py:22
  178.9 5.7 %collective-permute-start.41 = (f32[6,6,1]{2,1,0:T(8,128)S(1)}, f32[6,6,1]{2,1,0:T(8,128)S(1)}, u32[]{:S(2)}, u32[]{:S(2)}) collective-permute-start(f32[6,6,1]{2,1,0:T(8,128)S(1)} %get-tuple-element.91), channel_id=1, source_target_pairs={{0,4},{4,8},{8,12},{1,5},{5,9},{9,13},{2,6},{6,10},{10,14},{3,7},{... | collective-permute-start | bytes 440 | tf_op jit(solution)/shard_map/ppermute | solution.py:22
  226.2 5.7 %collective-permute-start.47 = (f32[6,6,1]{2,1,0:T(8,128)S(1)}, f32[6,6,1]{2,1,0:T(8,128)S(1)}, u32[]{:S(2)}, u32[]{:S(2)}) collective-permute-start(f32[6,6,1]{2,1,0:T(8,128)S(1)} %get-tuple-element.89), channel_id=1, source_target_pairs={{0,4},{4,8},{8,12},{1,5},{5,9},{9,13},{2,6},{6,10},{10,14},{3,7},{... | collective-permute-start | bytes 440 | tf_op jit(solution)/shard_map/ppermute | solution.py:22
  249.7 5.7 %collective-permute-start.53 = (f32[6,6,1]{2,1,0:T(8,128)S(1)}, f32[6,6,1]{2,1,0:T(8,128)S(1)}, u32[]{:S(2)}, u32[]{:S(2)}) collective-permute-start(f32[6,6,1]{2,1,0:T(8,128)S(1)} %get-tuple-element.87), channel_id=1, source_target_pairs={{0,4},{4,8},{8,12},{1,5},{5,9},{9,13},{2,6},{6,10},{10,14},{3,7},{... | collective-permute-start | bytes 440 | tf_op jit(solution)/shard_map/ppermute | solution.py:22
  272.6 6.3 %collective-permute-start.59 = (f32[10,10,1]{2,1,0:T(8,128)S(1)}, f32[10,10,1]{2,1,0:T(8,128)S(1)}, u32[]{:S(2)}, u32[]{:S(2)}) collective-permute-start(f32[10,10,1]{2,1,0:T(8,128)S(1)} %get-tuple-element.65), channel_id=1, source_target_pairs={{0,4},{4,8},{8,12},{1,5},{5,9},{9,13},{2,6},{6,10},{10,14},{3,7},{... | collective-permute-start | bytes 1208 | tf_op jit(solution)/shard_map/ppermute | solution.py:22
  295.1 6.3 %collective-permute-start.65 = (f32[10,10,1]{2,1,0:T(8,128)S(1)}, f32[10,10,1]{2,1,0:T(8,128)S(1)}, u32[]{:S(2)}, u32[]{:S(2)}) collective-permute-start(f32[10,10,1]{2,1,0:T(8,128)S(1)} %get-tuple-element.63), channel_id=1, source_target_pairs={{0,4},{4,8},{8,12},{1,5},{5,9},{9,13},{2,6},{6,10},{10,14},{3,7},{... | collective-permute-start | bytes 1208 | tf_op jit(solution)/shard_map/ppermute | solution.py:22
  321.1 5.6 %collective-permute-start.69 = (f32[18,1,128]{2,1,0:T(1,128)S(1)}, f32[18,1,128]{2,1,0:T(1,128)S(1)}, u32[]{:S(2)}, u32[]{:S(2)}) collective-permute-start(f32[18,1,128]{2,1,0:T(1,128)S(1)} %get-tuple-element.42), channel_id=1, source_target_pairs={{0,16},{1,17},{2,18},{3,19},{4,20},{5,21},{6,22},{7,23},{8,24},{9,... | collective-permute-start | bytes 27656 | tf_op jit(solution)/shard_map/ppermute | solution.py:22
  328.7 7.8 %collective-permute-start.71 = (f32[18,18,1]{2,1,0:T(8,128)S(1)}, f32[18,18,1]{2,1,0:T(8,128)S(1)}, u32[]{:S(2)}, u32[]{:S(2)}) collective-permute-start(f32[18,18,1]{2,1,0:T(8,128)S(1)} %get-tuple-element.31), channel_id=1, source_target_pairs={{0,4},{4,8},{8,12},{1,5},{5,9},{9,13},{2,6},{6,10},{10,14},{3,7},{... | collective-permute-start | bytes 3896 | tf_op jit(solution)/shard_map/ppermute | solution.py:22
  345.4 5.6 %collective-permute-start.75 = (f32[18,1,128]{2,1,0:T(1,128)S(1)}, f32[18,1,128]{2,1,0:T(1,128)S(1)}, u32[]{:S(2)}, u32[]{:S(2)}) collective-permute-start(f32[18,1,128]{2,1,0:T(1,128)S(1)} %get-tuple-element.40), channel_id=1, source_target_pairs={{0,16},{1,17},{2,18},{3,19},{4,20},{5,21},{6,22},{7,23},{8,24},{9,... | collective-permute-start | bytes 27656 | tf_op jit(solution)/shard_map/ppermute | solution.py:22
  353.0 7.8 %collective-permute-start.77 = (f32[18,18,1]{2,1,0:T(8,128)S(1)}, f32[18,18,1]{2,1,0:T(8,128)S(1)}, u32[]{:S(2)}, u32[]{:S(2)}) collective-permute-start(f32[18,18,1]{2,1,0:T(8,128)S(1)} %get-tuple-element.29), channel_id=1, source_target_pairs={{0,4},{4,8},{8,12},{1,5},{5,9},{9,13},{2,6},{6,10},{10,14},{3,7},{... | collective-permute-start | bytes 3896 | tf_op jit(solution)/shard_map/ppermute | solution.py:22
  369.7 5.6 %collective-permute-start.81 = (f32[18,1,128]{2,1,0:T(1,128)S(1)}, f32[18,1,128]{2,1,0:T(1,128)S(1)}, u32[]{:S(2)}, u32[]{:S(2)}) collective-permute-start(f32[18,1,128]{2,1,0:T(1,128)S(1)} %get-tuple-element.38), channel_id=1, source_target_pairs={{0,16},{1,17},{2,18},{3,19},{4,20},{5,21},{6,22},{7,23},{8,24},{9,... | collective-permute-start | bytes 27656 | tf_op jit(solution)/shard_map/ppermute | solution.py:22
  377.3 7.8 %collective-permute-start.83 = (f32[18,18,1]{2,1,0:T(8,128)S(1)}, f32[18,18,1]{2,1,0:T(8,128)S(1)}, u32[]{:S(2)}, u32[]{:S(2)}) collective-permute-start(f32[18,18,1]{2,1,0:T(8,128)S(1)} %get-tuple-element.27), channel_id=1, source_target_pairs={{0,4},{4,8},{8,12},{1,5},{5,9},{9,13},{2,6},{6,10},{10,14},{3,7},{... | collective-permute-start | bytes 3896 | tf_op jit(solution)/shard_map/ppermute | solution.py:22
  (63 other events, 423.6 us)
where the time goes:
time: 388 us; the launch traced here: 386 us
  waiting for transfers between devices  170 us (44%)
  starting transfers between devices  153 us (39%)
  local copies, waits for them, and re-layouts  27.2 us (7%)
  blocking collectives  22.7 us (6%)
  other arithmetic  11.8 us (3%)
    ppermute x42, waiting for transfers between devices, extended(): before = lax.ppermute(last, axis, up)  152 us
    ppermute x42, starting transfers between devices, extended(): after = lax.ppermute(first, axis, down)  83.8 us
    ppermute x42, starting transfers between devices, extended(): before = lax.ppermute(last, axis, up)  69 us
    ppermute x42, waiting for transfers between devices, extended(): after = lax.ppermute(first, axis, down)  17.2 us
    all_gather x1, blocking collectives, collect(): gathered = lax.all_gather(gathered, 'gy', axis=2, tiled=True)  13.1 us
    reshape x4, local copies, waits for them, and re-layouts, restrict(): blocks = values.reshape(shape_a // 2, 2, shape_b // 2, 2, shape_c // 2, 2)  11.5 us
    reshape x4, local copies, waits for them, and re-layouts, prolong(): return spread.reshape(2 * shape_a, 2 * shape_b, 2 * shape_c)  7.93 us
  transfers between devices with their start and end apart: 84, of which 62 were waited for; matrix products, arithmetic and copies ran while one was open for 0% of the time, Pallas kernels for 0%

commit v1 on v0

--- a/solution.py
+++ b/solution.py
@@ -11,26 +11,25 @@
 carry_coef = 0.6 * rho_one
 fresh_coef = 2.0 * rho_one / (0.75 * 6.0)
 
+AXES = (("gz", 0), ("gx", 1), ("gy", 2))
 
-def extended(x, sides, width):
-    for axis, dim in sides:
-        peers, length = (lax.axis_size(axis), x.shape[dim])
+
+def extended(x, width):
+    for axis, dim in AXES:
+        peers, length = (lax.axis_size(axis), x.shape[dim + 1])
         up = [(i, (i + 1) % peers) for i in range(peers - 1)]
         down = [(j, i) for i, j in up]
-        last = lax.slice_in_dim(x, length - width, length, axis=dim)
-        first = lax.slice_in_dim(x, 0, width, axis=dim)
+        last = lax.slice_in_dim(x, length - width, length, axis=dim + 1)
+        first = lax.slice_in_dim(x, 0, width, axis=dim + 1)
         before = lax.ppermute(last, axis, up)
         after = lax.ppermute(first, axis, down)
-        x = jnp.concatenate([before, x, after], axis=dim)
+        x = jnp.concatenate([before, x, after], axis=dim + 1)
     return x
 
 
 def stencil(values):
     padded = jnp.pad(values, 1)
-    beside = padded[2:, 1:-1, 1:-1] + padded[:-2, 1:-1, 1:-1]
-    beside = beside + padded[1:-1, 2:, 1:-1] + padded[1:-1, :-2, 1:-1]
-    beside = beside + padded[1:-1, 1:-1, 2:] + padded[1:-1, 1:-1, :-2]
-    return 6.0 * values - beside
+    return valid_op(padded)
 
 
 def valid_op(padded):
@@ -38,11 +37,6 @@
     beside = beside + padded[1:-1, 2:, 1:-1] + padded[1:-1, :-2, 1:-1]
     beside = beside + padded[1:-1, 1:-1, 2:] + padded[1:-1, 1:-1, :-2]
     return 6.0 * padded[1:-1, 1:-1, 1:-1] - beside
-
-
-def local_stencil(values):
-    padded = extended(values, (("gz", 0), ("gx", 1), ("gy", 2)), 1)
-    return valid_op(padded)
 
 
 def smooth_pass(iterate, source, apply_op, from_zero):
@@ -87,6 +81,10 @@
     return lax.all_gather(gathered, "gx", axis=1, tiled=True)
 
 
+def local_stencil(values):
+    return valid_op(extended(values[None], 1)[0])
+
+
 def own_block(whole, block_shape):
     start_z = lax.axis_index("gz") * block_shape[0]
     start_x = lax.axis_index("gx") * block_shape[1]
@@ -106,11 +104,63 @@
     return (smooth_pass(iterate, source, local_stencil, False), coarsest)
 
 
-def body(divergence, pressure_prev):
-    gather_at = 3
-    pressure, coarse_correction = body_cycle(0, pressure_prev, divergence, False, gather_at)
+def body_levels(divergence, pressure_prev):
+    pressure, coarse_correction = body_cycle(0, pressure_prev, divergence, False, 3)
     residual = divergence - local_stencil(pressure)
     return (pressure, residual, coarse_correction)
+
+
+def crop(x, n):
+    return x[n:-n, n:-n, n:-n]
+
+
+def body_wide(divergence, pressure_prev):
+    block = divergence.shape
+    wide = 5
+    both = extended(jnp.stack([pressure_prev, divergence]), wide)
+    x, b = both[0], both[1]
+
+    def inside(width):
+        keep = None
+        for axis, dim in AXES:
+            at = lax.broadcasted_iota(jnp.int32, tuple(n + 2 * width for n in block), dim) - width
+            at = at + lax.axis_index(axis) * block[dim]
+            good = (at >= 0) & (at < lax.axis_size(axis) * block[dim])
+            keep = good if keep is None else keep & good
+        return keep
+
+    def masked(values, width):
+        return jnp.where(inside(width), values, 0.0)
+
+    r = crop(b, 1) - valid_op(x)
+    d = masked(r * first_scale, 4)
+    r = crop(r, 1) - valid_op(d)
+    d2 = masked(carry_coef * crop(d, 1) + fresh_coef * r, 3)
+    r = crop(r, 1) - valid_op(d2)
+    x = pressure_prev + crop(d, 4) + crop(d2, 3)
+    coarse_source = collect(restrict(crop(r, 2)))
+    coarse, coarsest = vcycle(1, None, coarse_source)
+    half = tuple(n // 2 for n in block)
+    starts = tuple(lax.axis_index(axis) * half[dim] for axis, dim in AXES)
+    local = lax.dynamic_slice(jnp.pad(coarse, 2), starts, tuple(n + 4 for n in half))
+    e = prolong(local)
+    r = r - valid_op(crop(e, 1))
+    x = x + crop(e, 4)
+    d = masked(r * first_scale, 2)
+    r = crop(r, 1) - valid_op(d)
+    d2 = masked(carry_coef * crop(d, 1) + fresh_coef * r, 1)
+    r = crop(r, 1) - valid_op(d2)
+    return (x + crop(d, 2) + crop(d2, 1), r, coarsest)
+
+
+WHOLE_CELLS = 1 << 18
+
+
+def body(divergence, pressure_prev):
+    cells = lax.axis_size("gz") * lax.axis_size("gx") * lax.axis_size("gy") * divergence.size // 8
+    if cells <= WHOLE_CELLS and min(divergence.shape) > 5:
+        return body_wide(divergence, pressure_prev)
+    return body_levels(divergence, pressure_prev)
 
 
 def solution(mesh):

time: 388 us -> 216 us (0.56)
  the two profiles are of different devices: /device:TPU:30 before, /device:TPU:0 now
where the time goes in v1:
time: 216 us; the launch traced here: 215 us
  local copies, waits for them, and re-layouts  117 us (54%)
  blocking collectives  35.5 us (16%)
  other arithmetic  31.4 us (15%)
  waiting for transfers between devices  16.8 us (8%)
  starting transfers between devices  13.2 us (6%)
    reshape x4, local copies, waits for them, and re-layouts, restrict(): blocks = values.reshape(shape_a // 2, 2, shape_b // 2, 2, shape_c // 2, 2)  50.6 us
    reshape x4, local copies, waits for them, and re-layouts, prolong(): return spread.reshape(2 * shape_a, 2 * shape_b, 2 * shape_c)  40.8 us
    broadcast_in_dim x6, local copies, waits for them, and re-layouts, prolong(): jnp.broadcast_to(values[:, None, :, None, :, None], (shape_a, 2, shape_b,...  22.7 us
    all_gather x1, blocking collectives, collect(): gathered = lax.all_gather(gathered, 'gy', axis=2, tiled=True)  22.1 us
    reduce_sum x6, other arithmetic, restrict(): return 0.5 * jnp.sum(blocks, axis=(1, 3, 5))  19.1 us
    ppermute x3, waiting for transfers between devices, extended(): after = lax.ppermute(first, axis, down)  13.2 us
    ppermute x3, starting transfers between devices, extended(): before = lax.ppermute(last, axis, up)  9.29 us
    all_gather x1, blocking collectives, collect(): return lax.all_gather(gathered, 'gx', axis=1, tiled=True)  8 us
  transfers between devices with their start and end apart: 6, of which 5 were waited for; matrix products, arithmetic and copies ran while one was open for 0% of the time, Pallas kernels for 0%

profile of v1, /device:TPU:0, one launch (start us, length us, event | category | flops | bytes accessed | tf_op | source)
XLA Modules:
  0.0 215.3 jit_solution(6534104066657321581)
XLA Ops:
  1.6 2.4 %collective-permute-start = (f32[2,5,16,128]{3,2,1,0:T(8,128)S(1)}, f32[2,5,16,128]{3,2,1,0:T(8,128)S(1)}, u32[]{:S(2)}, u32[]{:S(2)}) collective-permute-start(f32[2,5,16,128]{3,2,1,0:T(8,128)S(1)} %get-tuple-element.38), channel_id=1, source_target_pairs={{0,1},{1,2},{2,3},{4,5},{5,6},{6,7},{8,9},{9,10},{10,11},{12,13},{... | collective-permute-start | bytes 245768 | tf_op jit(solution)/shard_map/ppermute | solution.py:24
  3.9 1.3 collective-permute-start.1
  5.3 3.9 %collective-permute-done.1 = f32[2,5,16,128]{3,2,1,0:T(8,128)S(1)} collective-permute-done((f32[2,5,16,128]{3,2,1,0:T(8,128)S(1)}, f32[2,5,16,128]{3,2,1,0:T(8,128)S(1)}, u32[]{:S(2)}, u32[]{:S(2)}) %collective-permute-start.1) | collective-permute-done | bytes 81952 | tf_op jit(solution)/shard_map/ppermute | solution.py:25
  10.2 3.4 %collective-permute-start.2 = (f32[2,26,5,128]{3,2,1,0:T(8,128)S(1)}, f32[2,26,5,128]{3,2,1,0:T(8,128)S(1)}, u32[]{:S(2)}, u32[]{:S(2)}) collective-permute-start(f32[2,26,5,128]{3,2,1,0:T(8,128)S(1)} %get-tuple-element.36), channel_id=1, source_target_pairs={{0,16},{1,17},{2,18},{3,19},{4,20},{5,21},{6,22},{7,23},{8,24},{9,... | collective-permute-start | bytes 399368 | tf_op jit(solution)/shard_map/ppermute | solution.py:24
  15.0 2.1 collective-permute-done.2
  17.1 4.7 %collective-permute-done.3 = f32[2,26,5,128]{3,2,1,0:T(8,128)S(1)} collective-permute-done((f32[2,26,5,128]{3,2,1,0:T(8,128)S(1)}, f32[2,26,5,128]{3,2,1,0:T(8,128)S(1)}, u32[]{:S(2)}, u32[]{:S(2)}) %collective-permute-start.3) | collective-permute-done | bytes 133152 | tf_op jit(solution)/shard_map/ppermute | solution.py:25
  22.7 3.5 %collective-permute-start.4 = (f32[2,26,26,5]{2,0,3,1:T(2,128)S(1)}, f32[2,26,26,5]{2,0,3,1:T(2,128)S(1)}, u32[]{:S(2)}, u32[]{:S(2)}) collective-permute-start(f32[2,26,26,5]{2,0,3,1:T(2,128)S(1)} %copy.8), channel_id=1, source_target_pairs={{0,4},{4,8},{8,12},{1,5},{5,9},{9,13},{2,6},{6,10},{10,14},{3,7},{... | collective-permute-start | bytes 81128 | tf_op jit(solution)/shard_map/ppermute | solution.py:24
  27.9 1.5 collective-permute-done.4
  29.8 4.7 %collective-permute-done.5 = f32[2,26,26,5]{2,0,3,1:T(2,128)S(1)} collective-permute-done((f32[2,26,26,5]{2,0,3,1:T(2,128)S(1)}, f32[2,26,26,5]{2,0,3,1:T(2,128)S(1)}, u32[]{:S(2)}, u32[]{:S(2)}) %collective-permute-start.5) | collective-permute-done | bytes 27072 | tf_op jit(solution)/shard_map/ppermute | solution.py:25
  39.4 9.7 %reshape.80 = f32[8,2,8,2,64,2]{5,4,3,2,1,0:T(8,128)} reshape(f32[16,16,128]{2,1,0:T(8,128)S(1)} %slice.740) | data formatting | bytes 262144 | tf_op jit(solution)/shard_map/reshape | solution.py:53
  49.2 4.0 %reduce_sum.52 = f32[8,8,64]{2,1,0:T(8,128)S(1)} reduce(f32[8,2,8,2,64,2]{5,4,3,2,1,0:T(8,128)} %reshape.80, f32[]{:T(128)} %constant.50.clone.1), dimensions={1,3,5}, to_apply=%region_0.1 | reduce | flops 28672 | bytes 147460 | tf_op jit(solution)/shard_map/reduce_sum | solution.py:54
  53.2 5.4 %all_gather.9 = f32[32,8,64]{2,1,0:T(8,128)S(1)} all-gather(f32[8,8,64]{2,1,0:T(8,128)S(1)} %broadcast_multiply_fusion.2), channel_id=1, replica_groups=mesh['gx'=2,'gy'=4,'gz'=4] {'gz'}, dimensions={0}, use_global_device_ids=true | all-gather | bytes 81920 | tf_op jit(solution)/shard_map/all_gather | solution.py:79
  58.8 22.1 %all_gather.10 = f32[32,8,256]{0,1,2:T(8,128)S(1)} all-gather(f32[32,8,64]{0,1,2:T(8,128)S(1)} %copy.12), channel_id=1, replica_groups=mesh['gx'=2,'gy'=4,'gz'=4] {'gy'}, dimensions={2}, use_global_device_ids=true | all-gather | bytes 327680 | tf_op jit(solution)/shard_map/all_gather | solution.py:80
  81.3 8.0 %all_gather.11 = f32[32,16,256]{2,1,0:T(8,128)S(1)} all-gather(f32[32,8,256]{2,1,0:T(8,128)S(1)} %copy.13), channel_id=1, replica_groups=mesh['gx'=2,'gy'=4,'gz'=4] {'gx'}, dimensions={1}, use_global_device_ids=true | all-gather | bytes 786432 | tf_op jit(solution)/shard_map/all_gather | solution.py:81
  90.1 34.8 %reshape.81 = f32[16,2,8,2,128,2]{5,4,3,2,1,0:T(8,128)} reshape(f32[32,16,256]{2,1,0:T(8,128)S(1)} %fusion.20) | data formatting | bytes 1048576 | tf_op jit(solution)/shard_map/reshape | solution.py:53
  124.9 12.2 %reduce_sum.53 = f32[16,8,128]{2,1,0:T(8,128)S(1)} reduce(f32[16,2,8,2,128,2]{5,4,3,2,1,0:T(8,128)} %reshape.81, f32[]{:T(128)} %constant.50.clone.1), dimensions={1,3,5}, to_apply=%region_1.2 | reduce | flops 114688 | bytes 589828 | tf_op jit(solution)/shard_map/reduce_sum | solution.py:54
  137.4 5.5 %reshape.82 = f32[8,2,4,2,64,2]{5,4,3,2,1,0:T(8,128)} reshape(f32[16,8,128]{2,1,0:T(8,128)S(1)} %fusion.63) | data formatting | bytes 131072 | tf_op jit(solution)/shard_map/reshape | solution.py:53
  142.9 2.5 %reduce_sum.54 = f32[8,4,64]{2,1,0:T(4,128)S(1)} reduce(f32[8,2,4,2,64,2]{5,4,3,2,1,0:T(8,128)} %reshape.82, f32[]{:T(128)} %constant.50.clone.1), dimensions={1,3,5}, to_apply=%region_2.3 | reduce | flops 14336 | bytes 73732 | tf_op jit(solution)/shard_map/reduce_sum | solution.py:54
  147.9 2.5 %broadcast_in_dim.59 = f32[8,2,4,2,64,2]{5,4,3,2,1,0:T(8,128)} broadcast(f32[8,4,64]{2,1,0:T(4,128)S(1)} %add_add_fusion), dimensions={0,2,4} | broadcast | bytes 73728 | tf_op jit(solution)/shard_map/broadcast_in_dim | solution.py:59
  150.5 4.0 %reshape.85 = f32[16,8,128]{2,1,0:T(8,128)S(1)} reshape(f32[8,2,4,2,64,2]{5,4,3,2,1,0:T(8,128)} %broadcast_in_dim.59) | data formatting | bytes 131072 | tf_op jit(solution)/shard_map/reshape | solution.py:62
  154.7 11.4 %broadcast_in_dim.60 = f32[16,2,8,2,128,2]{5,4,3,2,1,0:T(8,128)} broadcast(f32[16,8,128]{2,1,0:T(8,128)S(1)} %fusion.80), dimensions={0,2,4} | broadcast | bytes 589824 | tf_op jit(solution)/shard_map/broadcast_in_dim | solution.py:59
  166.1 24.2 %reshape.86 = f32[32,16,256]{2,1,0:T(8,128)S(1)} reshape(f32[16,2,8,2,128,2]{5,4,3,2,1,0:T(8,128)} %broadcast_in_dim.60) | data formatting | bytes 1048576 | tf_op jit(solution)/shard_map/reshape | solution.py:62
  191.3 8.5 %broadcast_in_dim.61 = f32[12,2,12,2,68,2]{5,4,3,2,1,0:T(8,128)} broadcast(f32[12,12,68]{2,1,0:T(8,128)S(1)} %pad_dynamic-slice_fusion), dimensions={0,2,4} | broadcast | bytes 352512 | tf_op jit(solution)/shard_map/broadcast_in_dim | solution.py:59
  199.8 12.4 %reshape.87 = f32[24,24,136]{2,1,0:T(8,128)S(1)} reshape(f32[12,2,12,2,68,2]{5,4,3,2,1,0:T(8,128)} %broadcast_in_dim.61) | data formatting | bytes 626688 | tf_op jit(solution)/shard_map/reshape | solution.py:62
  (77 shorter events, 19.5 us)
Async XLA Ops:
  0.6 21.2 %copy-start = (f32[16,16,128]{2,1,0:T(8,128)S(1)}, f32[16,16,128]{2,1,0:T(8,128)}, u32[]{:S(2)}) copy-start(f32[16,16,128]{2,1,0:T(8,128)} %param.3) | copy-start | bytes 393220
  0.6 21.2 %copy-start.1 = (f32[16,16,128]{2,1,0:T(8,128)S(1)}, f32[16,16,128]{2,1,0:T(8,128)}, u32[]{:S(2)}) copy-start(f32[16,16,128]{2,1,0:T(8,128)} %param.2) | copy-start | bytes 393220
  1.6 3.8 %collective-permute-start = (f32[2,5,16,128]{3,2,1,0:T(8,128)S(1)}, f32[2,5,16,128]{3,2,1,0:T(8,128)S(1)}, u32[]{:S(2)}, u32[]{:S(2)}) collective-permute-start(f32[2,5,16,128]{3,2,1,0:T(8,128)S(1)} %get-tuple-element.38), channel_id=1, source_target_pairs={{0,1},{1,2},{2,3},{4,5},{5,6},{6,7},{8,9},{9,10},{10,11},{12,13},{... | collective-permute-start | bytes 245768 | tf_op jit(solution)/shard_map/ppermute | solution.py:24
  3.9 5.3 %collective-permute-start.1 = (f32[2,5,16,128]{3,2,1,0:T(8,128)S(1)}, f32[2,5,16,128]{3,2,1,0:T(8,128)S(1)}, u32[]{:S(2)}, u32[]{:S(2)}) collective-permute-start(f32[2,5,16,128]{3,2,1,0:T(8,128)S(1)} %get-tuple-element.39), channel_id=1, source_target_pairs={{1,0},{2,1},{3,2},{5,4},{6,5},{7,6},{9,8},{10,9},{11,10},{13,12},{... | collective-permute-start | bytes 245768 | tf_op jit(solution)/shard_map/ppermute | solution.py:25
  10.2 6.9 %collective-permute-start.2 = (f32[2,26,5,128]{3,2,1,0:T(8,128)S(1)}, f32[2,26,5,128]{3,2,1,0:T(8,128)S(1)}, u32[]{:S(2)}, u32[]{:S(2)}) collective-permute-start(f32[2,26,5,128]{3,2,1,0:T(8,128)S(1)} %get-tuple-element.36), channel_id=1, source_target_pairs={{0,16},{1,17},{2,18},{3,19},{4,20},{5,21},{6,22},{7,23},{8,24},{9,... | collective-permute-start | bytes 399368 | tf_op jit(solution)/shard_map/ppermute | solution.py:24
  13.7 8.1 %collective-permute-start.3 = (f32[2,26,5,128]{3,2,1,0:T(8,128)S(1)}, f32[2,26,5,128]{3,2,1,0:T(8,128)S(1)}, u32[]{:S(2)}, u32[]{:S(2)}) collective-permute-start(f32[2,26,5,128]{3,2,1,0:T(8,128)S(1)} %get-tuple-element.37), channel_id=1, source_target_pairs={{16,0},{17,1},{18,2},{19,3},{20,4},{21,5},{22,6},{23,7},{24,8},{25... | collective-permute-start | bytes 399368 | tf_op jit(solution)/shard_map/ppermute | solution.py:25
  22.7 6.7 %collective-permute-start.4 = (f32[2,26,26,5]{2,0,3,1:T(2,128)S(1)}, f32[2,26,26,5]{2,0,3,1:T(2,128)S(1)}, u32[]{:S(2)}, u32[]{:S(2)}) collective-permute-start(f32[2,26,26,5]{2,0,3,1:T(2,128)S(1)} %copy.8), channel_id=1, source_target_pairs={{0,4},{4,8},{8,12},{1,5},{5,9},{9,13},{2,6},{6,10},{10,14},{3,7},{... | collective-permute-start | bytes 81128 | tf_op jit(solution)/shard_map/ppermute | solution.py:24
  26.6 7.9 %collective-permute-start.5 = (f32[2,26,26,5]{2,0,3,1:T(2,128)S(1)}, f32[2,26,26,5]{2,0,3,1:T(2,128)S(1)}, u32[]{:S(2)}, u32[]{:S(2)}) collective-permute-start(f32[2,26,26,5]{2,0,3,1:T(2,128)S(1)} %copy.9), channel_id=1, source_target_pairs={{4,0},{8,4},{12,8},{5,1},{9,5},{13,9},{6,2},{10,6},{14,10},{7,3},{... | collective-permute-start | bytes 81128 | tf_op jit(solution)/shard_map/ppermute | solution.py:25
  147.0 3.5 %copy-start.2 = (f32[2,1,16]{2,0,1:T(2,128)}, f32[2,1,16]{2,0,1:T(2,128)S(1)}, u32[]{:S(2)}) copy-start(f32[2,1,16]{2,0,1:T(2,128)S(1)} %fusion.153) | copy-start | bytes 388

commit v2 on v0

--- a/solution.py
+++ b/solution.py
@@ -1,6 +1,8 @@
 import jax
 import jax.numpy as jnp
 from jax import lax
+from jax.experimental import pallas as pl
+from jax.experimental.pallas import tpu as pltpu
 from jax.sharding import PartitionSpec as P
 
 LEVELS = 6
@@ -11,26 +13,27 @@
 carry_coef = 0.6 * rho_one
 fresh_coef = 2.0 * rho_one / (0.75 * 6.0)
 
-
-def extended(x, sides, width):
-    for axis, dim in sides:
-        peers, length = (lax.axis_size(axis), x.shape[dim])
+LANES = 128
+F32 = jnp.float32
+AXES = (("gz", 0), ("gx", 1), ("gy", 2))
+
+
+def extended(x, width):
+    for axis, dim in AXES:
+        peers, length = (lax.axis_size(axis), x.shape[dim + 1])
         up = [(i, (i + 1) % peers) for i in range(peers - 1)]
         down = [(j, i) for i, j in up]
-        last = lax.slice_in_dim(x, length - width, length, axis=dim)
-        first = lax.slice_in_dim(x, 0, width, axis=dim)
+        last = lax.slice_in_dim(x, length - width, length, axis=dim + 1)
+        first = lax.slice_in_dim(x, 0, width, axis=dim + 1)
         before = lax.ppermute(last, axis, up)
         after = lax.ppermute(first, axis, down)
-        x = jnp.concatenate([before, x, after], axis=dim)
+        x = jnp.concatenate([before, x, after], axis=dim + 1)
     return x
 
 
 def stencil(values):
     padded = jnp.pad(values, 1)
-    beside = padded[2:, 1:-1, 1:-1] + padded[:-2, 1:-1, 1:-1]
-    beside = beside + padded[1:-1, 2:, 1:-1] + padded[1:-1, :-2, 1:-1]
-    beside = beside + padded[1:-1, 1:-1, 2:] + padded[1:-1, 1:-1, :-2]
-    return 6.0 * values - beside
+    return valid_op(padded)
 
 
 def valid_op(padded):
@@ -38,11 +41,6 @@
     beside = beside + padded[1:-1, 2:, 1:-1] + padded[1:-1, :-2, 1:-1]
     beside = beside + padded[1:-1, 1:-1, 2:] + padded[1:-1, 1:-1, :-2]
     return 6.0 * padded[1:-1, 1:-1, 1:-1] - beside
-
-
-def local_stencil(values):
-    padded = extended(values, (("gz", 0), ("gx", 1), ("gy", 2)), 1)
-    return valid_op(padded)
 
 
 def smooth_pass(iterate, source, apply_op, from_zero):
@@ -87,6 +85,10 @@
     return lax.all_gather(gathered, "gx", axis=1, tiled=True)
 
 
+def local_stencil(values):
+    return valid_op(extended(values[None], 1)[0])
+
+
 def own_block(whole, block_shape):
     start_z = lax.axis_index("gz") * block_shape[0]
     start_x = lax.axis_index("gx") * block_shape[1]
@@ -106,11 +108,668 @@
     return (smooth_pass(iterate, source, local_stencil, False), coarsest)
 
 
-def body(divergence, pressure_prev):
-    gather_at = 3
-    pressure, coarse_correction = body_cycle(0, pressure_prev, divergence, False, gather_at)
+def body_levels(divergence, pressure_prev):
+    pressure, coarse_correction = body_cycle(0, pressure_prev, divergence, False, 3)
     residual = divergence - local_stencil(pressure)
     return (pressure, residual, coarse_correction)
+
+
+def iota(shape, dim):
+    return lax.broadcasted_iota(jnp.int32, shape, dim)
+
+
+def signed(index, size, extent):
+    return jnp.where(index >= (size + extent) // 2, index - extent, index)
+
+
+def split(values):
+    terms = []
+    for _ in range(3):
+        term = values.astype(jnp.bfloat16)
+        terms.append(term)
+        values = values - term.astype(F32)
+    return terms
+
+
+def right_dot(values, table):
+    parts = [jnp.dot(t, table, preferred_element_type=F32) for t in split(values)]
+    return parts[0] + parts[1] + parts[2]
+
+
+def left_dot(table, values):
+    parts = [jnp.dot(table, t, preferred_element_type=F32) for t in split(values)]
+    return parts[0] + parts[1] + parts[2]
+
+
+def as_table(keep, value=1.0):
+    return jnp.where(keep, value, 0.0).astype(jnp.bfloat16)
+
+
+def lateral(v):
+    rows, lanes = v.shape
+    return (
+        pltpu.roll(v, 1, 0) + pltpu.roll(v, rows - 1, 0)
+        + pltpu.roll(v, 1, 1) + pltpu.roll(v, lanes - 1, 1)
+    )
+
+
+def apply_at(ref, k, lateral_of=lateral):
+    centre = ref[k]
+    beside = lateral_of(centre)
+    if k > 0:
+        beside = beside + ref[k - 1]
+    if k < ref.shape[0] - 1:
+        beside = beside + ref[k + 1]
+    return 6.0 * centre - beside
+
+
+def wrapped_mask(shape, sizes, low, high):
+    keep = None
+    for dim, size in sizes.items():
+        at = signed(iota(shape, dim), size, shape[dim])
+        good = ((at >= 0) | low[dim]) & ((at < size) | high[dim])
+        keep = good if keep is None else keep & good
+    return jnp.where(keep, 1.0, 0.0).astype(F32)
+
+
+def side(index, step):
+    low_bits = (1 << step) - 1
+    above = ((index >> step) & 1) == 0
+    near = jnp.where(above, (index & low_bits) == low_bits, (index & low_bits) == 0)
+    return above, near
+
+
+def place(axis, count):
+    index = lax.axis_index(axis)
+    return index, index > 0, index < count - 1
+
+
+def first_kernel(peers, steps, b_ref, p_ref, r_ref, x_ref, coarse_ref, *rest):
+    slabs, (b_ext, p_ext, d_one, d_two, pairs, lines) = rest[:steps], rest[steps:]
+    bz, bx, by = b_ref.shape
+    ez, ex, ey = r_ref.shape
+    iz, z_low, z_high = place("gz", peers[0])
+    _, x_low, x_high = place("gx", peers[1])
+    _, y_low, y_high = place("gy", peers[2])
+    flat = wrapped_mask((ex, ey), {0: bx, 1: by}, (x_low, y_low), (x_high, y_high))
+    below = jnp.where(z_low, 1.0, 0.0).astype(F32)
+    above = jnp.where(z_high, 1.0, 0.0).astype(F32)
+
+    def masked(k, v):
+        v = v * flat
+        if k < 3:
+            v = v * below
+        if k >= 3 + bz:
+            v = v * above
+        return v
+
+    zero = jnp.zeros((ex, ey), F32)
+    for k in range(ez):
+        p_ext[k] = zero
+        b_ext[k] = zero
+        if 3 <= k < 3 + bz:
+            b_ext[k, 0:bx, 0:by] = b_ref[k - 3]
+            p_ext[k, 0:bx, 0:by] = p_ref[k - 3]
+    for k in range(ez):
+        if 2 <= k < ez - 2:
+            r = b_ext[k] - apply_at(p_ext, k)
+            r_ref[k] = r
+            d_one[k] = masked(k, r * first_scale)
+        else:
+            d_one[k] = zero
+    for k in range(ez):
+        if 1 <= k < ez - 1:
+            r = -apply_at(d_one, k)
+            if 2 <= k < ez - 2:
+                r = r + r_ref[k]
+            r_ref[k] = r
+            d_two[k] = masked(k, carry_coef * d_one[k] + fresh_coef * r)
+        else:
+            d_two[k] = zero
+    for k in range(ez):
+        r = -apply_at(d_two, k)
+        if 1 <= k < ez - 1:
+            r = r + r_ref[k]
+        r_ref[k] = masked(k, r)
+        x_ref[k] = p_ext[k] + d_one[k] + d_two[k]
+
+    for step, out in enumerate(slabs):
+        up, _ = side(iz, step)
+        start = jnp.where(up, ez - 5, 0)
+        start_x = jnp.where(up, ez - 3, 1)
+        for j in range(5):
+            out[j * ex:(j + 1) * ex, :] = r_ref[start + j]
+        for j in range(2):
+            out[(5 + j) * ex:(6 + j) * ex, :] = x_ref[start_x + j]
+
+    coarse_z, rows, lanes = bz // 2 + 4, bx // 2, coarse_ref.shape[1] // 2
+    half = coarse_z // 2
+    for zc in range(coarse_z):
+        low, high = 2 * zc - 1, 2 * zc
+        if low < 0:
+            total = r_ref[high]
+        elif high >= ez:
+            total = r_ref[low]
+        else:
+            total = r_ref[low] + r_ref[high]
+        base = zc * ex
+        for tile in range(ey // LANES):
+            here = slice(tile * LANES, (tile + 1) * LANES)
+            pairs[tile, base:base + ex, :] = total[:, here]
+            even = pairs.at[tile][pl.ds(base, ex // 2, 2), :]
+            odd = pairs.at[tile][pl.ds(base + 1, ex // 2, 2), :]
+            sums = even + odd
+            at = zc // 2 * rows
+            lines[zc % 2, at:at + rows, here] = sums[0:rows]
+            at = half * rows + zc // 2 * 4
+            lines[zc % 2, at:at + 4, here] = sums[rows:rows + 4]
+    fine = signed(iota((ey, lanes), 0), by, ey)
+    coarse = signed(iota((ey, lanes), 1), by // 2, lanes)
+    table = as_table((fine >> 1) == coarse, 0.5)
+    for part in range(2):
+        coarse_ref[:, part * lanes:(part + 1) * lanes] = right_dot(lines[part], table)
+
+
+def z_kernel(peers, steps, *refs):
+    r_in, x_in = refs[0:2]
+    slabs = refs[2:2 + steps]
+    r_ref, x_ref, slab_ref = refs[2 + steps:]
+    ez, ex, ey = r_in.shape
+    iz, _, _ = place("gz", peers[0])
+    ix, _, _ = place("gx", peers[1])
+    for k in range(r_ref.shape[0]):
+        r_ref[k] = r_in[k + 1]
+    for k in range(x_ref.shape[0]):
+        x_ref[k] = x_in[k + 3]
+    for step, slab in enumerate(slabs):
+        up, near = side(iz, step)
+
+        @pl.when(near)
+        def _():
+            start = jnp.where(up, r_ref.shape[0] - 5, 0)
+            start_x = jnp.where(up, x_ref.shape[0] - 2, 0)
+            for j in range(5):
+                r_ref[start + j] += slab[j * ex:(j + 1) * ex, :]
+            for j in range(2):
+                x_ref[start_x + j] += slab[(5 + j) * ex:(6 + j) * ex, :]
+
+    bx = ex - 8
+    up = (ix & 1) == 0
+    row = iota((8, ey), 0)
+    for k in range(r_ref.shape[0]):
+        first, last, spill = r_ref[k, 0:8], r_ref[k, bx - 8:bx], r_ref[k, bx:ex]
+        to_high = pltpu.roll(jnp.where(row >= 6, last, spill), 2, 0)
+        to_low = pltpu.roll(jnp.where(row >= 5, spill, first), 3, 0)
+        out = jnp.where(up, to_high, to_low)
+        if 2 <= k < 2 + x_ref.shape[0]:
+            spill = x_ref[k - 2, bx:ex]
+            extra = jnp.where(up, pltpu.roll(spill, 5, 0), pltpu.roll(spill, 7, 0))
+            out = jnp.where((row == 5) | (row == 6), extra, out)
+        slab_ref[8 * k:8 * k + 8, :] = out
+
+
+def edge_lanes(low_tile, high_tile, first, count, slot):
+    lane = iota(low_tile.shape, 1)
+    at = first % LANES
+    source = low_tile if first < LANES else high_tile
+    after = high_tile if first < LANES else low_tile
+    taken = jnp.where(lane >= at, source, after)
+    keep = (lane - at) % LANES if at == 0 else jnp.where(lane >= at, lane - at, lane + LANES - at)
+    taken = jnp.where(keep < count, taken, 0.0)
+    return pltpu.roll(taken, (slot - at) % LANES, 1)
+
+
+def one_tile_lanes(tile, first, count, slot):
+    lane = iota(tile.shape, 1)
+    at = first % LANES
+    gone = jnp.where(lane >= at, lane - at, lane + LANES - at)
+    return pltpu.roll(jnp.where(gone < count, tile, 0.0), (slot - at) % LANES, 1)
+
+
+def y_kernel(peers, steps, r_in, x_in, mine, got, r_ref, x_ref, r1_ref, x1_ref, sum_ref, *rest):
+    slabs = rest[:steps]
+    b1, d1, d2, x_all, pairs, lines, edges = rest[steps:]
+    layers, ex, ey = r_in.shape
+    bx, by = ex - 8, ey - LANES
+    ix, _, _ = place("gx", peers[1])
+    iy, y_low, y_high = place("gy", peers[2])
+    up = (ix & 1) == 0
+    row = iota((8, ey), 0)
+    own_z = x_in.shape[0]
+
+    for k in range(layers):
+        slab = got[8 * k:8 * k + 8, :]
+        from_high = pltpu.roll(slab, 5, 0)
+        from_low = pltpu.roll(slab, 6, 0)
+        first, last, spill = r_in[k, 0:8], r_in[k, bx - 8:bx], r_in[k, bx:ex]
+        if bx > 16:
+            r_ref[k] = r_in[k]
+        r_ref[k, 0:8] = first + jnp.where(up | (row >= 3), 0.0, from_low)
+        r_ref[k, bx - 8:bx] = last + jnp.where(up & (row >= 5), from_high, 0.0)
+        r_ref[k, bx:ex] = spill + jnp.where(
+            up, jnp.where(row < 2, from_high, 0.0), jnp.where(row >= 6, from_low, 0.0)
+        )
+        if 2 <= k < 2 + own_z:
+            j = k - 2
+            if bx > 16:
+                x_all[j] = x_in[j, 0:bx]
+            x_all[j, 0:8] = x_in[j, 0:8] + jnp.where(up | (row >= 2), 0.0, pltpu.roll(slab, 3, 0))
+            x_all[j, bx - 8:bx] = x_in[j, bx - 8:bx] + jnp.where(
+                up & (row >= 6), pltpu.roll(slab, 1, 0), 0.0
+            )
+            x_ref[j] = x_all[j, :, 0:by]
+
+    per_tile = LANES // 8
+    groups = -(-layers // per_tile)
+    tall = edges.shape[1]
+    for which in range(2):
+        for group in range(groups):
+            total = jnp.zeros((ex, LANES), F32)
+            total_x = jnp.zeros((bx, LANES), F32)
+            for k in range(group * per_tile, min(layers, (group + 1) * per_tile)):
+                slot = 8 * (k % per_tile)
+                a, c = r_ref[k, :, by - LANES:by], r_ref[k, :, by:ey]
+                if which == 0:
+                    total = total + edge_lanes(a, c, LANES - 2, 5, slot)
+                else:
+                    total = total + edge_lanes(r_ref[k, :, 0:LANES], c, 2 * LANES - 3, 5, slot)
+                if 2 <= k < 2 + own_z:
+                    v = x_all[k - 2, :, by:ey]
+                    total_x = total_x + one_tile_lanes(v, 0 if which == 0 else LANES - 2, 2, slot + 5)
+            edges[which, group * ex:(group + 1) * ex, :] = total
+            edges[which, group * ex:group * ex + bx, :] += total_x
+
+    nz1, nx1, _ = b1.shape
+    zp_rows = nz1 // 2 * nx1 // 2
+    own_rows = nx1 // 2
+    base = 8 * layers
+    row = iota((own_rows, ey), 0)
+    row8 = iota((8, ey), 0)
+    for zp in range(nz1 // 2):
+        at = base + zp * own_rows
+        ours, theirs = mine[at - base:at - base + own_rows, :], got[at:at + own_rows, :]
+        low, high = jnp.where(up, ours, theirs), jnp.where(up, theirs, ours)
+        at = zp_rows + (zp // 2) * 8
+        ours, theirs = mine[at:at + 8, :], got[base + at:base + at + 8, :]
+        low_spill, high_spill = jnp.where(up, ours, theirs), jnp.where(up, theirs, ours)
+        if zp % 2 == 0:
+            high_spill = pltpu.roll(high_spill, 4, 0)
+        else:
+            low_spill = pltpu.roll(low_spill, 4, 0)
+        low_add = jnp.where(row8 >= 6, high_spill, 0.0)
+        high_add = jnp.where(row8 < 2, low_spill, 0.0)
+        for part in range(2):
+            lanes = slice(part * LANES, (part + 1) * LANES)
+            b1[2 * zp + part, 0:own_rows, :] = low[:, lanes]
+            b1[2 * zp + part, own_rows:nx1, :] = high[:, lanes]
+            b1[2 * zp + part, own_rows - 8:own_rows, :] += low_add[:, lanes]
+            b1[2 * zp + part, own_rows:own_rows + 8, :] += high_add[:, lanes]
+
+    lateral1 = level_lateral((nx1, LANES))
+    keep = wrapped_mask((nx1, LANES), {1: by // 2}, (None, y_low), (None, y_high))
+    for k in range(nz1):
+        d1[k] = b1[k] * first_scale
+    for k in range(nz1):
+        r = b1[k] - apply_at(d1, k, lateral1)
+        r1_ref[k] = r
+        d2[k] = keep * (carry_coef * d1[k] + fresh_coef * r)
+    for k in range(nz1):
+        r1_ref[k] = keep * (r1_ref[k] - apply_at(d2, k, lateral1))
+        x1_ref[k] = d1[k] + d2[k]
+
+    for zc in range(nz1 // 2):
+        pairs[zc * nx1:(zc + 1) * nx1, :] = r1_ref[2 * zc] + r1_ref[2 * zc + 1]
+        lines[zc * own_rows:(zc + 1) * own_rows, :] = (
+            pairs[pl.ds(zc * nx1, own_rows, 2), :] + pairs[pl.ds(zc * nx1 + 1, own_rows, 2), :]
+        )
+    fine = signed(iota((LANES, LANES), 0), by // 2, LANES)
+    coarse = iota((LANES, LANES), 1) - iy * (by // 4)
+    sum_ref[...] = right_dot(lines[...], as_table((fine >> 1) == coarse, 0.5))
+
+    fine_rows = groups * ex
+    per_tile = LANES // 16
+    for which in range(2):
+        for group in range(nz1 // per_tile):
+            total = jnp.zeros((nx1, LANES), F32)
+            for j in range(per_tile):
+                k = group * per_tile + j
+                first = by // 2 - 3 if which == 0 else LANES - 4
+                total = total + one_tile_lanes(r1_ref[k], first, 7, 16 * j)
+                first = by // 2 - 2 if which == 0 else LANES - 3
+                total = total + one_tile_lanes(x1_ref[k], first, 5, 16 * j + 7)
+            at = fine_rows + group * nx1
+            edges[which, at:at + nx1, :] = total
+    for step, out in enumerate(slabs):
+        above, _ = side(iy, step)
+        out[...] = jnp.where(above, edges[0], edges[1])
+
+
+def level_lateral(shape):
+    row = iota(shape, 0)
+    not_first = jnp.where(row > 0, 1.0, 0.0).astype(F32)
+    not_last = jnp.where(row < shape[0] - 1, 1.0, 0.0).astype(F32)
+
+    def beside(v):
+        return (
+            not_first * pltpu.roll(v, 1, 0) + not_last * pltpu.roll(v, shape[0] - 1, 0)
+            + pltpu.roll(v, 1, 1) + pltpu.roll(v, LANES - 1, 1)
+        )
+
+    return beside
+
+
+def small_cycle(level, source, sizes):
+    nz, nx, ny = sizes
+    rows = source.shape[0]
+    row, lane = iota((rows, LANES), 0), iota((rows, LANES), 1)
+    inside = (row < nz * nx) & (lane < ny)
+
+    def factor(keep):
+        return jnp.where(keep & inside, 1.0, 0.0).astype(F32)
+
+    shifts = [(nx, 0, factor(row >= nx)), (rows - nx, 0, factor(row < (nz - 1) * nx))]
+    if nx > 1:
+        shifts += [(1, 0, factor(row % nx > 0)), (rows - 1, 0, factor(row % nx < nx - 1))]
+    shifts += [(1, 1, factor(lane > 0)), (LANES - 1, 1, factor(lane < ny - 1))]
+
+    def op(v):
+        beside = None
+        for shift, dim, keep in shifts:
+            moved = keep * (v if shift % v.shape[dim] == 0 else pltpu.roll(v, shift, dim))
+            beside = moved if beside is None else beside + moved
+        return 6.0 * v - beside
+
+    d = source * first_scale
+    r = source - op(d)
+    d2 = carry_coef * d + fresh_coef * r
+    x = d + d2
+    r = r - op(d2)
+    coarsest = None
+    if level < LEVELS - 1:
+        half = tuple(max(n // 2, 1) for n in sizes)
+        coarse_rows = max(half[0] * half[1], 8)
+        shape = (coarse_rows, rows)
+        fine, coarse = iota(shape, 1), iota(shape, 0)
+        wanted = (fine // nx // 2) * half[1] + fine % nx // 2
+        gather = (wanted == coarse) & (fine < nz * nx)
+        fine, coarse = iota((LANES, LANES), 0), iota((LANES, LANES), 1)
+        halve = as_table((fine // 2 == coarse) & (fine < ny), 0.5)
+        shape = (rows, coarse_rows)
+        fine, coarse = iota(shape, 0), iota(shape, 1)
+        wanted = (fine // nx // 2) * half[1] + fine % nx // 2
+        spread = as_table((wanted == coarse) & (fine < nz * nx))
+        fine, coarse = iota((LANES, LANES), 1), iota((LANES, LANES), 0)
+        double = as_table((fine // 2 == coarse) & (fine < ny))
+        e, coarsest = small_cycle(
+            level + 1, right_dot(left_dot(as_table(gather), r), halve), half
+        )
+        e = right_dot(left_dot(spread, e), double)
+        x = x + e
+        r = r - op(e)
+    d = r * first_scale
+    r = r - op(d)
+    x = x + d + (carry_coef * d + fresh_coef * r)
+    return x, (x if level == LEVELS - 1 else coarsest)
+
+
+def last_kernel(peers, steps, sizes, r_in, x_in, r1_in, x1_in, *refs):
+    slabs, (part_a, part_b) = refs[:steps], refs[steps:steps + 2]
+    p_ref, res_ref, last_ref = refs[steps + 2:steps + 5]
+    r, x, q1, e1, e0, d0, d1, r1, lines, wide = refs[steps + 5:]
+    layers, ex, ey = r_in.shape
+    nz1, nx1, _ = r1_in.shape
+    bz, bx, by = p_ref.shape
+    iz, z_low, z_high = place("gz", peers[0])
+    ix, x_low, x_high = place("gx", peers[1])
+    iy, y_low, y_high = place("gy", peers[2])
+
+    def pick(wanted_above, rows):
+        total = None
+        for step, slab in enumerate(slabs):
+            above, near = side(iy, step)
+            good = near & (above if wanted_above else jnp.logical_not(above))
+            term = jnp.where(good, slab[rows[0]:rows[1], :], 0.0)
+            total = term if total is None else total + term
+        return total
+
+    e2, coarsest = small_cycle(2, part_a[...] + part_b[...], sizes)
+    last_ref[...] = coarsest
+
+    fine = signed(iota((LANES, LANES), 1), by // 2, LANES)
+    coarse = iota((LANES, LANES), 0) - iy * (by // 4)
+    e2 = right_dot(e2, as_table((fine >> 1) == coarse))
+    half_x = nx1 // 2
+    lines[...] = e2
+    for zc in range(nz1 // 2):
+        v = lines[zc * half_x:(zc + 1) * half_x, :]
+        for part in range(2):
+            q1.at[2 * zc + part][pl.ds(0, half_x, 2), :] = v
+            q1.at[2 * zc + part][pl.ds(1, half_x, 2), :] = v
+    fine_rows = -(-layers // (LANES // 8)) * ex
+    per_tile = LANES // 16
+    lane = iota((nx1, LANES), 1)
+
+    def landed(v, slot, at, count):
+        gone = jnp.where(lane_of(v) >= at, lane_of(v) - at, lane_of(v) + LANES - at)
+        return jnp.where(gone < count, pltpu.roll(v, (at - slot) % LANES, 1), 0.0)
+
+    def lane_of(v):
+        return iota(v.shape, 1)
+
+    lateral1 = level_lateral((nx1, LANES))
+    keep = wrapped_mask((nx1, LANES), {1: by // 2}, (None, y_low), (None, y_high))
+    for group in range(nz1 // per_tile):
+        at = fine_rows + group * nx1
+        high, low = pick(True, (at, at + nx1)), pick(False, (at, at + nx1))
+        for j in range(per_tile):
+            k = group * per_tile + j
+            s = 16 * j
+            r1[k] = (
+                r1_in[k] + landed(high, s, by // 2 - 4, 7) + landed(low, s, LANES - 3, 7)
+                - apply_at(q1, k, lateral1)
+            )
+            e1[k + 2, 8:8 + nx1, :] = (
+                x1_in[k] + q1[k]
+                + landed(high, s + 7, by // 2 - 3, 5) + landed(low, s + 7, LANES - 2, 5)
+            )
+    for k in range(nz1):
+        d1[k] = keep * (r1[k] * first_scale)
+    nothing = jnp.zeros((8, LANES), F32)
+    for k in range(nz1 + 4):
+        e1[k, 0:8, :] = nothing
+        e1[k, 8 + nx1:16 + nx1, :] = nothing
+        if not 2 <= k < nz1 + 2:
+            e1[k, 8:8 + nx1, :] = jnp.zeros((nx1, LANES), F32)
+    for k in range(nz1):
+        v = r1[k] - apply_at(d1, k, lateral1)
+        e1[k + 2, 8:8 + nx1, :] += d1[k] + keep * (carry_coef * d1[k] + fresh_coef * v)
+
+    coarse = signed(iota((LANES, ey), 0), by // 2, LANES)
+    fine = signed(iota((LANES, ey), 1), by, ey)
+    double = as_table((fine >> 1) == coarse)
+    half_z, half_x = bz // 2, bx // 2
+    for zc in range(half_z + 4):
+        start = pl.multiple_of(ix * half_x, 8)
+        v = e1[iz * half_z + zc, pl.ds(start, half_x + 16), :]
+        own, low, high = v[8:8 + half_x], v[0:8], v[8 + half_x:16 + half_x]
+        at = zc * ex
+        wide[pl.ds(at, half_x, 2), :] = own
+        wide[pl.ds(at + 1, half_x, 2), :] = own
+        for j in range(2):
+            for twin in range(2):
+                row = at + bx + 2 * j + twin
+                wide[row:row + 1, :] = high[j:j + 1]
+                row = at + ex - 4 + 2 * j + twin
+                wide[row:row + 1, :] = low[6 + j:7 + j]
+    for zc in range(half_z + 4):
+        v = right_dot(wide[zc * ex:(zc + 1) * ex, :], double)
+        for k in (2 * zc - 1, 2 * zc):
+            if 0 <= k < bz + 6:
+                e0[k] = v
+    flat = wrapped_mask((ex, ey), {0: bx, 1: by}, (x_low, y_low), (x_high, y_high))
+    below = jnp.where(z_low, 1.0, 0.0).astype(F32)
+    above = jnp.where(z_high, 1.0, 0.0).astype(F32)
+
+    def masked(k, v):
+        v = v * flat
+        if k < 3:
+            v = v * below
+        if k >= 3 + bz:
+            v = v * above
+        return v
+
+    per_tile = LANES // 8
+    for group in range(-(-layers // per_tile)):
+        rows = (group * ex, (group + 1) * ex)
+        high, low = pick(True, rows), pick(False, rows)
+        for k in range(group * per_tile, min(layers, (group + 1) * per_tile)):
+            s = 8 * (k % per_tile)
+            v = r_in[k] - apply_at(e0, k + 1)
+            own, spill = v[:, by - LANES:by], v[:, by:ey]
+            own = own + landed(high, s, LANES - 3, 3)
+            spill = spill + landed(high, s + 3, 0, 2) + landed(low, s, LANES - 2, 2)
+            if by > LANES:
+                r[k, :, 0:by - LANES] = v[:, 0:by - LANES]
+                r[k, :, by - LANES:by] = own
+                r[k, :, 0:LANES] += landed(low, s + 2, 0, 3)
+            else:
+                r[k, :, 0:LANES] = own + landed(low, s + 2, 0, 3)
+            r[k, :, by:ey] = spill
+            d0[k] = masked(k + 1, r[k] * first_scale)
+            if 2 <= k < 2 + bz:
+                x[k - 2] = x_in[k - 2] + e0[k + 1, 0:bx, 0:by]
+                x[k - 2, :, by - LANES:by] += landed(high, s + 5, LANES - 2, 2)[0:bx]
+                x[k - 2, :, 0:LANES] += landed(low, s + 5, 0, 2)[0:bx]
+    for k in range(1, layers - 1):
+        v = r[k] - apply_at(d0, k)
+        r[k] = v
+        e0[k] = masked(k + 1, carry_coef * d0[k] + fresh_coef * v)
+    for k in range(2, layers - 2):
+        p_ref[k - 2] = x[k - 2] + (d0[k, 0:bx, 0:by] + e0[k, 0:bx, 0:by])
+        v = r[k] - apply_at(e0, k)
+        res_ref[k - 2] = v[0:bx, 0:by]
+
+
+def whole(shape, dtype=F32):
+    return jax.ShapeDtypeStruct(shape, dtype)
+
+
+def run(kernel, outs, scratch, *operands):
+    return pl.pallas_call(
+        kernel,
+        out_shape=[whole(s) for s in outs],
+        in_specs=[pl.BlockSpec(memory_space=pltpu.VMEM)] * len(operands),
+        out_specs=[pl.BlockSpec(memory_space=pltpu.VMEM)] * len(outs),
+        scratch_shapes=[pltpu.VMEM(s, F32) for s in scratch],
+        compiler_params=pltpu.CompilerParams(vmem_limit_bytes=VMEM_BYTES),
+    )(*operands)
+
+
+def swap(values, axis, step):
+    count = lax.axis_size(axis)
+    flip = (2 << step) - 1
+    return lax.ppermute(values, axis, [(i, i ^ flip) for i in range(count)])
+
+
+def join_z(mine, got, index, step, half, rows):
+    above, _ = side(index, step)
+    out = []
+    at = 0
+    for width in (rows, 4):
+        a, b = mine[at:at + half * width], got[at:at + half * width]
+        low, high = jnp.where(above, a, b), jnp.where(above, b, a)
+        meet = 2 * width
+        out += [low[:-meet], low[-meet:] + high[:meet], high[meet:]]
+        at += half * width
+    return jnp.concatenate(out, axis=0)
+
+
+def body_fast(divergence, pressure_prev):
+    bz, bx, by = divergence.shape
+    peers = tuple(lax.axis_size(a) for a in ("gz", "gx", "gy"))
+    nz, nx, ny = peers
+    steps_z, steps_y = nz.bit_length() - 1, ny.bit_length() - 1
+    ez, ex, ey = bz + 6, bx + 8, by + LANES
+    rows, half = bx // 2, bz // 4 + 2
+    ext, slab = (ez, ex, ey), (7 * ex, ey)
+    coarse_rows = half * (rows + 4)
+    r, x, coarse, *slabs = run(
+        lambda *refs: first_kernel(peers, steps_z, *refs),
+        [ext, ext, (coarse_rows, 2 * LANES)] + [slab] * steps_z,
+        [ext, ext, ext, ext, (ey // LANES, (bz // 2 + 4) * ex, LANES),
+         (2, coarse_rows, ey)],
+        divergence, pressure_prev,
+    )
+    got = []
+    iz = lax.axis_index("gz")
+    for step in range(steps_z):
+        there = swap(jnp.concatenate([slabs[step], coarse], axis=0), "gz", step)
+        got.append(there[:7 * ex])
+        coarse = join_z(coarse, there[7 * ex:], iz, step, half, rows)
+        half = 2 * half - 2
+    inner = half - 2
+    coarse = jnp.concatenate(
+        [coarse[rows:half * rows - rows], coarse[half * rows + 4:half * (rows + 4) - 4]], axis=0
+    )
+    layers = bz + 4
+    r, x, slab_x = run(
+        lambda *refs: z_kernel(peers, steps_z, *refs),
+        [(layers, ex, ey), (bz, ex, ey), (layers * 8, ey)],
+        [],
+        r, x, *got,
+    )
+    there = swap(jnp.concatenate([slab_x, coarse], axis=0), "gx", 0)
+    nz1, nx1 = nz * bz // 2, nx * bx // 2
+    level1 = (nz1, nx1, LANES)
+    edge_rows = -(-layers // (LANES // 8)) * ex + nz1 // (LANES // 16) * nx1
+    level2_rows = nz1 // 2 * nx1 // 2
+    r, x, r1, x1, total, *slabs = run(
+        lambda *refs: y_kernel(peers, steps_y, *refs),
+        [(layers, ex, ey), (bz, bx, by), level1, level1, (level2_rows, LANES)]
+        + [(edge_rows, LANES)] * steps_y,
+        [level1, level1, level1, (bz, bx, ey), (nz1 // 2 * nx1, LANES), (level2_rows, LANES),
+         (2, edge_rows, LANES)],
+        r, x, coarse, there,
+    )
+    got = []
+    other = None
+    for step in range(steps_y):
+        if other is not None:
+            total = total + other
+        there = swap(jnp.concatenate([slabs[step], total], axis=0), "gy", step)
+        got.append(there[:edge_rows])
+        other = there[edge_rows:]
+    sizes = (nz1 // 2, nx1 // 2, ny * by // 4)
+    pressure, residual, last = run(
+        lambda *refs: last_kernel(peers, steps_y, sizes, *refs),
+        [divergence.shape, divergence.shape, (8, LANES)],
+        [(layers, ex, ey), divergence.shape, level1, (nz1 + 4, nx1 + 16, LANES), ext,
+         (layers, ex, ey), level1, level1, (level2_rows, LANES), ((bz // 2 + 4) * ex, LANES)],
+        r, x, r1, x1, *got, total, other,
+    )
+    z5, x5, y5 = (n >> 3 for n in sizes)
+    coarsest = last[:z5 * x5, :y5].reshape(z5, x5, y5)
+    return pressure, residual, coarsest
+
+
+VMEM_BYTES = 24 << 20
+
+
+def fits_fast(shape, peers):
+    bz, bx, by = shape
+    nz, nx, ny = peers
+    return (
+        nx == 2 and nz > 1 and ny > 1 and not (nz & (nz - 1) or ny & (ny - 1))
+        and bz % 16 == 0 and bx == 16 and by == LANES and ny * by // 4 <= LANES
+        and nz * bz <= 128
+    )
+
+
+def body(divergence, pressure_prev):
+    peers = tuple(lax.axis_size(a) for a in ("gz", "gx", "gy"))
+    if fits_fast(divergence.shape, peers):
+        return body_fast(divergence, pressure_prev)
+    return body_levels(divergence, pressure_prev)
 
 
 def solution(mesh):

time: 388 us -> 45.1 us (0.12)
  the two profiles are of different devices: /device:TPU:30 before, /device:TPU:0 now
where the time goes in v2:
time: 45.1 us; the launch traced here: 44.9 us
  waiting for transfers between devices  23 us (51%)
  starting transfers between devices  11.2 us (25%)
  Pallas kernels  7.32 us (16%)
  local copies, waits for them, and re-layouts  2.46 us (5%)
  between operations  0.85 us (2%)
    ppermute x5, waiting for transfers between devices, swap(): return lax.ppermute(values, axis, [(i, i ^ flip) for i in range(count)])  23 us
    ppermute x5, starting transfers between devices, swap(): return lax.ppermute(values, axis, [(i, i ^ flip) for i in range(count)])  11.2 us
    pallas_call x4, Pallas kernels, run(): pl.pallas_call(kernel, out_shape=[whole(s) for s in outs], in_specs=[pl.B...  7.32 us
    unnamed x5, local copies, waits for them, and re-layouts  1.81 us
  transfers between devices with their start and end apart: 5, of which 5 were waited for; matrix products, arithmetic and copies ran while one was open for 0% of the time, Pallas kernels for 0%

profile of v2, /device:TPU:0, one launch (start us, length us, event | category | flops | bytes accessed | tf_op | source)
XLA Modules:
  0.0 44.9 jit_solution(12475141870280084665)
XLA Ops:
  0.6 0.0 copy-start
  0.6 0.9 %copy-done = f32[16,16,128]{2,1,0:T(8,128)S(1)} copy-done((f32[16,16,128]{2,1,0:T(8,128)S(1)}, f32[16,16,128]{2,1,0:T(8,128)}, u32[]{:S(2)}) %copy-start) | copy-done | bytes 131096
  1.5 0.0 copy-start.1
  1.5 0.9 %copy-done.1 = f32[16,16,128]{2,1,0:T(8,128)S(1)} copy-done((f32[16,16,128]{2,1,0:T(8,128)S(1)}, f32[16,16,128]{2,1,0:T(8,128)}, u32[]{:S(2)}) %copy-start.1) | copy-done | bytes 131096
  2.4 1.1 %shard_map.49 = (f32[22,24,256]{2,1,0:T(8,128)S(1)}, f32[22,24,256]{2,1,0:T(8,128)S(1)}, f32[72,256]{1,0:T(8,128)S(1)}, f32[168,256]{1,0:T(8,128)S(1)}, f32[168,256]{1,0:T(8,128)S(1)}) custom-call(f32[16,16,128]{2,1,0:T(8,128)S(1)} %copy-done, f32[16,16,128]{2,1,0:T(8,128)S(1)} %copy-done.1), custom_call_target="tpu_custom_call" | custom-call | tf_op jit(solution)/shard_map/pallas_call | solution.py:658
  3.6 0.5 %collective-permute-start = (f32[240,256]{1,0:T(8,128)S(1)}, f32[240,256]{1,0:T(8,128)S(1)}, u32[]{:S(2)}, u32[]{:S(2)}) collective-permute-start(f32[240,256]{1,0:T(8,128)S(1)} %pad_maximum_fusion.1), channel_id=1, source_target_pairs={{0,1},{1,0},{2,3},{3,2},{4,5},{5,4},{6,7},{7,6},{8,9},{9,8},{10,11... | collective-permute-start | bytes 737288 | tf_op jit(solution)/shard_map/ppermute | solution.py:671
  4.2 1.1 %collective-permute-done = f32[240,256]{1,0:T(8,128)S(1)} collective-permute-done((f32[240,256]{1,0:T(8,128)S(1)}, f32[240,256]{1,0:T(8,128)S(1)}, u32[]{:S(2)}, u32[]{:S(2)}) %collective-permute-start) | collective-permute-done | bytes 245792 | tf_op jit(solution)/shard_map/ppermute | solution.py:671
  5.4 2.7 %collective-permute-start.1 = (f32[288,256]{1,0:T(8,128)S(1)}, f32[288,256]{1,0:T(8,128)S(1)}, u32[]{:S(2)}, u32[]{:S(2)}) collective-permute-start(f32[288,256]{1,0:T(8,128)S(1)} %get-tuple-element.61), channel_id=1, source_target_pairs={{0,3},{1,2},{2,1},{3,0},{4,7},{5,6},{6,5},{7,4},{8,11},{9,10},{10,... | collective-permute-start | bytes 884744 | tf_op jit(solution)/shard_map/ppermute | solution.py:671
  8.1 7.1 %collective-permute-done.1 = f32[288,256]{1,0:T(8,128)S(1)} collective-permute-done((f32[288,256]{1,0:T(8,128)S(1)}, f32[288,256]{1,0:T(8,128)S(1)}, u32[]{:S(2)}, u32[]{:S(2)}) %collective-permute-start.1) | collective-permute-done | bytes 294944 | tf_op jit(solution)/shard_map/ppermute | solution.py:671
  15.3 0.1 shard_map.50
  15.5 2.3 %collective-permute-start.2 = (f32[352,256]{1,0:T(8,128)S(1)}, f32[352,256]{1,0:T(8,128)S(1)}, u32[]{:S(2)}, u32[]{:S(2)}) collective-permute-start(f32[352,256]{1,0:T(8,128)S(1)} %pad_maximum_fusion), channel_id=1, source_target_pairs={{0,16},{16,0},{1,17},{17,1},{2,18},{18,2},{3,19},{19,3},{4,20},{20... | collective-permute-start | bytes 1081352 | tf_op jit(solution)/shard_map/ppermute | solution.py:671
  17.8 8.7 %collective-permute-done.2.refs_3_ = f32[352,256]{1,0:T(8,128)S(1)} collective-permute-done((f32[352,256]{1,0:T(8,128)S(1)}, f32[352,256]{1,0:T(8,128)S(1)}, u32[]{:S(2)}, u32[]{:S(2)}) %collective-permute-start.2) | collective-permute-done | bytes 360480 | tf_op jit(solution)/shard_map/ppermute | solution.py:671
  26.5 0.9 %shard_map.51 = (f32[20,24,256]{2,1,0:T(8,128)S(1)}, f32[16,16,128]{2,1,0:T(8,128)S(1)}, f32[32,16,128]{2,1,0:T(8,128)S(1)}, f32[32,16,128]{2,1,0:T(8,128)S(1)},...) custom-call(f32[20,24,256]{2,1,0:T(8,128)S(1)} %get-tuple-element.26.refs_0_, ...), custom_call_target="tpu_custom_call" | custom-call | tf_op jit(solution)/shard_map/pallas_call | solution.py:658
  27.4 1.9 %collective-permute-start.3 = (f32[240,128]{1,0:T(8,128)S(1)}, f32[240,128]{1,0:T(8,128)S(1)}, u32[]{:S(2)}, u32[]{:S(2)}) collective-permute-start(f32[240,128]{1,0:T(8,128)S(1)} %pad_maximum_fusion.5), channel_id=1, source_target_pairs={{0,4},{4,0},{8,12},{12,8},{1,5},{5,1},{9,13},{13,9},{2,6},{6,2},{1... | collective-permute-start | bytes 368648 | tf_op jit(solution)/shard_map/ppermute | solution.py:671
  29.3 3.1 %collective-permute-done.3 = f32[240,128]{1,0:T(8,128)S(1)} collective-permute-done((f32[240,128]{1,0:T(8,128)S(1)}, f32[240,128]{1,0:T(8,128)S(1)}, u32[]{:S(2)}, u32[]{:S(2)}) %collective-permute-start.3) | collective-permute-done | bytes 122912 | tf_op jit(solution)/shard_map/ppermute | solution.py:671
  32.4 3.9 %collective-permute-start.4 = (f32[240,128]{1,0:T(8,128)S(1)}, f32[240,128]{1,0:T(8,128)S(1)}, u32[]{:S(2)}, u32[]{:S(2)}) collective-permute-start(f32[240,128]{1,0:T(8,128)S(1)} %pad_maximum_fusion.6), channel_id=1, source_target_pairs={{0,12},{4,8},{8,4},{12,0},{1,13},{5,9},{9,5},{13,1},{2,14},{6,10},... | collective-permute-start | bytes 368648 | tf_op jit(solution)/shard_map/ppermute | solution.py:671
  36.3 3.0 %collective-permute-done.4 = f32[240,128]{1,0:T(8,128)S(1)} collective-permute-done((f32[240,128]{1,0:T(8,128)S(1)}, f32[240,128]{1,0:T(8,128)S(1)}, u32[]{:S(2)}, u32[]{:S(2)}) %collective-permute-start.4) | collective-permute-done | bytes 122912 | tf_op jit(solution)/shard_map/ppermute | solution.py:671
  39.3 5.1 %shard_map.52 = (f32[16,16,128]{2,1,0:T(8,128)}, f32[16,16,128]{2,1,0:T(8,128)}, f32[8,128]{1,0:T(8,128)S(1)}) custom-call(f32[20,24,256]{2,1,0:T(8,128)S(1)} %get-tuple-element.29.refs_0_, f32[16,16,128]{2,1,0:T(8,128)S(1)} %get-tuple-element.30.refs_1_, f32[32,16,128]{2,1,0:T(8,128)S(1)} %get-tuple-element.31.refs_2_, ...), custom_call_target="tpu_custom_call" | custom-call | tf_op jit(solution)/shard_map/pallas_call | solution.py:658
  44.4 0.6 %slice.135 = f32[2,16]{1,0:T(2,128)} slice(f32[8,128]{1,0:T(8,128)S(1)} %get-tuple-element.38), slice={[0:2], [0:16]} | slice | bytes 256 | tf_op jit(solution)/shard_map/slice | solution.py:751
  (30 shorter events, 0.3 us)
Async XLA Ops:
  0.6 0.9 %copy-start = (f32[16,16,128]{2,1,0:T(8,128)S(1)}, f32[16,16,128]{2,1,0:T(8,128)}, u32[]{:S(2)}) copy-start(f32[16,16,128]{2,1,0:T(8,128)} %refs_0_.1) | copy-start | bytes 393220
  1.5 0.9 %copy-start.1 = (f32[16,16,128]{2,1,0:T(8,128)S(1)}, f32[16,16,128]{2,1,0:T(8,128)}, u32[]{:S(2)}) copy-start(f32[16,16,128]{2,1,0:T(8,128)} %refs_1_.1) | copy-start | bytes 393220
  3.6 1.7 %collective-permute-start = (f32[240,256]{1,0:T(8,128)S(1)}, f32[240,256]{1,0:T(8,128)S(1)}, u32[]{:S(2)}, u32[]{:S(2)}) collective-permute-start(f32[240,256]{1,0:T(8,128)S(1)} %pad_maximum_fusion.1), channel_id=1, source_target_pairs={{0,1},{1,0},{2,3},{3,2},{4,5},{5,4},{6,7},{7,6},{8,9},{9,8},{10,11... | collective-permute-start | bytes 737288 | tf_op jit(solution)/shard_map/ppermute | solution.py:671
  5.4 9.8 %collective-permute-start.1 = (f32[288,256]{1,0:T(8,128)S(1)}, f32[288,256]{1,0:T(8,128)S(1)}, u32[]{:S(2)}, u32[]{:S(2)}) collective-permute-start(f32[288,256]{1,0:T(8,128)S(1)} %get-tuple-element.61), channel_id=1, source_target_pairs={{0,3},{1,2},{2,1},{3,0},{4,7},{5,6},{6,5},{7,4},{8,11},{9,10},{10,... | collective-permute-start | bytes 884744 | tf_op jit(solution)/shard_map/ppermute | solution.py:671
  15.5 11.0 %collective-permute-start.2 = (f32[352,256]{1,0:T(8,128)S(1)}, f32[352,256]{1,0:T(8,128)S(1)}, u32[]{:S(2)}, u32[]{:S(2)}) collective-permute-start(f32[352,256]{1,0:T(8,128)S(1)} %pad_maximum_fusion), channel_id=1, source_target_pairs={{0,16},{16,0},{1,17},{17,1},{2,18},{18,2},{3,19},{19,3},{4,20},{20... | collective-permute-start | bytes 1081352 | tf_op jit(solution)/shard_map/ppermute | solution.py:671
  27.4 4.9 %collective-permute-start.3 = (f32[240,128]{1,0:T(8,128)S(1)}, f32[240,128]{1,0:T(8,128)S(1)}, u32[]{:S(2)}, u32[]{:S(2)}) collective-permute-start(f32[240,128]{1,0:T(8,128)S(1)} %pad_maximum_fusion.5), channel_id=1, source_target_pairs={{0,4},{4,0},{8,12},{12,8},{1,5},{5,1},{9,13},{13,9},{2,6},{6,2},{1... | collective-permute-start | bytes 368648 | tf_op jit(solution)/shard_map/ppermute | solution.py:671
  32.4 6.9 %collective-permute-start.4 = (f32[240,128]{1,0:T(8,128)S(1)}, f32[240,128]{1,0:T(8,128)S(1)}, u32[]{:S(2)}, u32[]{:S(2)}) collective-permute-start(f32[240,128]{1,0:T(8,128)S(1)} %pad_maximum_fusion.6), channel_id=1, source_target_pairs={{0,12},{4,8},{8,4},{12,0},{1,13},{5,9},{9,5},{13,1},{2,14},{6,10},... | collective-permute-start | bytes 368648 | tf_op jit(solution)/shard_map/ppermute | solution.py:671

commit v3 on v0

--- a/solution.py
+++ b/solution.py
@@ -1,6 +1,10 @@
+import functools
+
 import jax
 import jax.numpy as jnp
 from jax import lax
+from jax.experimental import pallas as pl
+from jax.experimental.pallas import tpu as pltpu
 from jax.sharding import PartitionSpec as P
 
 LEVELS = 6
@@ -11,26 +15,27 @@
 carry_coef = 0.6 * rho_one
 fresh_coef = 2.0 * rho_one / (0.75 * 6.0)
 
-
-def extended(x, sides, width):
-    for axis, dim in sides:
-        peers, length = (lax.axis_size(axis), x.shape[dim])
+LANES = 128
+F32 = jnp.float32
+AXES = (("gz", 0), ("gx", 1), ("gy", 2))
+
+
+def extended(x, width):
+    for axis, dim in AXES:
+        peers, length = (lax.axis_size(axis), x.shape[dim + 1])
         up = [(i, (i + 1) % peers) for i in range(peers - 1)]
         down = [(j, i) for i, j in up]
-        last = lax.slice_in_dim(x, length - width, length, axis=dim)
-        first = lax.slice_in_dim(x, 0, width, axis=dim)
+        last = lax.slice_in_dim(x, length - width, length, axis=dim + 1)
+        first = lax.slice_in_dim(x, 0, width, axis=dim + 1)
         before = lax.ppermute(last, axis, up)
         after = lax.ppermute(first, axis, down)
-        x = jnp.concatenate([before, x, after], axis=dim)
+        x = jnp.concatenate([before, x, after], axis=dim + 1)
     return x
 
 
 def stencil(values):
     padded = jnp.pad(values, 1)
-    beside = padded[2:, 1:-1, 1:-1] + padded[:-2, 1:-1, 1:-1]
-    beside = beside + padded[1:-1, 2:, 1:-1] + padded[1:-1, :-2, 1:-1]
-    beside = beside + padded[1:-1, 1:-1, 2:] + padded[1:-1, 1:-1, :-2]
-    return 6.0 * values - beside
+    return valid_op(padded)
 
 
 def valid_op(padded):
@@ -38,11 +43,6 @@
     beside = beside + padded[1:-1, 2:, 1:-1] + padded[1:-1, :-2, 1:-1]
     beside = beside + padded[1:-1, 1:-1, 2:] + padded[1:-1, 1:-1, :-2]
     return 6.0 * padded[1:-1, 1:-1, 1:-1] - beside
-
-
-def local_stencil(values):
-    padded = extended(values, (("gz", 0), ("gx", 1), ("gy", 2)), 1)
-    return valid_op(padded)
 
 
 def smooth_pass(iterate, source, apply_op, from_zero):
@@ -87,6 +87,10 @@
     return lax.all_gather(gathered, "gx", axis=1, tiled=True)
 
 
+def local_stencil(values):
+    return valid_op(extended(values[None], 1)[0])
+
+
 def own_block(whole, block_shape):
     start_z = lax.axis_index("gz") * block_shape[0]
     start_x = lax.axis_index("gx") * block_shape[1]
@@ -106,11 +110,783 @@
     return (smooth_pass(iterate, source, local_stencil, False), coarsest)
 
 
-def body(divergence, pressure_prev):
-    gather_at = 3
-    pressure, coarse_correction = body_cycle(0, pressure_prev, divergence, False, gather_at)
+def body_levels(divergence, pressure_prev):
+    pressure, coarse_correction = body_cycle(0, pressure_prev, divergence, False, 3)
     residual = divergence - local_stencil(pressure)
     return (pressure, residual, coarse_correction)
+
+
+def iota(shape, dim):
+    return lax.broadcasted_iota(jnp.int32, shape, dim)
+
+
+def signed(index, size, extent):
+    return jnp.where(index >= (size + extent) // 2, index - extent, index)
+
+
+def split(values):
+    terms = []
+    for _ in range(3):
+        term = values.astype(jnp.bfloat16)
+        terms.append(term)
+        values = values - term.astype(F32)
+    return terms
+
+
+def right_dot(values, table):
+    parts = [jnp.dot(t, table, preferred_element_type=F32) for t in split(values)]
+    return parts[0] + parts[1] + parts[2]
+
+
+def left_dot(table, values):
+    parts = [jnp.dot(table, t, preferred_element_type=F32) for t in split(values)]
+    return parts[0] + parts[1] + parts[2]
+
+
+def as_table(keep, value=1.0):
+    return jnp.where(keep, value, 0.0).astype(jnp.bfloat16)
+
+
+def lateral(v):
+    rows, lanes = v.shape
+    return (
+        pltpu.roll(v, 1, 0) + pltpu.roll(v, rows - 1, 0)
+        + pltpu.roll(v, 1, 1) + pltpu.roll(v, lanes - 1, 1)
+    )
+
+
+def apply_at(ref, k, lateral_of=lateral):
+    centre = ref[k]
+    beside = lateral_of(centre)
+    if k > 0:
+        beside = beside + ref[k - 1]
+    if k < ref.shape[0] - 1:
+        beside = beside + ref[k + 1]
+    return 6.0 * centre - beside
+
+
+def wrapped_mask(shape, sizes, low, high):
+    keep = None
+    for dim, size in sizes.items():
+        at = signed(iota(shape, dim), size, shape[dim])
+        good = ((at >= 0) | low[dim]) & ((at < size) | high[dim])
+        keep = good if keep is None else keep & good
+    return jnp.where(keep, 1.0, 0.0).astype(F32)
+
+
+def side(index, flip):
+    if flip == 1:
+        return (index & 1) == 0, None
+    return index < 2, (index == 1) | (index == 2)
+
+
+def place(axis, count):
+    index = lax.axis_index(axis)
+    return index, index > 0, index < count - 1
+
+
+def only(keep, v):
+    return jnp.where(keep, v, 0.0)
+
+
+def shifted(v, lanes):
+    lanes = lanes % LANES
+    return v if lanes == 0 else pltpu.roll(v, lanes, 1)
+
+
+def lanes_of(v, first, count):
+    lane = iota(v.shape, 1)
+    last = first + count
+    if last <= LANES:
+        return (lane >= first) & (lane < last)
+    return (lane >= first) | (lane < last - LANES)
+
+
+def moved(v, first, count, to):
+    first = first % LANES
+    return shifted(only(lanes_of(v, first, count), v), to - first)
+
+
+def side_pack(tile, slot):
+    return moved(tile, LANES - 3, 6, 8 * slot)
+
+
+def side_unpack(packed, slot):
+    return moved(packed, 8 * slot, 6, LANES - 3)
+
+
+SLOTS = LANES // 8
+
+
+def slab_emit(r_ref, x_ref, out, at, up):
+    ez, ex, _ = r_ref.shape
+    start = jnp.where(up, ez - 5, 0)
+    start_x = jnp.where(up, ez - 3, 1)
+    lat = None
+    for j in range(7):
+        v = r_ref[start + j] if j < 5 else x_ref[start_x + j - 5]
+        out[at + j * ex:at + (j + 1) * ex, :] = v[:, 0:LANES]
+        part = side_pack(v[:, LANES:], j)
+        lat = part if lat is None else lat + part
+    out[at + 7 * ex:at + 8 * ex, :] = lat
+
+
+def slab_add(r_ref, x_ref, slab, at, up):
+    ez, ex, _ = r_ref.shape
+    start = jnp.where(up, ez - 6, 1)
+    start_x = jnp.where(up, ez - 5, 3)
+    lat = slab[at + 7 * ex:at + 8 * ex, :]
+    for j in range(7):
+        ref, k = (r_ref, start + j) if j < 5 else (x_ref, start_x + j - 5)
+        ref[k, :, 0:LANES] += slab[at + j * ex:at + (j + 1) * ex, :]
+        ref[k, :, LANES:] += side_unpack(lat, j)
+
+
+def rows_out(r, x, up):
+    bx = r.shape[0] - 8
+    row = iota((8, r.shape[1]), 0)
+    first, last, spill = r[0:8], r[bx - 8:bx], r[bx:]
+    to_high = pltpu.roll(jnp.where(row >= 6, last, spill), 2, 0)
+    to_low = pltpu.roll(jnp.where(row >= 5, spill, first), 3, 0)
+    out = jnp.where(up, to_high, to_low)
+    if x is None:
+        return only(row < 5, out)
+    spill = x[bx:]
+    extra = jnp.where(up, pltpu.roll(spill, 5, 0), pltpu.roll(spill, 7, 0))
+    return jnp.where(row < 5, out, only(row < 7, extra))
+
+
+def rows_in(r_ref, x_ref, k, rows, up):
+    bx = r_ref.shape[1] - 8
+    row = iota(rows.shape, 0)
+    high, low = pltpu.roll(rows, 5, 0), pltpu.roll(rows, 6, 0)
+    r_ref[k, 0:8] += only(jnp.logical_not(up) & (row < 3), low)
+    r_ref[k, bx - 8:bx] += only(up & (row >= 5), high)
+    r_ref[k, bx:] += jnp.where(up, only(row < 2, high), only(row >= 6, low))
+    if x_ref is not None:
+        x_ref[k, 0:8] += only(jnp.logical_not(up) & (row < 2), pltpu.roll(rows, 3, 0))
+        x_ref[k, bx - 8:bx] += only(up & (row >= 6), pltpu.roll(rows, 1, 0))
+
+
+class Plan:
+    def __init__(self, shape, peers):
+        self.peers = peers
+        self.block = bz, bx, by = shape
+        self.ext = self.ez, self.ex, self.ey = bz + 6, bx + 8, by + LANES
+        self.rows, self.pairs = bx // 2, bz // 4 + 2
+        self.lat_at = self.pairs * (self.rows + 4)
+        self.coarse = self.lat_at + 16
+        self.slab = 8 * self.ex
+        self.x_groups = -(-self.ez // SLOTS)
+        self.x_rows = (self.ez + self.x_groups) * 8
+        self.corner = 6 * 8
+        self.layers = bz + 4
+        self.level1 = (peers[0] * bz // 2, peers[1] * bx // 2, LANES)
+        self.level2 = (peers[0] * bz // 4, peers[1] * bx // 4, peers[2] * by // 4)
+        self.y_groups = -(-self.layers // SLOTS)
+        self.fine_rows = self.y_groups * self.ex
+        self.edge = self.fine_rows + self.level1[0] * self.level1[1] // 8
+        self.share = self.level2[0] * self.level2[1] // 2
+
+
+def first_kernel(plan, b_in, p_in, r_ref, x_ref, pay_z, pay_x, pay_d, *scratch):
+    b_own, p_own, b_ext, p_ext, d_one, d_two, pairs, lines, sem = scratch
+    bz, bx, by = plan.block
+    ez, ex, ey = plan.ext
+    peers = plan.peers
+    copies = [
+        pltpu.make_async_copy(p_in, p_own, sem.at[0]),
+        pltpu.make_async_copy(b_in, b_own, sem.at[1]),
+    ]
+    for copy in copies:
+        copy.start()
+    iz, z_low, z_high = place("gz", peers[0])
+    ix, x_low, x_high = place("gx", peers[1])
+    _, y_low, y_high = place("gy", peers[2])
+    flat = wrapped_mask((ex, ey), {0: bx, 1: by}, (x_low, y_low), (x_high, y_high))
+    below = jnp.where(z_low, 1.0, 0.0).astype(F32)
+    above = jnp.where(z_high, 1.0, 0.0).astype(F32)
+
+    def masked(k, v):
+        v = v * flat
+        if k < 3:
+            v = v * below
+        if k >= 3 + bz:
+            v = v * above
+        return v
+
+    zero = jnp.zeros((ex, ey), F32)
+    for k in range(ez):
+        p_ext[k] = zero
+        b_ext[k] = zero
+    for copy in copies:
+        copy.wait()
+    for k in range(bz):
+        b_ext[k + 3, 0:bx, 0:by] = b_own[k]
+        p_ext[k + 3, 0:bx, 0:by] = p_own[k]
+    for k in range(ez):
+        if 2 <= k < ez - 2:
+            r = b_ext[k] - apply_at(p_ext, k)
+            r_ref[k] = r
+            d_one[k] = masked(k, r * first_scale)
+        else:
+            d_one[k] = zero
+    for k in range(ez):
+        if 1 <= k < ez - 1:
+            r = -apply_at(d_one, k)
+            if 2 <= k < ez - 2:
+                r = r + r_ref[k]
+            r_ref[k] = r
+            d_two[k] = masked(k, carry_coef * d_one[k] + fresh_coef * r)
+        else:
+            d_two[k] = zero
+    for k in range(ez):
+        r = -apply_at(d_two, k)
+        if 1 <= k < ez - 1:
+            r = r + r_ref[k]
+        r_ref[k] = masked(k, r)
+        x_ref[k] = p_ext[k] + d_one[k] + d_two[k]
+
+
+    coarse_z, rows = 2 * plan.pairs, plan.rows
+    for zc in range(coarse_z):
+        low, high = 2 * zc - 1, 2 * zc
+        if low < 0:
+            total = r_ref[high]
+        elif high >= ez:
+            total = r_ref[low]
+        else:
+            total = r_ref[low] + r_ref[high]
+        base = zc * ex
+        for tile in range(ey // LANES):
+            here = slice(tile * LANES, (tile + 1) * LANES)
+            pairs[tile, base:base + ex, :] = total[:, here]
+            even = pairs.at[tile][pl.ds(base, ex // 2, 2), :]
+            odd = pairs.at[tile][pl.ds(base + 1, ex // 2, 2), :]
+            sums = even + odd
+            at = zc // 2 * rows
+            lines[zc % 2, at:at + rows, here] = sums[0:rows]
+            at = plan.pairs * rows + zc // 2 * 4
+            lines[zc % 2, at:at + 4, here] = sums[rows:rows + 4]
+    fine = signed(iota((ey, LANES), 0), by, ey)
+    coarse = signed(iota((ey, LANES), 1), by // 2, LANES)
+    table = as_table((fine >> 1) == coarse, 0.5)
+    even, odd = right_dot(lines[0], table), right_dot(lines[1], table)
+    lane = iota(even.shape, 1)
+    at = plan.slab
+    pay_z[at:at + plan.lat_at, :] = jnp.where(lane < LANES // 2, even, shifted(odd, LANES // 2))
+    own_lat = spill_lat = None
+    row = iota((8, LANES), 0)
+    for zc in range(coarse_z):
+        source = (even, odd)[zc % 2]
+        base = zc // 2 * rows
+        tile = source[base:base + rows]
+        part = moved(tile, by // 2, 2, 4 * zc) + moved(tile, LANES - 2, 2, 4 * zc + 2)
+        own_lat = part if own_lat is None else own_lat + part
+        base = plan.pairs * rows + zc // 4 * 8
+        tile = source[base:base + 8]
+        if zc // 2 % 2:
+            tile = pltpu.roll(tile, 4, 0)
+        tile = only(row < 4, tile)
+        part = moved(tile, by // 2, 2, 4 * zc) + moved(tile, LANES - 2, 2, 4 * zc + 2)
+        spill_lat = part if spill_lat is None else spill_lat + part
+    at = plan.slab + plan.lat_at
+    pay_z[at:at + 8, :] = own_lat
+    pay_z[at + 8:at + 16, :] = spill_lat
+    block = pay_z[plan.slab:plan.slab + plan.coarse, :]
+    pay_x[plan.x_rows:plan.x_rows + plan.coarse, :] = block
+    pay_d[plan.corner:plan.corner + plan.coarse, :] = block
+
+    up_z, _ = side(iz, 3)
+    up_x, _ = side(ix, 1)
+    slab_emit(r_ref, x_ref, pay_z, 0, up_z)
+    for group in range(plan.x_groups):
+        lat = jnp.zeros((8, LANES), F32)
+        for k in range(group * SLOTS, min(ez, (group + 1) * SLOTS)):
+            out = rows_out(r_ref[k], x_ref[k], up_x)
+            pay_x[8 * k:8 * k + 8, :] = out[:, 0:LANES]
+            lat = lat + side_pack(out[:, LANES:], k - group * SLOTS)
+        pay_x[8 * (ez + group):8 * (ez + group) + 8, :] = lat
+    start = jnp.where(up_z, ez - 5, 0)
+    lat = jnp.zeros((8, LANES), F32)
+    for j in range(5):
+        out = rows_out(r_ref[start + j], x_ref[start + j] if j == 2 else None, up_x)
+        pay_d[8 * j:8 * j + 8, :] = out[:, 0:LANES]
+        lat = lat + side_pack(out[:, LANES:], j)
+    pay_d[40:48, :] = lat
+
+
+def chip_kernel(plan, r_in, x_in, ours, from_z, from_x, from_d, r_ref, x_ref, pay):
+    ez, ex, ey = plan.ext
+    iz, _, _ = place("gz", plan.peers[0])
+    ix, _, _ = place("gx", plan.peers[1])
+    up_z, near = side(iz, 3)
+    up_x, _ = side(ix, 1)
+    for k in range(ez):
+        r_ref[k] = r_in[k]
+        x_ref[k] = x_in[k]
+        lat = from_x[8 * (ez + k // SLOTS):8 * (ez + k // SLOTS) + 8, :]
+        rows = from_x[8 * k:8 * k + 8, :]
+        rows = jnp.concatenate([rows, side_unpack(lat, k % SLOTS)], axis=1)
+        rows_in(r_ref, x_ref, k, rows, up_x)
+
+    @pl.when(near)
+    def _():
+        slab_add(r_ref, x_ref, from_z, 0, up_z)
+        start = jnp.where(up_z, ez - 6, 1)
+        lat = from_d[40:48, :]
+        for j in range(5):
+            rows = from_d[8 * j:8 * j + 8, :]
+            rows = jnp.concatenate([rows, side_unpack(lat, j)], axis=1)
+            rows_in(r_ref, x_ref if j == 2 else None, start + j, rows, up_x)
+
+    up, _ = side(iz, 1)
+    slab_emit(r_ref, x_ref, pay, 0, up)
+    for j, (ref, at) in enumerate(
+        ((ours, plan.slab), (from_z, plan.slab), (from_x, plan.x_rows), (from_d, plan.corner))
+    ):
+        here = plan.slab + j * plan.coarse
+        pay[here:here + plan.coarse, :] = ref[at:at + plan.coarse, :]
+
+
+def plane_kernel(plan, r_in, x_in, ours, theirs, r_ref, x_ref, r1_ref, x1_ref, pay_a, pay_b, pay_c,
+                 r_all, x_all, b1, d1, d2, pairs, lines):
+    bz, bx, by = plan.block
+    ez, ex, ey = plan.ext
+    layers = plan.layers
+    iz, _, _ = place("gz", plan.peers[0])
+    ix, _, _ = place("gx", plan.peers[1])
+    iy, y_low, y_high = place("gy", plan.peers[2])
+    up, _ = side(iz, 1)
+    for k in range(ez):
+        r_all[k] = r_in[k]
+        x_all[k] = x_in[k]
+    slab_add(r_all, x_all, theirs, 0, up)
+    for k in range(layers):
+        r_ref[k] = r_all[k + 1]
+    for k in range(bz):
+        x_ref[k] = x_all[k + 3, 0:bx, 0:by]
+
+    up_a, _ = side(iy, 1)
+    up_b, _ = side(iy, 3)
+    edges = []
+    for which in range(2):
+        tiles = []
+        for group in range(plan.y_groups):
+            total = jnp.zeros((ex, LANES), F32)
+            for k in range(group * SLOTS, min(layers, (group + 1) * SLOTS)):
+                slot = 8 * (k - group * SLOTS)
+                v, spill = r_all[k + 1, :, 0:by], r_all[k + 1, :, by:ey]
+                if which == 0:
+                    total = total + moved(jnp.where(lanes_of(v, 0, 3), spill, v), LANES - 2, 5, slot)
+                else:
+                    total = total + moved(jnp.where(lanes_of(v, 0, 2), v, spill), LANES - 3, 5, slot)
+                if 2 <= k < 2 + bz:
+                    spill = x_all[k + 1, :, by:ey]
+                    total = total + moved(spill, 0 if which == 0 else LANES - 2, 2, slot + 5)
+            tiles.append(total)
+        edges.append(tiles)
+    for group in range(plan.y_groups):
+        here = slice(group * ex, (group + 1) * ex)
+        pay_a[here, :] = jnp.where(up_a, edges[0][group], edges[1][group])
+        pay_b[here, :] = jnp.where(up_b, edges[0][group], edges[1][group])
+
+    nz1, nx1, _ = plan.level1
+    rows, half = plan.rows, by // 2
+    for k in range(nz1):
+        b1[k] = jnp.zeros((nx1, LANES), F32)
+    row = iota((8, LANES), 0)
+    for j in range(plan.peers[0]):
+        for i in range(plan.peers[1]):
+            flip = iz ^ j
+            chip = (flip >> 1) + 2 * (ix ^ i)
+            other = ((flip ^ (flip >> 1)) & 1) == 1
+            at = pl.multiple_of(plan.slab + chip * plan.coarse, 8)
+
+            def rows_at(offset, count):
+                here = pl.ds(pl.multiple_of(at + offset, 8), count)
+                return jnp.where(other, theirs[here, :], ours[here, :])
+
+            own_lat = rows_at(plan.lat_at, 8)
+            spill_lat = rows_at(plan.lat_at + 8, 8)
+            for zp in range(plan.pairs):
+                own = rows_at(zp * rows, rows)
+                if zp % 2 == 0:
+                    spill_two = rows_at(plan.pairs * rows + zp * 4, 8)
+                spill = spill_two if zp % 2 == 0 else pltpu.roll(spill_two, 4, 0)
+                for part in range(2):
+                    zc = 2 * zp + part
+                    k = j * (bz // 2) + zc - 2
+                    if not 0 <= k < nz1:
+                        continue
+
+                    def wide(main, lat):
+                        return (
+                            moved(main, part * half, half, 0)
+                            + moved(lat, 4 * zc, 2, half) + moved(lat, 4 * zc + 2, 2, LANES - 2)
+                        )
+
+                    b1[k, i * rows:(i + 1) * rows, :] += wide(own, own_lat)
+                    v = wide(spill, spill_lat)
+                    if i + 1 < plan.peers[1]:
+                        at_row = (i + 1) * rows
+                        b1[k, at_row:at_row + 8, :] += only(row < 2, v)
+                    if i > 0:
+                        at_row = i * rows - 8
+                        b1[k, at_row:at_row + 8, :] += only(row >= 6, pltpu.roll(v, 4, 0))
+
+    lateral1 = level_lateral((nx1, LANES))
+    keep = wrapped_mask((nx1, LANES), {1: half}, (None, y_low), (None, y_high))
+    for k in range(nz1):
+        d1[k] = b1[k] * first_scale
+    for k in range(nz1):
+        r = b1[k] - apply_at(d1, k, lateral1)
+        r1_ref[k] = r
+        d2[k] = keep * (carry_coef * d1[k] + fresh_coef * r)
+    for k in range(nz1):
+        r1_ref[k] = keep * (r1_ref[k] - apply_at(d2, k, lateral1))
+        x1_ref[k] = d1[k] + d2[k]
+
+    nz2, nx2, _ = plan.level2
+    for zc in range(nz2):
+        pairs[zc * nx1:(zc + 1) * nx1, :] = r1_ref[2 * zc] + r1_ref[2 * zc + 1]
+        part, at = divmod(zc, nz2 // 2)
+        lines[at * nx2:(at + 1) * nx2, part * LANES:(part + 1) * LANES] = (
+            pairs[pl.ds(zc * nx1, nx2, 2), :] + pairs[pl.ds(zc * nx1 + 1, nx2, 2), :]
+        )
+    fine = iota((2 * LANES, LANES), 0)
+    part, fine = fine // LANES, signed(fine % LANES, half, LANES)
+    coarse = iota((2 * LANES, LANES), 1)
+    table = as_table(
+        (coarse // (LANES // 2) == part)
+        & (signed(coarse % (LANES // 2), half // 2, LANES // 2) == (fine >> 1)), 0.5
+    )
+    share = right_dot(lines[...], table)
+    pay_c[...] = share
+    pay_a[plan.edge:plan.edge + plan.share, :] = share
+    pay_b[plan.edge:plan.edge + plan.share, :] = share
+
+    per_tile = LANES // 16
+    for group in range(nz1 // per_tile):
+        tiles = []
+        for which in range(2):
+            total = jnp.zeros((nx1, LANES), F32)
+            for j in range(per_tile):
+                k = group * per_tile + j
+                first = half - 3 if which == 0 else LANES - 4
+                total = total + moved(r1_ref[k], first, 7, 16 * j)
+                first = half - 2 if which == 0 else LANES - 3
+                total = total + moved(x1_ref[k], first, 5, 16 * j + 7)
+            tiles.append(total)
+        here = slice(plan.fine_rows + group * nx1, plan.fine_rows + (group + 1) * nx1)
+        pay_a[here, :] = jnp.where(up_a, tiles[0], tiles[1])
+        pay_b[here, :] = jnp.where(up_b, tiles[0], tiles[1])
+
+
+def level_lateral(shape):
+    row = iota(shape, 0)
+    not_first = jnp.where(row > 0, 1.0, 0.0).astype(F32)
+    not_last = jnp.where(row < shape[0] - 1, 1.0, 0.0).astype(F32)
+
+    def beside(v):
+        return (
+            not_first * pltpu.roll(v, 1, 0) + not_last * pltpu.roll(v, shape[0] - 1, 0)
+            + pltpu.roll(v, 1, 1) + pltpu.roll(v, LANES - 1, 1)
+        )
+
+    return beside
+
+
+def small_cycle(level, source):
+    step = 1 << (level - 2)
+    row, lane = iota((8, LANES), 0), iota((8, LANES), 1)
+    count = len(source)
+    shifts = []
+    if step < 8:
+        shifts += [(step, 0, row >= step), (8 - step, 0, row < 8 - step)]
+    shifts += [(step, 1, lane >= step), (LANES - step, 1, lane < LANES - step)]
+
+    def op(v):
+        out = []
+        for k in range(count):
+            beside = None
+            for shift, dim, keep in shifts:
+                part = only(keep, pltpu.roll(v[k], shift, dim))
+                beside = part if beside is None else beside + part
+            if k > 0:
+                beside = beside + v[k - 1]
+            if k < count - 1:
+                beside = beside + v[k + 1]
+            out.append(6.0 * v[k] - beside)
+        return out
+
+    d = [first_scale * v for v in source]
+    r = [b - t for b, t in zip(source, op(d))]
+    d2 = [carry_coef * v + fresh_coef * t for v, t in zip(d, r)]
+    x = [v + t for v, t in zip(d, d2)]
+    r = [v - t for v, t in zip(r, op(d2))]
+    coarsest = None
+    if level < LEVELS - 1:
+        keep = only((row % (2 * step) == 0) & (lane % (2 * step) == 0), 0.5)
+        coarse = []
+        for k in range(0, count, 2):
+            v = r[k] + r[k + 1]
+            v = v + pltpu.roll(v, 8 - step, 0)
+            coarse.append(keep * (v + pltpu.roll(v, LANES - step, 1)))
+        coarse, coarsest = small_cycle(level + 1, coarse)
+        e = []
+        for v in coarse:
+            v = v + pltpu.roll(v, step, 0)
+            e += [v + pltpu.roll(v, step, 1)] * 2
+        x = [v + t for v, t in zip(x, e)]
+        r = [v - t for v, t in zip(r, op(e))]
+    d = [first_scale * v for v in r]
+    r = [v - t for v, t in zip(r, op(d))]
+    x = [v + (t + (carry_coef * t + fresh_coef * u)) for v, t, u in zip(x, d, r)]
+    return x, (x if level == LEVELS - 1 else coarsest)
+
+
+def last_kernel(plan, r_in, x_in, r1_in, x1_in, share, from_a, from_b, from_c, p_out, res_out, last_ref, *scratch):
+    shares, p_ref, res_ref, r, q1, e1, e0, d0, d1, r1, lines, wide, sem = scratch
+    bz, bx, by = plan.block
+    ez, ex, ey = plan.ext
+    nz1, nx1, _ = plan.level1
+    nz2, nx2, ny2 = plan.level2
+    layers, half = plan.layers, by // 2
+    iz, z_low, z_high = place("gz", plan.peers[0])
+    ix, x_low, x_high = place("gx", plan.peers[1])
+    iy, y_low, y_high = place("gy", plan.peers[2])
+
+    shares[0] = share[...]
+    shares[1] = from_a[plan.edge:plan.edge + plan.share, :]
+    shares[3] = from_b[plan.edge:plan.edge + plan.share, :]
+    shares[2] = from_c[...]
+    lower = upper = None
+    own2 = half // 2
+    for j in range(plan.peers[2]):
+        v = shares[iy ^ j]
+        at = own2 * j
+        mid = LANES // 2
+        low = moved(v, 0, own2 + 2, at) + moved(v, mid - 2, 2, at - 2)
+        high = moved(v, mid, own2 + 2, at) + moved(v, LANES - 2, 2, at - 2)
+        lower = low if lower is None else lower + low
+        upper = high if upper is None else upper + high
+    source = [lower[8 * k:8 * k + 8] for k in range(nz2 // 2)]
+    source += [upper[8 * k:8 * k + 8] for k in range(nz2 // 2)]
+    e2, coarsest = small_cycle(2, source)
+    for k in range(nz2):
+        lines[k * nx2:(k + 1) * nx2, :] = e2[k]
+    thin = as_table(iota((LANES, LANES), 0) == 8 * iota((LANES, LANES), 1))
+    for k in range(last_ref.shape[0]):
+        last_ref[k] = right_dot(coarsest[k], thin)[0:1, 0:last_ref.shape[2]]
+
+    up_a, _ = side(iy, 1)
+    _, near_b = side(iy, 3)
+    a_low = jnp.logical_not(up_a)
+
+    def sent(rows):
+        a, b = from_a[rows[0]:rows[1], :], from_b[rows[0]:rows[1], :]
+        b = only(near_b, b)
+        return jnp.where(up_a, a, b), jnp.where(up_a, b, a)
+
+    fine = signed(iota((LANES, LANES), 1), half, LANES)
+    coarse = iota((LANES, LANES), 0) - iy * own2
+    e2 = right_dot(lines[...], as_table((fine >> 1) == coarse))
+    for zc in range(nz2):
+        v = e2[zc * nx2:(zc + 1) * nx2]
+        for part in range(2):
+            q1.at[2 * zc + part][pl.ds(0, nx2, 2), :] = v
+            q1.at[2 * zc + part][pl.ds(1, nx2, 2), :] = v
+    per_tile = LANES // 16
+    lateral1 = level_lateral((nx1, LANES))
+    keep = wrapped_mask((nx1, LANES), {1: half}, (None, y_low), (None, y_high))
+    for group in range(nz1 // per_tile):
+        at = plan.fine_rows + group * nx1
+        high, low = sent((at, at + nx1))
+        for j in range(per_tile):
+            k = group * per_tile + j
+            s = 16 * j
+            r1[k] = (
+                r1_in[k] + moved(high, s, 7, half - 4) + moved(low, s, 7, LANES - 3)
+                - apply_at(q1, k, lateral1)
+            )
+            e1[k + 2, 8:8 + nx1, :] = (
+                x1_in[k] + q1[k]
+                + moved(high, s + 7, 5, half - 3) + moved(low, s + 7, 5, LANES - 2)
+            )
+    for k in range(nz1):
+        d1[k] = keep * (r1[k] * first_scale)
+    nothing = jnp.zeros((8, LANES), F32)
+    for k in range(nz1 + 4):
+        e1[k, 0:8, :] = nothing
+        e1[k, 8 + nx1:16 + nx1, :] = nothing
+        if not 2 <= k < nz1 + 2:
+            e1[k, 8:8 + nx1, :] = jnp.zeros((nx1, LANES), F32)
+    for k in range(nz1):
+        v = r1[k] - apply_at(d1, k, lateral1)
+        e1[k + 2, 8:8 + nx1, :] += d1[k] + keep * (carry_coef * d1[k] + fresh_coef * v)
+
+    coarse = signed(iota((LANES, ey), 0), half, LANES)
+    fine = signed(iota((LANES, ey), 1), by, ey)
+    double = as_table((fine >> 1) == coarse)
+    half_z, half_x = bz // 2, bx // 2
+    for zc in range(half_z + 4):
+        start = pl.multiple_of(ix * half_x, 8)
+        v = e1[iz * half_z + zc, pl.ds(start, half_x + 16), :]
+        own, low, high = v[8:8 + half_x], v[0:8], v[8 + half_x:16 + half_x]
+        at = zc * ex
+        wide[pl.ds(at, half_x, 2), :] = own
+        wide[pl.ds(at + 1, half_x, 2), :] = own
+        for j in range(2):
+            for twin in range(2):
+                row = at + bx + 2 * j + twin
+                wide[row:row + 1, :] = high[j:j + 1]
+                row = at + ex - 4 + 2 * j + twin
+                wide[row:row + 1, :] = low[6 + j:7 + j]
+    for zc in range(half_z + 4):
+        v = right_dot(wide[zc * ex:(zc + 1) * ex, :], double)
+        for k in (2 * zc - 1, 2 * zc):
+            if 0 <= k < ez:
+                e0[k] = v
+    flat = wrapped_mask((ex, ey), {0: bx, 1: by}, (x_low, y_low), (x_high, y_high))
+    below = jnp.where(z_low, 1.0, 0.0).astype(F32)
+    above = jnp.where(z_high, 1.0, 0.0).astype(F32)
+
+    def masked(k, v):
+        v = v * flat
+        if k < 3:
+            v = v * below
+        if k >= 3 + bz:
+            v = v * above
+        return v
+
+    for group in range(plan.y_groups):
+        high, low = sent((group * ex, (group + 1) * ex))
+        for k in range(group * SLOTS, min(layers, (group + 1) * SLOTS)):
+            s = 8 * (k - group * SLOTS)
+            v = r_in[k] - apply_at(e0, k + 1)
+            r[k, :, 0:by] = v[:, 0:by] + moved(high, s, 3, LANES - 3) + moved(low, s + 2, 3, 0)
+            r[k, :, by:ey] = v[:, by:ey] + moved(high, s + 3, 2, 0) + moved(low, s, 2, LANES - 2)
+            d0[k] = masked(k + 1, r[k] * first_scale)
+            if 2 <= k < 2 + bz:
+                p_ref[k - 2] = (
+                    x_in[k - 2] + e0[k + 1, 0:bx, 0:by]
+                    + (moved(high, s + 5, 2, LANES - 2) + moved(low, s + 5, 2, 0))[0:bx]
+                )
+    for k in range(1, layers - 1):
+        v = r[k] - apply_at(d0, k)
+        r[k] = v
+        v = masked(k + 1, carry_coef * d0[k] + fresh_coef * v)
+        e0[k] = v
+        if 2 <= k < 2 + bz:
+            p_ref[k - 2] += d0[k, 0:bx, 0:by] + v[0:bx, 0:by]
+    copy = pltpu.make_async_copy(p_ref, p_out, sem.at[0])
+    copy.start()
+    copies = [copy]
+    parts = 2
+    for part in range(parts):
+        here = range(part * bz // parts, (part + 1) * bz // parts)
+        for j in here:
+            v = r[j + 2] - apply_at(e0, j + 2)
+            res_ref[j] = v[0:bx, 0:by]
+        here = pl.ds(here[0], bz // parts)
+        copy = pltpu.make_async_copy(res_ref.at[here], res_out.at[here], sem.at[1 + part])
+        copy.start()
+        copies.append(copy)
+    for copy in copies:
+        copy.wait()
+
+
+def whole(shape):
+    return jax.ShapeDtypeStruct(shape, F32)
+
+
+VMEM = pl.BlockSpec(memory_space=pltpu.VMEM)
+ANY = pl.BlockSpec(memory_space=pl.ANY)
+VMEM_BYTES = 24 << 20
+
+
+def run(kernel, plan, outs, scratch, *operands, in_specs=None, out_specs=None, semaphores=0):
+    scratch = [pltpu.VMEM(s, F32) for s in scratch]
+    if semaphores:
+        scratch.append(pltpu.SemaphoreType.DMA((semaphores,)))
+    return pl.pallas_call(
+        functools.partial(kernel, plan),
+        out_shape=[whole(s) for s in outs],
+        in_specs=in_specs or [VMEM] * len(operands),
+        out_specs=out_specs or [VMEM] * len(outs),
+        scratch_shapes=scratch,
+        compiler_params=pltpu.CompilerParams(vmem_limit_bytes=VMEM_BYTES),
+    )(*operands)
+
+
+def swap(values, **flips):
+    axes = ("gx", "gy", "gz")
+    counts = [lax.axis_size(a) for a in axes]
+    pairs = []
+    for i in range(counts[0] * counts[1] * counts[2]):
+        at = [i // (counts[1] * counts[2]), i // counts[2] % counts[1], i % counts[2]]
+        to = [n ^ flips.get(a, 0) for n, a in zip(at, axes)]
+        pairs.append((i, (to[0] * counts[1] + to[1]) * counts[2] + to[2]))
+    return lax.ppermute(values, axes, pairs)
+
+
+def body_fast(divergence, pressure_prev):
+    plan = Plan(divergence.shape, tuple(lax.axis_size(a) for a in ("gz", "gx", "gy")))
+    bz, bx, by = plan.block
+    ext, lines = plan.ext, plan.lat_at
+    flat = (plan.ex, plan.ey)
+    level1 = plan.level1
+    r, x, pay_z, pay_x, pay_d = run(
+        first_kernel, plan,
+        [ext, ext, (plan.slab + plan.coarse, LANES), (plan.x_rows + plan.coarse, LANES),
+         (plan.corner + plan.coarse, LANES)],
+        [plan.block, plan.block, ext, ext, ext, ext, (2, 2 * plan.pairs * plan.ex, LANES),
+         (2, plan.lat_at, plan.ey)],
+        divergence, pressure_prev, in_specs=[ANY, ANY], semaphores=2,
+    )
+    from_z, from_x = swap(pay_z, gz=3), swap(pay_x, gx=1)
+    from_d = swap(pay_d, gz=3, gx=1)
+    r, x, ours = run(
+        chip_kernel, plan, [ext, ext, (plan.slab + 4 * plan.coarse, LANES)], [],
+        r, x, pay_z, from_z, from_x, from_d,
+    )
+    theirs = swap(ours, gz=1)
+    nz2, nx2, _ = plan.level2
+    edge = plan.edge + plan.share
+    r, x, r1, x1, pay_a, pay_b, share = run(
+        plane_kernel, plan,
+        [(plan.layers,) + flat, plan.block, level1, level1, (edge, LANES), (edge, LANES),
+         (plan.share, LANES)],
+        [ext, ext, level1, level1, level1, (nz2 * level1[1], LANES), (plan.share, 2 * LANES)],
+        r, x, ours, theirs,
+    )
+    from_a, from_b, from_c = swap(pay_a, gy=1), swap(pay_b, gy=3), swap(share, gy=2)
+    return run(
+        last_kernel, plan,
+        [plan.block, plan.block, tuple(n >> 3 for n in plan.level2)],
+        [(4, plan.share, LANES), plan.block, plan.block, (plan.layers,) + flat, level1,
+         (level1[0] + 4, level1[1] + 16, LANES), ext, (plan.layers,) + flat, level1, level1,
+         (nz2 * nx2, LANES), (2 * plan.pairs * plan.ex, LANES)],
+        r, x, r1, x1, share, from_a, from_b, from_c,
+        out_specs=[ANY, ANY, VMEM], semaphores=3,
+    )
+
+
+def fits_fast(shape, peers):
+    bz, bx, by = shape
+    nz, nx, ny = peers
+    return (
+        nz == 4 and nx == 2 and ny == 4 and bz == 16 and by == LANES
+        and nx * bx == 4 * 8 and ny * by == 4 * LANES
+    )
+
+
+def body(divergence, pressure_prev):
+    peers = tuple(lax.axis_size(a) for a in ("gz", "gx", "gy"))
+    if fits_fast(divergence.shape, peers):
+        return tuple(body_fast(divergence, pressure_prev))
+    return body_levels(divergence, pressure_prev)
 
 
 def solution(mesh):

time: 388 us -> 33.1 us (0.09)
  the two profiles are of different devices: /device:TPU:30 before, /device:TPU:0 now
where the time goes in v3:
time: 33.1 us; the launch traced here: 32.9 us
  waiting for transfers between devices  12.7 us (38%)
  starting transfers between devices  9.67 us (29%)
  Pallas kernels  8.07 us (24%)
  local copies, waits for them, and re-layouts  1.8 us (5%)
  between operations  0.67 us (2%)
    ppermute x7, waiting for transfers between devices, swap(): return lax.ppermute(values, axes, pairs)  12.7 us
    ppermute x7, starting transfers between devices, swap(): return lax.ppermute(values, axes, pairs)  9.67 us
    pallas_call x4, Pallas kernels, run(): pl.pallas_call(functools.partial(kernel, plan), out_shape=[whole(s) for s...  8.07 us
    unnamed x4, local copies, waits for them, and re-layouts  1.8 us
  transfers between devices with their start and end apart: 7, of which 3 were waited for; matrix products, arithmetic and copies ran while one was open for 0% of the time, Pallas kernels for 0%

profile of v3, /device:TPU:0, one launch (start us, length us, event | category | flops | bytes accessed | tf_op | source)
XLA Modules:
  0.0 32.9 jit_solution(2396287177260529730)
XLA Ops:
  0.6 0.0 copy-start
  0.6 0.9 %copy-done = f32[16,16,128]{2,1,0:T(8,128)S(1)} copy-done((f32[16,16,128]{2,1,0:T(8,128)S(1)}, f32[16,16,128]{2,1,0:T(8,128)}, u32[]{:S(2)}) %copy-start) | copy-done | bytes 131096
  1.5 0.0 copy-start.1
  1.5 0.9 %copy-done.1 = f32[16,16,128]{2,1,0:T(8,128)S(1)} copy-done((f32[16,16,128]{2,1,0:T(8,128)S(1)}, f32[16,16,128]{2,1,0:T(8,128)}, u32[]{:S(2)}) %copy-start.1) | copy-done | bytes 131096
  2.4 1.7 %shard_map.49 = (f32[22,24,256]{2,1,0:T(8,128)S(1)}, f32[22,24,256]{2,1,0:T(8,128)S(1)}, f32[280,128]{1,0:T(8,128)S(1)}, f32[280,128]{1,0:T(8,128)S(1)}, f32[136,128]{1,0:T(8,128)S(1)}) custom-call(f32[16,16,128]{2,1,0:T(8,128)S(1)} %copy-done, f32[16,16,128]{2,1,0:T(8,128)S(1)} %copy-done.1), custom_call_target="tpu_custom_call" | custom-call | tf_op jit(solution)/shard_map/pallas_call | solution.py:813
  4.1 3.0 %collective-permute-start.1 = (f32[280,128]{1,0:T(8,128)S(1)}, f32[280,128]{1,0:T(8,128)S(1)}, u32[]{:S(2)}, u32[]{:S(2)}) collective-permute-start(f32[280,128]{1,0:T(8,128)S(1)} %get-tuple-element.21), channel_id=1, source_target_pairs={{0,16},{1,17},{2,18},{3,19},{4,20},{5,21},{6,22},{7,23},{8,24},{9,... | collective-permute-start | bytes 430088 | tf_op jit(solution)/shard_map/ppermute | solution.py:831
  7.2 0.6 %collective-permute-start = (f32[280,128]{1,0:T(8,128)S(1)}, f32[280,128]{1,0:T(8,128)S(1)}, u32[]{:S(2)}, u32[]{:S(2)}) collective-permute-start(f32[280,128]{1,0:T(8,128)S(1)} %get-tuple-element.20.ours), channel_id=1, source_target_pairs={{0,3},{1,2},{2,1},{3,0},{4,7},{5,6},{6,5},{7,4},{8,11},{9,10},{10,... | collective-permute-start | bytes 430088 | tf_op jit(solution)/shard_map/ppermute | solution.py:831
  7.8 0.6 %collective-permute-start.2 = (f32[136,128]{1,0:T(8,128)S(1)}, f32[136,128]{1,0:T(8,128)S(1)}, u32[]{:S(2)}, u32[]{:S(2)}) collective-permute-start(f32[136,128]{1,0:T(8,128)S(1)} %get-tuple-element.22), channel_id=1, source_target_pairs={{0,19},{1,18},{2,17},{3,16},{4,23},{5,22},{6,21},{7,20},{8,27},{9,... | collective-permute-start | bytes 208904 | tf_op jit(solution)/shard_map/ppermute | solution.py:831
  8.4 5.4 %collective-permute-done.2.from_d = f32[136,128]{1,0:T(8,128)S(1)} collective-permute-done((f32[136,128]{1,0:T(8,128)S(1)}, f32[136,128]{1,0:T(8,128)S(1)}, u32[]{:S(2)}, u32[]{:S(2)}) %collective-permute-start.2) | collective-permute-done | bytes 69664 | tf_op jit(solution)/shard_map/ppermute | solution.py:831
  13.9 0.0 collective-permute-done.1.from_x
  13.9 0.0 collective-permute-done.from_z
  13.9 0.3 shard_map.50
  14.1 0.4 %collective-permute-start.3 = (f32[544,128]{1,0:T(8,128)S(1)}, f32[544,128]{1,0:T(8,128)S(1)}, u32[]{:S(2)}, u32[]{:S(2)}) collective-permute-start(f32[544,128]{1,0:T(8,128)S(1)} %get-tuple-element.25.ours), channel_id=1, source_target_pairs={{0,1},{1,0},{2,3},{3,2},{4,5},{5,4},{6,7},{7,6},{8,9},{9,8},{10,11... | collective-permute-start | bytes 835592 | tf_op jit(solution)/shard_map/ppermute | solution.py:831
  14.5 1.3 %collective-permute-done.3.theirs = f32[544,128]{1,0:T(8,128)S(1)} collective-permute-done((f32[544,128]{1,0:T(8,128)S(1)}, f32[544,128]{1,0:T(8,128)S(1)}, u32[]{:S(2)}, u32[]{:S(2)}) %collective-permute-start.3) | collective-permute-done | bytes 278560 | tf_op jit(solution)/shard_map/ppermute | solution.py:831
  15.8 1.6 %shard_map.51 = (f32[20,24,256]{2,1,0:T(8,128)S(1)}, f32[16,16,128]{2,1,0:T(8,128)S(1)}, f32[32,16,128]{2,1,0:T(8,128)S(1)}, f32[32,16,128]{2,1,0:T(8,128)S(1)},...) custom-call(f32[22,24,256]{2,1,0:T(8,128)S(1)} %get-tuple-element.23.r_in, ...), custom_call_target="tpu_custom_call" | custom-call | tf_op jit(solution)/shard_map/pallas_call | solution.py:813
  17.3 2.4 %collective-permute-start.4 = (f32[176,128]{1,0:T(8,128)S(1)}, f32[176,128]{1,0:T(8,128)S(1)}, u32[]{:S(2)}, u32[]{:S(2)}) collective-permute-start(f32[176,128]{1,0:T(8,128)S(1)} %get-tuple-element.31), channel_id=1, source_target_pairs={{0,4},{1,5},{2,6},{3,7},{4,0},{5,1},{6,2},{7,3},{8,12},{9,13},{10,... | collective-permute-start | bytes 270344 | tf_op jit(solution)/shard_map/ppermute | solution.py:831
  19.7 2.5 %collective-permute-start.5 = (f32[176,128]{1,0:T(8,128)S(1)}, f32[176,128]{1,0:T(8,128)S(1)}, u32[]{:S(2)}, u32[]{:S(2)}) collective-permute-start(f32[176,128]{1,0:T(8,128)S(1)} %get-tuple-element.32), channel_id=1, source_target_pairs={{0,12},{1,13},{2,14},{3,15},{4,8},{5,9},{6,10},{7,11},{8,4},{9,5},... | collective-permute-start | bytes 270344 | tf_op jit(solution)/shard_map/ppermute | solution.py:831
  22.2 0.1 collective-permute-start.6
  22.3 6.0 %collective-permute-done.6.from_c = f32[64,128]{1,0:T(8,128)S(1)} collective-permute-done((f32[64,128]{1,0:T(8,128)S(1)}, f32[64,128]{1,0:T(8,128)S(1)}, u32[]{:S(2)}, u32[]{:S(2)}) %collective-permute-start.6) | collective-permute-done | bytes 32800 | tf_op jit(solution)/shard_map/ppermute | solution.py:831
  28.4 0.0 collective-permute-done.4.from_a
  28.4 0.0 collective-permute-done.5.from_b
  28.4 4.5 %shard_map.52 = (f32[16,16,128]{2,1,0:T(8,128)}, f32[16,16,128]{2,1,0:T(8,128)}, f32[2,1,16]{2,1,0:T(1,128)}) custom-call(f32[20,24,256]{2,1,0:T(8,128)S(1)} %get-tuple-element.26.r_in, f32[16,16,128]{2,1,0:T(8,128)S(1)} %get-tuple-element.27.x_in, f32[32,16,128]{2,1,0:T(8,128)S(1)} %get-tuple-element.28.r1_in, f32[32,16,128]{2,1,0:T(8,128)S(1)} %get-tuple-element.29.x1_in, ...), custom_call_target="tpu_custom_call" | custom-call | tf_op jit(solution)/shard_map/pallas_call | solution.py:813
Async XLA Ops:
  0.6 0.9 %copy-start = (f32[16,16,128]{2,1,0:T(8,128)S(1)}, f32[16,16,128]{2,1,0:T(8,128)}, u32[]{:S(2)}) copy-start(f32[16,16,128]{2,1,0:T(8,128)} %b_in.1) | copy-start | bytes 393220
  1.5 0.9 %copy-start.1 = (f32[16,16,128]{2,1,0:T(8,128)S(1)}, f32[16,16,128]{2,1,0:T(8,128)}, u32[]{:S(2)}) copy-start(f32[16,16,128]{2,1,0:T(8,128)} %p_in.1) | copy-start | bytes 393220
  4.1 9.7 %collective-permute-start.1 = (f32[280,128]{1,0:T(8,128)S(1)}, f32[280,128]{1,0:T(8,128)S(1)}, u32[]{:S(2)}, u32[]{:S(2)}) collective-permute-start(f32[280,128]{1,0:T(8,128)S(1)} %get-tuple-element.21), channel_id=1, source_target_pairs={{0,16},{1,17},{2,18},{3,19},{4,20},{5,21},{6,22},{7,23},{8,24},{9,... | collective-permute-start | bytes 430088 | tf_op jit(solution)/shard_map/ppermute | solution.py:831
  7.2 6.7 %collective-permute-start = (f32[280,128]{1,0:T(8,128)S(1)}, f32[280,128]{1,0:T(8,128)S(1)}, u32[]{:S(2)}, u32[]{:S(2)}) collective-permute-start(f32[280,128]{1,0:T(8,128)S(1)} %get-tuple-element.20.ours), channel_id=1, source_target_pairs={{0,3},{1,2},{2,1},{3,0},{4,7},{5,6},{6,5},{7,4},{8,11},{9,10},{10,... | collective-permute-start | bytes 430088 | tf_op jit(solution)/shard_map/ppermute | solution.py:831
  7.8 6.0 %collective-permute-start.2 = (f32[136,128]{1,0:T(8,128)S(1)}, f32[136,128]{1,0:T(8,128)S(1)}, u32[]{:S(2)}, u32[]{:S(2)}) collective-permute-start(f32[136,128]{1,0:T(8,128)S(1)} %get-tuple-element.22), channel_id=1, source_target_pairs={{0,19},{1,18},{2,17},{3,16},{4,23},{5,22},{6,21},{7,20},{8,27},{9,... | collective-permute-start | bytes 208904 | tf_op jit(solution)/shard_map/ppermute | solution.py:831
  14.1 1.6 %collective-permute-start.3 = (f32[544,128]{1,0:T(8,128)S(1)}, f32[544,128]{1,0:T(8,128)S(1)}, u32[]{:S(2)}, u32[]{:S(2)}) collective-permute-start(f32[544,128]{1,0:T(8,128)S(1)} %get-tuple-element.25.ours), channel_id=1, source_target_pairs={{0,1},{1,0},{2,3},{3,2},{4,5},{5,4},{6,7},{7,6},{8,9},{9,8},{10,11... | collective-permute-start | bytes 835592 | tf_op jit(solution)/shard_map/ppermute | solution.py:831
  17.3 11.1 %collective-permute-start.4 = (f32[176,128]{1,0:T(8,128)S(1)}, f32[176,128]{1,0:T(8,128)S(1)}, u32[]{:S(2)}, u32[]{:S(2)}) collective-permute-start(f32[176,128]{1,0:T(8,128)S(1)} %get-tuple-element.31), channel_id=1, source_target_pairs={{0,4},{1,5},{2,6},{3,7},{4,0},{5,1},{6,2},{7,3},{8,12},{9,13},{10,... | collective-permute-start | bytes 270344 | tf_op jit(solution)/shard_map/ppermute | solution.py:831
  19.7 8.6 %collective-permute-start.5 = (f32[176,128]{1,0:T(8,128)S(1)}, f32[176,128]{1,0:T(8,128)S(1)}, u32[]{:S(2)}, u32[]{:S(2)}) collective-permute-start(f32[176,128]{1,0:T(8,128)S(1)} %get-tuple-element.32), channel_id=1, source_target_pairs={{0,12},{1,13},{2,14},{3,15},{4,8},{5,9},{6,10},{7,11},{8,4},{9,5},... | collective-permute-start | bytes 270344 | tf_op jit(solution)/shard_map/ppermute | solution.py:831
  22.2 6.2 %collective-permute-start.6 = (f32[64,128]{1,0:T(8,128)S(1)}, f32[64,128]{1,0:T(8,128)S(1)}, u32[]{:S(2)}, u32[]{:S(2)}) collective-permute-start(f32[64,128]{1,0:T(8,128)S(1)} %get-tuple-element.30.share), channel_id=1, source_target_pairs={{0,8},{1,9},{2,10},{3,11},{4,12},{5,13},{6,14},{7,15},{8,0},{9,1},... | collective-permute-start | bytes 98312 | tf_op jit(solution)/shard_map/ppermute | solution.py:831

commit v4 on v3

--- a/solution.py
+++ b/solution.py
@@ -268,6 +268,26 @@
         x_ref[k, bx - 8:bx] += only(up & (row >= 6), pltpu.roll(rows, 1, 0))
 
 
+def rows_emit(r_ref, x_ref, out, up):
+    ez = r_ref.shape[0]
+    for group in range(-(-ez // SLOTS)):
+        lat = jnp.zeros((8, LANES), F32)
+        for k in range(group * SLOTS, min(ez, (group + 1) * SLOTS)):
+            rows = rows_out(r_ref[k], x_ref[k], up)
+            out[8 * k:8 * k + 8, :] = rows[:, 0:LANES]
+            lat = lat + side_pack(rows[:, LANES:], k - group * SLOTS)
+        out[8 * (ez + group):8 * (ez + group) + 8, :] = lat
+
+
+def rows_add(r_ref, x_ref, slab, up):
+    ez = r_ref.shape[0]
+    for k in range(ez):
+        at = 8 * (ez + k // SLOTS)
+        lat = side_unpack(slab[at:at + 8, :], k % SLOTS)
+        rows = jnp.concatenate([slab[8 * k:8 * k + 8, :], lat], axis=1)
+        rows_in(r_ref, x_ref, k, rows, up)
+
+
 class Plan:
     def __init__(self, shape, peers):
         self.peers = peers
@@ -276,10 +296,8 @@
         self.rows, self.pairs = bx // 2, bz // 4 + 2
         self.lat_at = self.pairs * (self.rows + 4)
         self.coarse = self.lat_at + 16
-        self.slab = 8 * self.ex
         self.x_groups = -(-self.ez // SLOTS)
-        self.x_rows = (self.ez + self.x_groups) * 8
-        self.corner = 6 * 8
+        self.slab = max(8 * self.ex, (self.ez + self.x_groups) * 8)
         self.layers = bz + 4
         self.level1 = (peers[0] * bz // 2, peers[1] * bx // 2, LANES)
         self.level2 = (peers[0] * bz // 4, peers[1] * bx // 4, peers[2] * by // 4)
@@ -289,7 +307,7 @@
         self.share = self.level2[0] * self.level2[1] // 2
 
 
-def first_kernel(plan, b_in, p_in, r_ref, x_ref, pay_z, pay_x, pay_d, *scratch):
+def first_kernel(plan, b_in, p_in, r_ref, x_ref, pay, *scratch):
     b_own, p_own, b_ext, p_ext, d_one, d_two, pairs, lines, sem = scratch
     bz, bx, by = plan.block
     ez, ex, ey = plan.ext
@@ -374,7 +392,7 @@
     even, odd = right_dot(lines[0], table), right_dot(lines[1], table)
     lane = iota(even.shape, 1)
     at = plan.slab
-    pay_z[at:at + plan.lat_at, :] = jnp.where(lane < LANES // 2, even, shifted(odd, LANES // 2))
+    pay[at:at + plan.lat_at, :] = jnp.where(lane < LANES // 2, even, shifted(odd, LANES // 2))
     own_lat = spill_lat = None
     row = iota((8, LANES), 0)
     for zc in range(coarse_z):
@@ -391,65 +409,63 @@
         part = moved(tile, by // 2, 2, 4 * zc) + moved(tile, LANES - 2, 2, 4 * zc + 2)
         spill_lat = part if spill_lat is None else spill_lat + part
     at = plan.slab + plan.lat_at
-    pay_z[at:at + 8, :] = own_lat
-    pay_z[at + 8:at + 16, :] = spill_lat
-    block = pay_z[plan.slab:plan.slab + plan.coarse, :]
-    pay_x[plan.x_rows:plan.x_rows + plan.coarse, :] = block
-    pay_d[plan.corner:plan.corner + plan.coarse, :] = block
-
-    up_z, _ = side(iz, 3)
-    up_x, _ = side(ix, 1)
-    slab_emit(r_ref, x_ref, pay_z, 0, up_z)
-    for group in range(plan.x_groups):
-        lat = jnp.zeros((8, LANES), F32)
-        for k in range(group * SLOTS, min(ez, (group + 1) * SLOTS)):
-            out = rows_out(r_ref[k], x_ref[k], up_x)
-            pay_x[8 * k:8 * k + 8, :] = out[:, 0:LANES]
-            lat = lat + side_pack(out[:, LANES:], k - group * SLOTS)
-        pay_x[8 * (ez + group):8 * (ez + group) + 8, :] = lat
-    start = jnp.where(up_z, ez - 5, 0)
-    lat = jnp.zeros((8, LANES), F32)
-    for j in range(5):
-        out = rows_out(r_ref[start + j], x_ref[start + j] if j == 2 else None, up_x)
-        pay_d[8 * j:8 * j + 8, :] = out[:, 0:LANES]
-        lat = lat + side_pack(out[:, LANES:], j)
-    pay_d[40:48, :] = lat
-
-
-def chip_kernel(plan, r_in, x_in, ours, from_z, from_x, from_d, r_ref, x_ref, pay):
-    ez, ex, ey = plan.ext
+    pay[at:at + 8, :] = own_lat
+    pay[at + 8:at + 16, :] = spill_lat
+    inner = (iz == 1) | (iz == 2)
+
+    @pl.when(inner)
+    def _():
+        slab_emit(r_ref, x_ref, pay, 0, side(iz, 3)[0])
+
+    @pl.when(jnp.logical_not(inner))
+    def _():
+        rows_emit(r_ref, x_ref, pay, side(ix, 1)[0])
+
+
+def step_kernel(plan, r_in, x_in, ours, got, r_ref, x_ref, pay):
     iz, _, _ = place("gz", plan.peers[0])
     ix, _, _ = place("gx", plan.peers[1])
-    up_z, near = side(iz, 3)
+    up_z, inner = side(iz, 3)
     up_x, _ = side(ix, 1)
-    for k in range(ez):
+    for k in range(plan.ez):
         r_ref[k] = r_in[k]
         x_ref[k] = x_in[k]
-        lat = from_x[8 * (ez + k // SLOTS):8 * (ez + k // SLOTS) + 8, :]
-        rows = from_x[8 * k:8 * k + 8, :]
-        rows = jnp.concatenate([rows, side_unpack(lat, k % SLOTS)], axis=1)
-        rows_in(r_ref, x_ref, k, rows, up_x)
-
-    @pl.when(near)
+
+    @pl.when(inner)
     def _():
-        slab_add(r_ref, x_ref, from_z, 0, up_z)
-        start = jnp.where(up_z, ez - 6, 1)
-        lat = from_d[40:48, :]
-        for j in range(5):
-            rows = from_d[8 * j:8 * j + 8, :]
-            rows = jnp.concatenate([rows, side_unpack(lat, j)], axis=1)
-            rows_in(r_ref, x_ref if j == 2 else None, start + j, rows, up_x)
-
-    up, _ = side(iz, 1)
-    slab_emit(r_ref, x_ref, pay, 0, up)
-    for j, (ref, at) in enumerate(
-        ((ours, plan.slab), (from_z, plan.slab), (from_x, plan.x_rows), (from_d, plan.corner))
-    ):
+        slab_add(r_ref, x_ref, got, 0, up_z)
+        rows_emit(r_ref, x_ref, pay, up_x)
+
+    @pl.when(jnp.logical_not(inner))
+    def _():
+        rows_add(r_ref, x_ref, got, up_x)
+        pay[0:plan.slab, :] = jnp.zeros((plan.slab, LANES), F32)
+
+    for j, ref in enumerate((ours, got)):
         here = plan.slab + j * plan.coarse
-        pay[here:here + plan.coarse, :] = ref[at:at + plan.coarse, :]
-
-
-def plane_kernel(plan, r_in, x_in, ours, theirs, r_ref, x_ref, r1_ref, x1_ref, pay_a, pay_b, pay_c,
+        pay[here:here + plan.coarse, :] = ref[plan.slab:plan.slab + plan.coarse, :]
+
+
+def core_kernel(plan, r_in, x_in, ours, got, r_ref, x_ref, pay):
+    iz, _, _ = place("gz", plan.peers[0])
+    ix, _, _ = place("gx", plan.peers[1])
+    _, inner = side(iz, 3)
+    up_x, _ = side(ix, 1)
+    for k in range(plan.ez):
+        r_ref[k] = r_in[k]
+        x_ref[k] = x_in[k]
+
+    @pl.when(inner)
+    def _():
+        rows_add(r_ref, x_ref, got, up_x)
+
+    slab_emit(r_ref, x_ref, pay, 0, side(iz, 1)[0])
+    for j, ref in enumerate((ours, got)):
+        here = plan.slab + 2 * j * plan.coarse
+        pay[here:here + 2 * plan.coarse, :] = ref[plan.slab:plan.slab + 2 * plan.coarse, :]
+
+
+def plane_kernel(plan, r_in, x_in, ours, theirs, r_ref, x_ref, r1_ref, x1_ref, pay, later,
                  r_all, x_all, b1, d1, d2, pairs, lines):
     bz, bx, by = plan.block
     ez, ex, ey = plan.ext
@@ -467,8 +483,10 @@
     for k in range(bz):
         x_ref[k] = x_all[k + 3, 0:bx, 0:by]
 
-    up_a, _ = side(iy, 1)
-    up_b, _ = side(iy, 3)
+    even = (iz & 1) == 0
+    up_a, up_b = side(iy, 1)[0], side(iy, 3)[0]
+    up_now = (even & up_a) | (jnp.logical_not(even) & up_b)
+    up_later = (even & up_b) | (jnp.logical_not(even) & up_a)
     edges = []
     for which in range(2):
         tiles = []
@@ -488,8 +506,8 @@
         edges.append(tiles)
     for group in range(plan.y_groups):
         here = slice(group * ex, (group + 1) * ex)
-        pay_a[here, :] = jnp.where(up_a, edges[0][group], edges[1][group])
-        pay_b[here, :] = jnp.where(up_b, edges[0][group], edges[1][group])
+        pay[here, :] = jnp.where(up_now, edges[0][group], edges[1][group])
+        later[here, :] = jnp.where(up_later, edges[0][group], edges[1][group])
 
     nz1, nx1, _ = plan.level1
     rows, half = plan.rows, by // 2
@@ -499,8 +517,10 @@
     for j in range(plan.peers[0]):
         for i in range(plan.peers[1]):
             flip = iz ^ j
-            chip = (flip >> 1) + 2 * (ix ^ i)
             other = ((flip ^ (flip >> 1)) & 1) == 1
+            along_z, along_x = flip >> 1, ix ^ i
+            met_z = ((iz == 1) | (iz == 2)) ^ other
+            chip = jnp.where(met_z, along_z + 2 * along_x, along_x + 2 * along_z)
             at = pl.multiple_of(plan.slab + chip * plan.coarse, 8)
 
             def rows_at(offset, count):
@@ -562,9 +582,7 @@
         & (signed(coarse % (LANES // 2), half // 2, LANES // 2) == (fine >> 1)), 0.5
     )
     share = right_dot(lines[...], table)
-    pay_c[...] = share
-    pay_a[plan.edge:plan.edge + plan.share, :] = share
-    pay_b[plan.edge:plan.edge + plan.share, :] = share
+    pay[plan.edge:plan.edge + plan.share, :] = share
 
     per_tile = LANES // 16
     for group in range(nz1 // per_tile):
@@ -579,8 +597,8 @@
                 total = total + moved(x1_ref[k], first, 5, 16 * j + 7)
             tiles.append(total)
         here = slice(plan.fine_rows + group * nx1, plan.fine_rows + (group + 1) * nx1)
-        pay_a[here, :] = jnp.where(up_a, tiles[0], tiles[1])
-        pay_b[here, :] = jnp.where(up_b, tiles[0], tiles[1])
+        pay[here, :] = jnp.where(up_now, tiles[0], tiles[1])
+        later[here, :] = jnp.where(up_later, tiles[0], tiles[1])
 
 
 def level_lateral(shape):
@@ -646,7 +664,7 @@
     return x, (x if level == LEVELS - 1 else coarsest)
 
 
-def last_kernel(plan, r_in, x_in, r1_in, x1_in, share, from_a, from_b, from_c, p_out, res_out, last_ref, *scratch):
+def last_kernel(plan, r_in, x_in, r1_in, x1_in, ours, got, then, p_out, res_out, last_ref, *scratch):
     shares, p_ref, res_ref, r, q1, e1, e0, d0, d1, r1, lines, wide, sem = scratch
     bz, bx, by = plan.block
     ez, ex, ey = plan.ext
@@ -657,10 +675,13 @@
     ix, x_low, x_high = place("gx", plan.peers[1])
     iy, y_low, y_high = place("gy", plan.peers[2])
 
-    shares[0] = share[...]
-    shares[1] = from_a[plan.edge:plan.edge + plan.share, :]
-    shares[3] = from_b[plan.edge:plan.edge + plan.share, :]
-    shares[2] = from_c[...]
+    even = (iz & 1) == 0
+    first = jnp.where(even, 1, 3)
+    here = plan.edge + plan.share
+    shares[0] = ours[plan.edge:here, :]
+    shares[first] = got[plan.edge:here, :]
+    shares[4 - first] = then[plan.edge:here, :]
+    shares[2] = then[here:here + plan.share, :]
     lower = upper = None
     own2 = half // 2
     for j in range(plan.peers[2]):
@@ -682,11 +703,10 @@
 
     up_a, _ = side(iy, 1)
     _, near_b = side(iy, 3)
-    a_low = jnp.logical_not(up_a)
 
     def sent(rows):
-        a, b = from_a[rows[0]:rows[1], :], from_b[rows[0]:rows[1], :]
-        b = only(near_b, b)
+        a, b = got[rows[0]:rows[1], :], then[rows[0]:rows[1], :]
+        a, b = jnp.where(even, a, b), only(near_b, jnp.where(even, b, a))
         return jnp.where(up_a, a, b), jnp.where(up_a, b, a)
 
     fine = signed(iota((LANES, LANES), 1), half, LANES)
@@ -803,6 +823,7 @@
 
 VMEM = pl.BlockSpec(memory_space=pltpu.VMEM)
 ANY = pl.BlockSpec(memory_space=pl.ANY)
+HBM = pl.BlockSpec(memory_space=pltpu.HBM)
 VMEM_BYTES = 24 << 20
 
 
@@ -820,55 +841,49 @@
     )(*operands)
 
 
-def swap(values, **flips):
+def swap(values, partner):
     axes = ("gx", "gy", "gz")
     counts = [lax.axis_size(a) for a in axes]
     pairs = []
     for i in range(counts[0] * counts[1] * counts[2]):
-        at = [i // (counts[1] * counts[2]), i // counts[2] % counts[1], i % counts[2]]
-        to = [n ^ flips.get(a, 0) for n, a in zip(at, axes)]
-        pairs.append((i, (to[0] * counts[1] + to[1]) * counts[2] + to[2]))
+        x, y, z = partner(i // (counts[1] * counts[2]), i // counts[2] % counts[1], i % counts[2])
+        pairs.append((i, (x * counts[1] + y) * counts[2] + z))
     return lax.ppermute(values, axes, pairs)
 
 
 def body_fast(divergence, pressure_prev):
     plan = Plan(divergence.shape, tuple(lax.axis_size(a) for a in ("gz", "gx", "gy")))
-    bz, bx, by = plan.block
-    ext, lines = plan.ext, plan.lat_at
-    flat = (plan.ex, plan.ey)
-    level1 = plan.level1
-    r, x, pay_z, pay_x, pay_d = run(
-        first_kernel, plan,
-        [ext, ext, (plan.slab + plan.coarse, LANES), (plan.x_rows + plan.coarse, LANES),
-         (plan.corner + plan.coarse, LANES)],
+    ext, level1 = plan.ext, plan.level1
+    payload = [(plan.slab + n * plan.coarse, LANES) for n in (1, 2, 4)]
+    r, x, ours = run(
+        first_kernel, plan, [ext, ext, payload[0]],
         [plan.block, plan.block, ext, ext, ext, ext, (2, 2 * plan.pairs * plan.ex, LANES),
          (2, plan.lat_at, plan.ey)],
-        divergence, pressure_prev, in_specs=[ANY, ANY], semaphores=2,
+        divergence, pressure_prev, in_specs=[HBM, HBM], semaphores=2,
     )
-    from_z, from_x = swap(pay_z, gz=3), swap(pay_x, gx=1)
-    from_d = swap(pay_d, gz=3, gx=1)
-    r, x, ours = run(
-        chip_kernel, plan, [ext, ext, (plan.slab + 4 * plan.coarse, LANES)], [],
-        r, x, pay_z, from_z, from_x, from_d,
+    got = swap(ours, lambda x, y, z: (x, y, z ^ 3) if z in (1, 2) else (x ^ 1, y, z))
+    r, x, ours = run(step_kernel, plan, [ext, ext, payload[1]], [], r, x, ours, got)
+    got = swap(ours, lambda x, y, z: (x ^ 1, y, z) if z in (1, 2) else (x, y, z ^ 3))
+    r, x, ours = run(core_kernel, plan, [ext, ext, payload[2]], [], r, x, ours, got)
+    got = swap(ours, lambda x, y, z: (x, y, z ^ 1))
+    nz2, nx2, _ = plan.level2
+    layers = (plan.layers, plan.ex, plan.ey)
+    r, x, r1, x1, ours, later = run(
+        plane_kernel, plan,
+        [layers, plan.block, level1, level1, (plan.edge + plan.share, LANES), (plan.edge, LANES)],
+        [ext, ext, level1, level1, level1, (nz2 * level1[1], LANES), (plan.share, 2 * LANES)],
+        r, x, ours, got,
     )
-    theirs = swap(ours, gz=1)
-    nz2, nx2, _ = plan.level2
-    edge = plan.edge + plan.share
-    r, x, r1, x1, pay_a, pay_b, share = run(
-        plane_kernel, plan,
-        [(plan.layers,) + flat, plan.block, level1, level1, (edge, LANES), (edge, LANES),
-         (plan.share, LANES)],
-        [ext, ext, level1, level1, level1, (nz2 * level1[1], LANES), (plan.share, 2 * LANES)],
-        r, x, ours, theirs,
-    )
-    from_a, from_b, from_c = swap(pay_a, gy=1), swap(pay_b, gy=3), swap(share, gy=2)
+    got = swap(ours, lambda x, y, z: (x, y ^ (1, 3)[z & 1], z))
+    then = jnp.concatenate([later, ours[plan.edge:], got[plan.edge:]], axis=0)
+    then = swap(then, lambda x, y, z: (x, y ^ (3, 1)[z & 1], z))
     return run(
         last_kernel, plan,
         [plan.block, plan.block, tuple(n >> 3 for n in plan.level2)],
-        [(4, plan.share, LANES), plan.block, plan.block, (plan.layers,) + flat, level1,
-         (level1[0] + 4, level1[1] + 16, LANES), ext, (plan.layers,) + flat, level1, level1,
+        [(4, plan.share, LANES), plan.block, plan.block, layers, level1,
+         (level1[0] + 4, level1[1] + 16, LANES), ext, layers, level1, level1,
          (nz2 * nx2, LANES), (2 * plan.pairs * plan.ex, LANES)],
-        r, x, r1, x1, share, from_a, from_b, from_c,
+        r, x, r1, x1, ours, got, then,
         out_specs=[ANY, ANY, VMEM], semaphores=3,
     )
 

time: 33.1 us -> 36.5 us (1.10)
  waiting for transfers between devices: 12.7 us -> 15.6 us
    ppermute x7 -> x5, waiting for transfers between devices: 12.7 us -> 15.6 us  [swap(): return lax.ppermute(values, axes, pairs)]
    ppermute x7 -> x5, starting transfers between devices: 9.67 us -> 10 us  [swap(): return lax.ppermute(values, axes, pairs)]
    pallas_call x4 -> x5, Pallas kernels: 8.07 us -> 8.18 us  [run(): pl.pallas_call(functools.partial(kernel, plan), out_shape=[whole(s) for s...]
  transfers between devices with their start and end apart: 7 -> 5, of which waited for: 3 -> 5; matrix products, arithmetic and copies ran while one was open for 0% -> 0% of each run, Pallas kernels for 0% -> 0%
where the time goes in v4:
time: 36.5 us; the launch traced here: 36.3 us
  waiting for transfers between devices  15.6 us (43%)
  starting transfers between devices  10 us (27%)
  Pallas kernels  8.18 us (22%)
  local copies, waits for them, and re-layouts  1.81 us (5%)
  between operations  0.68 us (2%)
    ppermute x5, waiting for transfers between devices, swap(): return lax.ppermute(values, axes, pairs)  15.6 us
    ppermute x5, starting transfers between devices, swap(): return lax.ppermute(values, axes, pairs)  10 us
    pallas_call x5, Pallas kernels, run(): pl.pallas_call(functools.partial(kernel, plan), out_shape=[whole(s) for s...  8.18 us
    unnamed x4, local copies, waits for them, and re-layouts  1.8 us
  transfers between devices with their start and end apart: 5, of which 5 were waited for; matrix products, arithmetic and copies ran while one was open for 0% of the time, Pallas kernels for 0%

profile of v4, /device:TPU:0, one launch (start us, length us, event | category | flops | bytes accessed | tf_op | source)
XLA Modules:
  0.0 36.3 jit_solution(12995519742696209526)
XLA Ops:
  0.6 0.0 copy-start
  0.6 0.9 %copy-done = f32[16,16,128]{2,1,0:T(8,128)S(1)} copy-done((f32[16,16,128]{2,1,0:T(8,128)S(1)}, f32[16,16,128]{2,1,0:T(8,128)}, u32[]{:S(2)}) %copy-start) | copy-done | bytes 131096
  1.5 0.0 copy-start.1
  1.5 0.9 %copy-done.1 = f32[16,16,128]{2,1,0:T(8,128)S(1)} copy-done((f32[16,16,128]{2,1,0:T(8,128)S(1)}, f32[16,16,128]{2,1,0:T(8,128)}, u32[]{:S(2)}) %copy-start.1) | copy-done | bytes 131096
  2.4 1.7 %shard_map.49 = (f32[22,24,256]{2,1,0:T(8,128)S(1)}, f32[22,24,256]{2,1,0:T(8,128)S(1)}, f32[280,128]{1,0:T(8,128)S(1)}) custom-call(f32[16,16,128]{2,1,0:T(8,128)S(1)} %copy-done, f32[16,16,128]{2,1,0:T(8,128)S(1)} %copy-done.1), custom_call_target="tpu_custom_call" | custom-call | tf_op jit(solution)/shard_map/pallas_call | solution.py:834
  4.2 3.0 %collective-permute-start = (f32[280,128]{1,0:T(8,128)S(1)}, f32[280,128]{1,0:T(8,128)S(1)}, u32[]{:S(2)}, u32[]{:S(2)}) collective-permute-start(f32[280,128]{1,0:T(8,128)S(1)} %get-tuple-element.20.ours), channel_id=1, source_target_pairs={{0,16},{1,2},{2,1},{3,19},{4,20},{5,6},{6,5},{7,23},{8,24},{9,10},... | collective-permute-start | bytes 430088 | tf_op jit(solution)/shard_map/ppermute | solution.py:851
  7.2 3.1 %collective-permute-done.got = f32[280,128]{1,0:T(8,128)S(1)} collective-permute-done((f32[280,128]{1,0:T(8,128)S(1)}, f32[280,128]{1,0:T(8,128)S(1)}, u32[]{:S(2)}, u32[]{:S(2)}) %collective-permute-start) | collective-permute-done | bytes 143392 | tf_op jit(solution)/shard_map/ppermute | solution.py:851
  10.3 0.2 shard_map.50
  10.5 0.6 %collective-permute-start.1 = (f32[368,128]{1,0:T(8,128)S(1)}, f32[368,128]{1,0:T(8,128)S(1)}, u32[]{:S(2)}, u32[]{:S(2)}) collective-permute-start(f32[368,128]{1,0:T(8,128)S(1)} %get-tuple-element.23.ours), channel_id=1, source_target_pairs={{0,3},{1,17},{2,18},{3,0},{4,7},{5,21},{6,22},{7,4},{8,11},{9,25},... | collective-permute-start | bytes 565256 | tf_op jit(solution)/shard_map/ppermute | solution.py:851
  11.1 4.4 %collective-permute-done.1.got = f32[368,128]{1,0:T(8,128)S(1)} collective-permute-done((f32[368,128]{1,0:T(8,128)S(1)}, f32[368,128]{1,0:T(8,128)S(1)}, u32[]{:S(2)}, u32[]{:S(2)}) %collective-permute-start.1) | collective-permute-done | bytes 188448 | tf_op jit(solution)/shard_map/ppermute | solution.py:851
  15.6 0.2 shard_map.51
  15.7 0.1 collective-permute-start.2
  15.8 1.5 %collective-permute-done.2.theirs = f32[544,128]{1,0:T(8,128)S(1)} collective-permute-done((f32[544,128]{1,0:T(8,128)S(1)}, f32[544,128]{1,0:T(8,128)S(1)}, u32[]{:S(2)}, u32[]{:S(2)}) %collective-permute-start.2) | collective-permute-done | bytes 278560 | tf_op jit(solution)/shard_map/ppermute | solution.py:851
  17.3 1.6 %shard_map.52 = (f32[20,24,256]{2,1,0:T(8,128)S(1)}, f32[16,16,128]{2,1,0:T(8,128)S(1)}, f32[32,16,128]{2,1,0:T(8,128)S(1)}, f32[32,16,128]{2,1,0:T(8,128)S(1)},...) custom-call(f32[22,24,256]{2,1,0:T(8,128)S(1)} %get-tuple-element.24.r_in, f32[22,24,256]{2,1,0:T(8,128)S(1)} %get-tuple-element.25.x_in, ...), custom_call_target="tpu_custom_call" | custom-call | tf_op jit(solution)/shard_map/pallas_call | solution.py:834
  18.9 2.1 %collective-permute-start.3 = (f32[176,128]{1,0:T(8,128)S(1)}, f32[176,128]{1,0:T(8,128)S(1)}, u32[]{:S(2)}, u32[]{:S(2)}) collective-permute-start(f32[176,128]{1,0:T(8,128)S(1)} %get-tuple-element.31.ours), channel_id=1, source_target_pairs={{0,4},{1,13},{2,6},{3,15},{4,0},{5,9},{6,2},{7,11},{8,12},{9,5},{1... | collective-permute-start | bytes 270344 | tf_op jit(solution)/shard_map/ppermute | solution.py:851
  21.1 2.5 %collective-permute-done.3.got = f32[176,128]{1,0:T(8,128)S(1)} collective-permute-done((f32[176,128]{1,0:T(8,128)S(1)}, f32[176,128]{1,0:T(8,128)S(1)}, u32[]{:S(2)}, u32[]{:S(2)}) %collective-permute-start.3) | collective-permute-done | bytes 90144 | tf_op jit(solution)/shard_map/ppermute | solution.py:851
  23.6 4.1 %collective-permute-start.4 = (f32[240,128]{1,0:T(8,128)S(1)}, f32[240,128]{1,0:T(8,128)S(1)}, u32[]{:S(2)}, u32[]{:S(2)}) collective-permute-start(f32[240,128]{1,0:T(8,128)S(1)} %pad_maximum_fusion), channel_id=1, source_target_pairs={{0,12},{1,5},{2,14},{3,7},{4,8},{5,1},{6,10},{7,3},{8,4},{9,13},{1... | collective-permute-start | bytes 368648 | tf_op jit(solution)/shard_map/ppermute | solution.py:851
  27.7 4.1 %collective-permute-done.4.then = f32[240,128]{1,0:T(8,128)S(1)} collective-permute-done((f32[240,128]{1,0:T(8,128)S(1)}, f32[240,128]{1,0:T(8,128)S(1)}, u32[]{:S(2)}, u32[]{:S(2)}) %collective-permute-start.4) | collective-permute-done | bytes 122912 | tf_op jit(solution)/shard_map/ppermute | solution.py:851
  31.8 4.5 %shard_map.53 = (f32[16,16,128]{2,1,0:T(8,128)}, f32[16,16,128]{2,1,0:T(8,128)}, f32[2,1,16]{2,1,0:T(1,128)}) custom-call(f32[20,24,256]{2,1,0:T(8,128)S(1)} %get-tuple-element.27.r_in, f32[16,16,128]{2,1,0:T(8,128)S(1)} %get-tuple-element.28.x_in, f32[32,16,128]{2,1,0:T(8,128)S(1)} %get-tuple-element.29.r1_in, f32[32,16,128]{2,1,0:T(8,128)S(1)} %get-tuple-element.30.x1_in, ...), custom_call_target="tpu_custom_call" | custom-call | tf_op jit(solution)/shard_map/pallas_call | solution.py:834
  (3 shorter events, 0.0 us)
Async XLA Ops:
  0.6 0.9 %copy-start = (f32[16,16,128]{2,1,0:T(8,128)S(1)}, f32[16,16,128]{2,1,0:T(8,128)}, u32[]{:S(2)}) copy-start(f32[16,16,128]{2,1,0:T(8,128)} %b_in.1) | copy-start | bytes 393220
  1.5 0.9 %copy-start.1 = (f32[16,16,128]{2,1,0:T(8,128)S(1)}, f32[16,16,128]{2,1,0:T(8,128)}, u32[]{:S(2)}) copy-start(f32[16,16,128]{2,1,0:T(8,128)} %p_in.1) | copy-start | bytes 393220
  4.2 6.1 %collective-permute-start = (f32[280,128]{1,0:T(8,128)S(1)}, f32[280,128]{1,0:T(8,128)S(1)}, u32[]{:S(2)}, u32[]{:S(2)}) collective-permute-start(f32[280,128]{1,0:T(8,128)S(1)} %get-tuple-element.20.ours), channel_id=1, source_target_pairs={{0,16},{1,2},{2,1},{3,19},{4,20},{5,6},{6,5},{7,23},{8,24},{9,10},... | collective-permute-start | bytes 430088 | tf_op jit(solution)/shard_map/ppermute | solution.py:851
  10.5 5.1 %collective-permute-start.1 = (f32[368,128]{1,0:T(8,128)S(1)}, f32[368,128]{1,0:T(8,128)S(1)}, u32[]{:S(2)}, u32[]{:S(2)}) collective-permute-start(f32[368,128]{1,0:T(8,128)S(1)} %get-tuple-element.23.ours), channel_id=1, source_target_pairs={{0,3},{1,17},{2,18},{3,0},{4,7},{5,21},{6,22},{7,4},{8,11},{9,25},... | collective-permute-start | bytes 565256 | tf_op jit(solution)/shard_map/ppermute | solution.py:851
  15.7 1.6 %collective-permute-start.2 = (f32[544,128]{1,0:T(8,128)S(1)}, f32[544,128]{1,0:T(8,128)S(1)}, u32[]{:S(2)}, u32[]{:S(2)}) collective-permute-start(f32[544,128]{1,0:T(8,128)S(1)} %get-tuple-element.26.ours), channel_id=1, source_target_pairs={{0,1},{1,0},{2,3},{3,2},{4,5},{5,4},{6,7},{7,6},{8,9},{9,8},{10,11... | collective-permute-start | bytes 835592 | tf_op jit(solution)/shard_map/ppermute | solution.py:851
  18.9 4.7 %collective-permute-start.3 = (f32[176,128]{1,0:T(8,128)S(1)}, f32[176,128]{1,0:T(8,128)S(1)}, u32[]{:S(2)}, u32[]{:S(2)}) collective-permute-start(f32[176,128]{1,0:T(8,128)S(1)} %get-tuple-element.31.ours), channel_id=1, source_target_pairs={{0,4},{1,13},{2,6},{3,15},{4,0},{5,9},{6,2},{7,11},{8,12},{9,5},{1... | collective-permute-start | bytes 270344 | tf_op jit(solution)/shard_map/ppermute | solution.py:851
  23.6 8.2 %collective-permute-start.4 = (f32[240,128]{1,0:T(8,128)S(1)}, f32[240,128]{1,0:T(8,128)S(1)}, u32[]{:S(2)}, u32[]{:S(2)}) collective-permute-start(f32[240,128]{1,0:T(8,128)S(1)} %pad_maximum_fusion), channel_id=1, source_target_pairs={{0,12},{1,5},{2,14},{3,7},{4,8},{5,1},{6,10},{7,3},{8,4},{9,13},{1... | collective-permute-start | bytes 368648 | tf_op jit(solution)/shard_map/ppermute | solution.py:851

commit v5 on v4

--- a/solution.py
+++ b/solution.py
@@ -301,23 +301,25 @@
         self.layers = bz + 4
         self.level1 = (peers[0] * bz // 2, peers[1] * bx // 2, LANES)
         self.level2 = (peers[0] * bz // 4, peers[1] * bx // 4, peers[2] * by // 4)
-        self.y_groups = -(-self.layers // SLOTS)
-        self.fine_rows = self.y_groups * self.ex
+        self.inner = [0, 1] + [2] * bz + [1, 0]
+        self.slots, at = [], 0
+        for count in self.inner:
+            self.slots.append(at)
+            at += 3 + count + (2 if count == 2 else 0)
+        assert at <= LANES
+        self.fine_rows = self.ex
         self.edge = self.fine_rows + self.level1[0] * self.level1[1] // 8
-        self.share = self.level2[0] * self.level2[1] // 2
-
-
-def first_kernel(plan, b_in, p_in, r_ref, x_ref, pay, *scratch):
-    b_own, p_own, b_ext, p_ext, d_one, d_two, pairs, lines, sem = scratch
+        self.wide2 = by // 4 + 4
+        self.fold = LANES // self.wide2
+        self.lines2 = -(-self.level2[0] // self.fold)
+        self.share = self.lines2 * self.level2[1]
+
+
+def first_kernel(plan, both, r_ref, x_ref, pay, d_one, d_two, pairs, lines):
+    p_ext, b_ext = both.at[0], both.at[1]
     bz, bx, by = plan.block
     ez, ex, ey = plan.ext
     peers = plan.peers
-    copies = [
-        pltpu.make_async_copy(p_in, p_own, sem.at[0]),
-        pltpu.make_async_copy(b_in, b_own, sem.at[1]),
-    ]
-    for copy in copies:
-        copy.start()
     iz, z_low, z_high = place("gz", peers[0])
     ix, x_low, x_high = place("gx", peers[1])
     _, y_low, y_high = place("gy", peers[2])
@@ -334,14 +336,6 @@
         return v
 
     zero = jnp.zeros((ex, ey), F32)
-    for k in range(ez):
-        p_ext[k] = zero
-        b_ext[k] = zero
-    for copy in copies:
-        copy.wait()
-    for k in range(bz):
-        b_ext[k + 3, 0:bx, 0:by] = b_own[k]
-        p_ext[k + 3, 0:bx, 0:by] = p_own[k]
     for k in range(ez):
         if 2 <= k < ez - 2:
             r = b_ext[k] - apply_at(p_ext, k)
@@ -465,7 +459,7 @@
         pay[here:here + 2 * plan.coarse, :] = ref[plan.slab:plan.slab + 2 * plan.coarse, :]
 
 
-def plane_kernel(plan, r_in, x_in, ours, theirs, r_ref, x_ref, r1_ref, x1_ref, pay, later,
+def plane_kernel(plan, r_in, x_in, ours, theirs, r_ref, x_ref, r1_ref, x1_ref, pay, later, share,
                  r_all, x_all, b1, d1, d2, pairs, lines):
     bz, bx, by = plan.block
     ez, ex, ey = plan.ext
@@ -473,41 +467,32 @@
     iz, _, _ = place("gz", plan.peers[0])
     ix, _, _ = place("gx", plan.peers[1])
     iy, y_low, y_high = place("gy", plan.peers[2])
-    up, _ = side(iz, 1)
+    up_z, _ = side(iz, 1)
     for k in range(ez):
         r_all[k] = r_in[k]
         x_all[k] = x_in[k]
-    slab_add(r_all, x_all, theirs, 0, up)
+    slab_add(r_all, x_all, theirs, 0, up_z)
     for k in range(layers):
         r_ref[k] = r_all[k + 1]
     for k in range(bz):
         x_ref[k] = x_all[k + 3, 0:bx, 0:by]
 
-    even = (iz & 1) == 0
-    up_a, up_b = side(iy, 1)[0], side(iy, 3)[0]
-    up_now = (even & up_a) | (jnp.logical_not(even) & up_b)
-    up_later = (even & up_b) | (jnp.logical_not(even) & up_a)
-    edges = []
-    for which in range(2):
-        tiles = []
-        for group in range(plan.y_groups):
-            total = jnp.zeros((ex, LANES), F32)
-            for k in range(group * SLOTS, min(layers, (group + 1) * SLOTS)):
-                slot = 8 * (k - group * SLOTS)
-                v, spill = r_all[k + 1, :, 0:by], r_all[k + 1, :, by:ey]
-                if which == 0:
-                    total = total + moved(jnp.where(lanes_of(v, 0, 3), spill, v), LANES - 2, 5, slot)
-                else:
-                    total = total + moved(jnp.where(lanes_of(v, 0, 2), v, spill), LANES - 3, 5, slot)
-                if 2 <= k < 2 + bz:
-                    spill = x_all[k + 1, :, by:ey]
-                    total = total + moved(spill, 0 if which == 0 else LANES - 2, 2, slot + 5)
-            tiles.append(total)
-        edges.append(tiles)
-    for group in range(plan.y_groups):
-        here = slice(group * ex, (group + 1) * ex)
-        pay[here, :] = jnp.where(up_now, edges[0][group], edges[1][group])
-        later[here, :] = jnp.where(up_later, edges[0][group], edges[1][group])
+    up, _ = side(iy, 1)
+    up_inner, _ = side(iy, 3)
+    high, low = jnp.zeros((ex, LANES), F32), jnp.zeros((ex, LANES), F32)
+    for k in range(layers):
+        slot, inner = plan.slots[k], plan.inner[k]
+        count = 3 + inner
+        v, spill = r_all[k + 1, :, 0:by], r_all[k + 1, :, by:ey]
+        high = high + moved(jnp.where(lanes_of(v, 0, 3), spill, v), LANES - inner, count, slot)
+        mixed = jnp.where(lanes_of(v, 0, 2), v, spill)
+        low = low + moved(mixed, LANES - 3, count, slot)
+        if inner == 2:
+            spill = x_all[k + 1, :, by:ey]
+            high = high + moved(spill, 0, 2, slot + count)
+            low = low + moved(spill, LANES - 2, 2, slot + count)
+    pay[0:ex, :] = jnp.where(up, high, low)
+    later[0:ex, :] = jnp.where(up_inner, high, low)
 
     nz1, nx1, _ = plan.level1
     rows, half = plan.rows, by // 2
@@ -570,19 +555,22 @@
     nz2, nx2, _ = plan.level2
     for zc in range(nz2):
         pairs[zc * nx1:(zc + 1) * nx1, :] = r1_ref[2 * zc] + r1_ref[2 * zc + 1]
-        part, at = divmod(zc, nz2 // 2)
-        lines[at * nx2:(at + 1) * nx2, part * LANES:(part + 1) * LANES] = (
+        part, at = divmod(zc, plan.lines2)
+        lines[part, at * nx2:(at + 1) * nx2, :] = (
             pairs[pl.ds(zc * nx1, nx2, 2), :] + pairs[pl.ds(zc * nx1 + 1, nx2, 2), :]
         )
-    fine = iota((2 * LANES, LANES), 0)
-    part, fine = fine // LANES, signed(fine % LANES, half, LANES)
-    coarse = iota((2 * LANES, LANES), 1)
-    table = as_table(
-        (coarse // (LANES // 2) == part)
-        & (signed(coarse % (LANES // 2), half // 2, LANES // 2) == (fine >> 1)), 0.5
-    )
-    share = right_dot(lines[...], table)
-    pay[plan.edge:plan.edge + plan.share, :] = share
+    fine = signed(iota((LANES, LANES), 0), half, LANES)
+    total = None
+    for part in range(plan.fold):
+        count = min(plan.lines2, nz2 - part * plan.lines2) * nx2
+        if count < plan.share:
+            lines[part, count:, :] = jnp.zeros((plan.share - count, LANES), F32)
+        coarse = iota((LANES, LANES), 1) - part * plan.wide2 - 2
+        near = (coarse >= -2) & (coarse < plan.wide2 - 2)
+        term = right_dot(lines[part], as_table(near & ((fine >> 1) == coarse), 0.5))
+        total = term if total is None else total + term
+    share[...] = total
+    pay[plan.edge:plan.edge + plan.share, :] = total
 
     per_tile = LANES // 16
     for group in range(nz1 // per_tile):
@@ -597,8 +585,8 @@
                 total = total + moved(x1_ref[k], first, 5, 16 * j + 7)
             tiles.append(total)
         here = slice(plan.fine_rows + group * nx1, plan.fine_rows + (group + 1) * nx1)
-        pay[here, :] = jnp.where(up_now, tiles[0], tiles[1])
-        later[here, :] = jnp.where(up_later, tiles[0], tiles[1])
+        pay[here, :] = jnp.where(up, tiles[0], tiles[1])
+        later[here, :] = jnp.where(up_inner, tiles[0], tiles[1])
 
 
 def level_lateral(shape):
@@ -664,7 +652,7 @@
     return x, (x if level == LEVELS - 1 else coarsest)
 
 
-def last_kernel(plan, r_in, x_in, r1_in, x1_in, ours, got, then, p_out, res_out, last_ref, *scratch):
+def last_kernel(plan, r_in, x_in, r1_in, x1_in, ours, from_a, from_b, from_3, from_2, p_out, res_out, last_ref, *scratch):
     shares, p_ref, res_ref, r, q1, e1, e0, d0, d1, r1, lines, wide, sem = scratch
     bz, bx, by = plan.block
     ez, ex, ey = plan.ext
@@ -675,25 +663,19 @@
     ix, x_low, x_high = place("gx", plan.peers[1])
     iy, y_low, y_high = place("gy", plan.peers[2])
 
-    even = (iz & 1) == 0
-    first = jnp.where(even, 1, 3)
-    here = plan.edge + plan.share
-    shares[0] = ours[plan.edge:here, :]
-    shares[first] = got[plan.edge:here, :]
-    shares[4 - first] = then[plan.edge:here, :]
-    shares[2] = then[here:here + plan.share, :]
-    lower = upper = None
+    shares[0] = ours[...]
+    shares[1] = from_a[plan.edge:plan.edge + plan.share, :]
+    shares[2] = from_2[...]
+    shares[3] = from_3[...]
     own2 = half // 2
-    for j in range(plan.peers[2]):
-        v = shares[iy ^ j]
-        at = own2 * j
-        mid = LANES // 2
-        low = moved(v, 0, own2 + 2, at) + moved(v, mid - 2, 2, at - 2)
-        high = moved(v, mid, own2 + 2, at) + moved(v, LANES - 2, 2, at - 2)
-        lower = low if lower is None else lower + low
-        upper = high if upper is None else upper + high
-    source = [lower[8 * k:8 * k + 8] for k in range(nz2 // 2)]
-    source += [upper[8 * k:8 * k + 8] for k in range(nz2 // 2)]
+    source = []
+    for part in range(plan.fold):
+        total = None
+        for j in range(plan.peers[2]):
+            v = moved(shares[iy ^ j], part * plan.wide2, plan.wide2, own2 * j - 2)
+            total = v if total is None else total + v
+        source += [total[nx2 * k:nx2 * (k + 1)] for k in range(plan.lines2)]
+    source = source[:nz2]
     e2, coarsest = small_cycle(2, source)
     for k in range(nz2):
         lines[k * nx2:(k + 1) * nx2, :] = e2[k]
@@ -705,8 +687,7 @@
     _, near_b = side(iy, 3)
 
     def sent(rows):
-        a, b = got[rows[0]:rows[1], :], then[rows[0]:rows[1], :]
-        a, b = jnp.where(even, a, b), only(near_b, jnp.where(even, b, a))
+        a, b = from_a[rows[0]:rows[1], :], only(near_b, from_b[rows[0]:rows[1], :])
         return jnp.where(up_a, a, b), jnp.where(up_a, b, a)
 
     fine = signed(iota((LANES, LANES), 1), half, LANES)
@@ -780,19 +761,23 @@
             v = v * above
         return v
 
-    for group in range(plan.y_groups):
-        high, low = sent((group * ex, (group + 1) * ex))
-        for k in range(group * SLOTS, min(layers, (group + 1) * SLOTS)):
-            s = 8 * (k - group * SLOTS)
-            v = r_in[k] - apply_at(e0, k + 1)
-            r[k, :, 0:by] = v[:, 0:by] + moved(high, s, 3, LANES - 3) + moved(low, s + 2, 3, 0)
-            r[k, :, by:ey] = v[:, by:ey] + moved(high, s + 3, 2, 0) + moved(low, s, 2, LANES - 2)
-            d0[k] = masked(k + 1, r[k] * first_scale)
-            if 2 <= k < 2 + bz:
-                p_ref[k - 2] = (
-                    x_in[k - 2] + e0[k + 1, 0:bx, 0:by]
-                    + (moved(high, s + 5, 2, LANES - 2) + moved(low, s + 5, 2, 0))[0:bx]
-                )
+    high, low = sent((0, ex))
+    for k in range(layers):
+        s, inner = plan.slots[k], plan.inner[k]
+        v = r_in[k] - apply_at(e0, k + 1)
+        own = v[:, 0:by] + moved(high, s, 3, LANES - 3) + moved(low, s + inner, 3, 0)
+        spill = v[:, by:ey]
+        if inner:
+            spill = spill + moved(high, s + 3, inner, 0) + moved(low, s, inner, LANES - inner)
+        r[k, :, 0:by] = own
+        r[k, :, by:ey] = spill
+        d0[k] = masked(k + 1, r[k] * first_scale)
+        if inner == 2:
+            s = s + 3 + inner
+            p_ref[k - 2] = (
+                x_in[k - 2] + e0[k + 1, 0:bx, 0:by]
+                + (moved(high, s, 2, LANES - 2) + moved(low, s, 2, 0))[0:bx]
+            )
     for k in range(1, layers - 1):
         v = r[k] - apply_at(d0, k)
         r[k] = v
@@ -823,18 +808,17 @@
 
 VMEM = pl.BlockSpec(memory_space=pltpu.VMEM)
 ANY = pl.BlockSpec(memory_space=pl.ANY)
-HBM = pl.BlockSpec(memory_space=pltpu.HBM)
 VMEM_BYTES = 24 << 20
 
 
-def run(kernel, plan, outs, scratch, *operands, in_specs=None, out_specs=None, semaphores=0):
+def run(kernel, plan, outs, scratch, *operands, out_specs=None, semaphores=0):
     scratch = [pltpu.VMEM(s, F32) for s in scratch]
     if semaphores:
         scratch.append(pltpu.SemaphoreType.DMA((semaphores,)))
     return pl.pallas_call(
         functools.partial(kernel, plan),
         out_shape=[whole(s) for s in outs],
-        in_specs=in_specs or [VMEM] * len(operands),
+        in_specs=[VMEM] * len(operands),
         out_specs=out_specs or [VMEM] * len(outs),
         scratch_shapes=scratch,
         compiler_params=pltpu.CompilerParams(vmem_limit_bytes=VMEM_BYTES),
@@ -846,44 +830,54 @@
     counts = [lax.axis_size(a) for a in axes]
     pairs = []
     for i in range(counts[0] * counts[1] * counts[2]):
-        x, y, z = partner(i // (counts[1] * counts[2]), i // counts[2] % counts[1], i % counts[2])
-        pairs.append((i, (x * counts[1] + y) * counts[2] + z))
+        to = partner(i // (counts[1] * counts[2]), i // counts[2] % counts[1], i % counts[2])
+        if to is not None:
+            pairs.append((i, (to[0] * counts[1] + to[1]) * counts[2] + to[2]))
     return lax.ppermute(values, axes, pairs)
+
+
+def swap_parts(values, partner):
+    cut = values.shape[0] * 5 // 64 * 8
+    parts = [swap(values[:cut], partner), swap(values[cut:], partner)]
+    return jnp.concatenate(parts, axis=0)
 
 
 def body_fast(divergence, pressure_prev):
     plan = Plan(divergence.shape, tuple(lax.axis_size(a) for a in ("gz", "gx", "gy")))
     ext, level1 = plan.ext, plan.level1
     payload = [(plan.slab + n * plan.coarse, LANES) for n in (1, 2, 4)]
+    both = jnp.stack([pressure_prev, divergence])
+    both = jnp.pad(both, ((0, 0), (3, 3), (0, plan.ex - plan.block[1]), (0, plan.ey - plan.block[2])))
     r, x, ours = run(
         first_kernel, plan, [ext, ext, payload[0]],
-        [plan.block, plan.block, ext, ext, ext, ext, (2, 2 * plan.pairs * plan.ex, LANES),
-         (2, plan.lat_at, plan.ey)],
-        divergence, pressure_prev, in_specs=[HBM, HBM], semaphores=2,
+        [ext, ext, (2, 2 * plan.pairs * plan.ex, LANES), (2, plan.lat_at, plan.ey)],
+        both,
     )
-    got = swap(ours, lambda x, y, z: (x, y, z ^ 3) if z in (1, 2) else (x ^ 1, y, z))
+    got = swap_parts(ours, lambda x, y, z: (x, y, z ^ 3) if z in (1, 2) else (x ^ 1, y, z))
     r, x, ours = run(step_kernel, plan, [ext, ext, payload[1]], [], r, x, ours, got)
-    got = swap(ours, lambda x, y, z: (x ^ 1, y, z) if z in (1, 2) else (x, y, z ^ 3))
+    got = swap_parts(ours, lambda x, y, z: (x ^ 1, y, z) if z in (1, 2) else (x, y, z ^ 3))
     r, x, ours = run(core_kernel, plan, [ext, ext, payload[2]], [], r, x, ours, got)
     got = swap(ours, lambda x, y, z: (x, y, z ^ 1))
     nz2, nx2, _ = plan.level2
     layers = (plan.layers, plan.ex, plan.ey)
-    r, x, r1, x1, ours, later = run(
+    share = (plan.share, LANES)
+    r, x, r1, x1, now, later, ours = run(
         plane_kernel, plan,
-        [layers, plan.block, level1, level1, (plan.edge + plan.share, LANES), (plan.edge, LANES)],
-        [ext, ext, level1, level1, level1, (nz2 * level1[1], LANES), (plan.share, 2 * LANES)],
+        [layers, plan.block, level1, level1, (plan.edge + plan.share, LANES), (plan.edge, LANES), share],
+        [ext, ext, level1, level1, level1, (nz2 * level1[1], LANES), (plan.fold,) + share],
         r, x, ours, got,
     )
-    got = swap(ours, lambda x, y, z: (x, y ^ (1, 3)[z & 1], z))
-    then = jnp.concatenate([later, ours[plan.edge:], got[plan.edge:]], axis=0)
-    then = swap(then, lambda x, y, z: (x, y ^ (3, 1)[z & 1], z))
+    from_a = swap(now, lambda x, y, z: (x, y ^ 1, z))
+    from_b = swap(later, lambda x, y, z: (x, y ^ 3, z) if y in (1, 2) else None)
+    from_3 = swap(ours, lambda x, y, z: (x, y ^ 3, z))
+    from_2 = swap(ours, lambda x, y, z: (x, y ^ 2, z))
     return run(
         last_kernel, plan,
         [plan.block, plan.block, tuple(n >> 3 for n in plan.level2)],
-        [(4, plan.share, LANES), plan.block, plan.block, layers, level1,
+        [(4,) + share, plan.block, plan.block, layers, level1,
          (level1[0] + 4, level1[1] + 16, LANES), ext, layers, level1, level1,
          (nz2 * nx2, LANES), (2 * plan.pairs * plan.ex, LANES)],
-        r, x, r1, x1, ours, got, then,
+        r, x, r1, x1, ours, from_a, from_b, from_3, from_2,
         out_specs=[ANY, ANY, VMEM], semaphores=3,
     )
 

time: 36.5 us -> 35.6 us (0.975)
  starting transfers between devices: 10 us -> 14.1 us
  waiting for transfers between devices: 15.6 us -> 11.6 us
  local copies, waits for them, and re-layouts: 1.81 us -> 0.03 us
  other arithmetic: 0.01 us -> 1.07 us
    ppermute x5 -> x9, starting transfers between devices: 10 us -> 14.1 us  [swap(): return lax.ppermute(values, axes, pairs)]
    ppermute x5 -> x9, waiting for transfers between devices: 15.6 us -> 11.6 us  [swap(): return lax.ppermute(values, axes, pairs)]
    unnamed x4 -> x0, local copies, waits for them, and re-layouts: 1.8 us -> none
    another operation x0 -> x1, other arithmetic: none -> 1.04 us  [body_fast(): both = jnp.stack([pressure_prev, divergence])]
  transfers between devices with their start and end apart: 5 -> 9, of which waited for: 5 -> 4; matrix products, arithmetic and copies ran while one was open for 0% -> 0% of each run, Pallas kernels for 0% -> 0%
where the time goes in v5:
time: 35.6 us; the launch traced here: 35.4 us
  starting transfers between devices  14.1 us (40%)
  waiting for transfers between devices  11.6 us (33%)
  Pallas kernels  7.91 us (22%)
  other arithmetic  1.07 us (3%)
  between operations  0.72 us (2%)
    ppermute x9, starting transfers between devices, swap(): return lax.ppermute(values, axes, pairs)  14.1 us
    ppermute x9, waiting for transfers between devices, swap(): return lax.ppermute(values, axes, pairs)  11.6 us
    pallas_call x5, Pallas kernels, run(): pl.pallas_call(functools.partial(kernel, plan), out_shape=[whole(s) for s...  7.91 us
    another operation x1, other arithmetic, body_fast(): both = jnp.stack([pressure_prev, divergence])  1.04 us
  transfers between devices with their start and end apart: 9, of which 4 were waited for; matrix products, arithmetic and copies ran while one was open for 0% of the time, Pallas kernels for 0%

profile of v5, /device:TPU:0, one launch (start us, length us, event | category | flops | bytes accessed | tf_op | source)
XLA Modules:
  0.0 35.4 jit_solution(9756066408440125271)
XLA Ops:
  0.6 1.0 %select_maximum_fusion.both = f32[2,22,24,256]{3,2,1,0:T(8,128)S(1)} fusion(f32[1,16,16,128]{3,2,1,0:T(8,128)} %bitcast.2, f32[1,16,16,128]{3,2,1,0:T(8,128)} %bitcast.3), kind=kLoop, calls=%fused_computation.2 | loop fusion | flops 3784704 | bytes 1343488 | tf_op jit(solution)/shard_map/stack | solution.py:849
  1.7 1.5 %shard_map.49 = (f32[22,24,256]{2,1,0:T(8,128)S(1)}, f32[22,24,256]{2,1,0:T(8,128)S(1)}, f32[280,128]{1,0:T(8,128)S(1)}) custom-call(f32[2,22,24,256]{3,2,1,0:T(8,128)S(1)} %select_maximum_fusion.both), custom_call_target="tpu_custom_call" | custom-call | tf_op jit(solution)/shard_map/pallas_call | solution.py:818
  3.2 3.0 %collective-permute-start = (f32[168,128]{1,0:T(8,128)S(1)}, f32[168,128]{1,0:T(8,128)S(1)}, u32[]{:S(2)}, u32[]{:S(2)}) collective-permute-start(f32[168,128]{1,0:T(8,128)S(1)} %slice.12), channel_id=1, source_target_pairs={{0,16},{1,2},{2,1},{3,19},{4,20},{5,6},{6,5},{7,23},{8,24},{9,10},... | collective-permute-start | bytes 258056 | tf_op jit(solution)/shard_map/ppermute | solution.py:836
  6.2 0.1 collective-permute-start.1
  6.3 4.1 %collective-permute-done.1 = f32[112,128]{1,0:T(8,128)S(1)} collective-permute-done((f32[112,128]{1,0:T(8,128)S(1)}, f32[112,128]{1,0:T(8,128)S(1)}, u32[]{:S(2)}, u32[]{:S(2)}) %collective-permute-start.1) | collective-permute-done | bytes 57376 | tf_op jit(solution)/shard_map/ppermute | solution.py:836
  10.4 0.0 collective-permute-done
  10.4 0.2 shard_map.50
  10.6 0.1 collective-permute-start.2
  10.7 1.7 %collective-permute-start.3 = (f32[144,128]{1,0:T(8,128)S(1)}, f32[144,128]{1,0:T(8,128)S(1)}, u32[]{:S(2)}, u32[]{:S(2)}) collective-permute-start(f32[144,128]{1,0:T(8,128)S(1)} %slice.15), channel_id=1, source_target_pairs={{0,3},{1,17},{2,18},{3,0},{4,7},{5,21},{6,22},{7,4},{8,11},{9,25},... | collective-permute-start | bytes 221192 | tf_op jit(solution)/shard_map/ppermute | solution.py:836
  12.5 3.3 %collective-permute-done.3 = f32[144,128]{1,0:T(8,128)S(1)} collective-permute-done((f32[144,128]{1,0:T(8,128)S(1)}, f32[144,128]{1,0:T(8,128)S(1)}, u32[]{:S(2)}, u32[]{:S(2)}) %collective-permute-start.3) | collective-permute-done | bytes 73760 | tf_op jit(solution)/shard_map/ppermute | solution.py:836
  15.7 0.0 collective-permute-done.2
  15.7 0.2 shard_map.51
  15.9 0.1 collective-permute-start.4
  16.0 1.5 %collective-permute-done.4.theirs = f32[544,128]{1,0:T(8,128)S(1)} collective-permute-done((f32[544,128]{1,0:T(8,128)S(1)}, f32[544,128]{1,0:T(8,128)S(1)}, u32[]{:S(2)}, u32[]{:S(2)}) %collective-permute-start.4) | collective-permute-done | bytes 278560 | tf_op jit(solution)/shard_map/ppermute | solution.py:836
  17.5 1.5 %shard_map.52 = (f32[20,24,256]{2,1,0:T(8,128)S(1)}, f32[16,16,128]{2,1,0:T(8,128)S(1)}, f32[32,16,128]{2,1,0:T(8,128)S(1)}, f32[32,16,128]{2,1,0:T(8,128)S(1)},...) custom-call(f32[22,24,256]{2,1,0:T(8,128)S(1)} %get-tuple-element.25.r_in, ...), custom_call_target="tpu_custom_call" | custom-call | tf_op jit(solution)/shard_map/pallas_call | solution.py:818
  19.1 1.6 %collective-permute-start.5 = (f32[136,128]{1,0:T(8,128)S(1)}, f32[136,128]{1,0:T(8,128)S(1)}, u32[]{:S(2)}, u32[]{:S(2)}) collective-permute-start(f32[136,128]{1,0:T(8,128)S(1)} %get-tuple-element.33), channel_id=1, source_target_pairs={{0,4},{1,5},{2,6},{3,7},{4,0},{5,1},{6,2},{7,3},{8,12},{9,13},{10,... | collective-permute-start | bytes 208904 | tf_op jit(solution)/shard_map/ppermute | solution.py:836
  20.7 0.7 %collective-permute-start.6 = (f32[88,128]{1,0:T(8,128)S(1)}, f32[88,128]{1,0:T(8,128)S(1)}, u32[]{:S(2)}, u32[]{:S(2)}) collective-permute-start(f32[88,128]{1,0:T(8,128)S(1)} %get-tuple-element.34), channel_id=1, source_target_pairs={{4,8},{5,9},{6,10},{7,11},{8,4},{9,5},{10,6},{11,7},{20,24},{21,25... | collective-permute-start | bytes 135176 | tf_op jit(solution)/shard_map/ppermute | solution.py:836
  21.4 3.9 %collective-permute-start.8 = (f32[48,128]{1,0:T(8,128)S(1)}, f32[48,128]{1,0:T(8,128)S(1)}, u32[]{:S(2)}, u32[]{:S(2)}) collective-permute-start(f32[48,128]{1,0:T(8,128)S(1)} %get-tuple-element.32.ours), channel_id=1, source_target_pairs={{0,8},{1,9},{2,10},{3,11},{4,12},{5,13},{6,14},{7,15},{8,0},{9,1},... | collective-permute-start | bytes 73736 | tf_op jit(solution)/shard_map/ppermute | solution.py:836
  25.3 2.9 %collective-permute-start.7 = (f32[48,128]{1,0:T(8,128)S(1)}, f32[48,128]{1,0:T(8,128)S(1)}, u32[]{:S(2)}, u32[]{:S(2)}) collective-permute-start(f32[48,128]{1,0:T(8,128)S(1)} %get-tuple-element.32.ours), channel_id=1, source_target_pairs={{0,12},{1,13},{2,14},{3,15},{4,8},{5,9},{6,10},{7,11},{8,4},{9,5},... | collective-permute-start | bytes 73736 | tf_op jit(solution)/shard_map/ppermute | solution.py:836
  28.2 0.0 collective-permute-done.8.from_2
  28.2 2.7 %collective-permute-done.7.from_3 = f32[48,128]{1,0:T(8,128)S(1)} collective-permute-done((f32[48,128]{1,0:T(8,128)S(1)}, f32[48,128]{1,0:T(8,128)S(1)}, u32[]{:S(2)}, u32[]{:S(2)}) %collective-permute-start.7) | collective-permute-done | bytes 24608 | tf_op jit(solution)/shard_map/ppermute | solution.py:836
  30.9 0.0 collective-permute-done.6.from_b
  30.9 0.0 collective-permute-done.5.from_a
  30.9 4.5 %shard_map.53 = (f32[16,16,128]{2,1,0:T(8,128)}, f32[16,16,128]{2,1,0:T(8,128)}, f32[2,1,16]{2,1,0:T(1,128)}) custom-call(f32[20,24,256]{2,1,0:T(8,128)S(1)} %get-tuple-element.28.r_in, f32[16,16,128]{2,1,0:T(8,128)S(1)} %get-tuple-element.29.x_in, f32[32,16,128]{2,1,0:T(8,128)S(1)} %get-tuple-element.30.r1_in, f32[32,16,128]{2,1,0:T(8,128)S(1)} %get-tuple-element.31.x1_in, ...), custom_call_target="tpu_custom_call" | custom-call | tf_op jit(solution)/shard_map/pallas_call | solution.py:818
  (6 shorter events, 0.1 us)
Async XLA Ops:
  3.2 7.2 %collective-permute-start = (f32[168,128]{1,0:T(8,128)S(1)}, f32[168,128]{1,0:T(8,128)S(1)}, u32[]{:S(2)}, u32[]{:S(2)}) collective-permute-start(f32[168,128]{1,0:T(8,128)S(1)} %slice.12), channel_id=1, source_target_pairs={{0,16},{1,2},{2,1},{3,19},{4,20},{5,6},{6,5},{7,23},{8,24},{9,10},... | collective-permute-start | bytes 258056 | tf_op jit(solution)/shard_map/ppermute | solution.py:836
  6.2 4.2 %collective-permute-start.1 = (f32[112,128]{1,0:T(8,128)S(1)}, f32[112,128]{1,0:T(8,128)S(1)}, u32[]{:S(2)}, u32[]{:S(2)}) collective-permute-start(f32[112,128]{1,0:T(8,128)S(1)} %slice.13), channel_id=1, source_target_pairs={{0,16},{1,2},{2,1},{3,19},{4,20},{5,6},{6,5},{7,23},{8,24},{9,10},... | collective-permute-start | bytes 172040 | tf_op jit(solution)/shard_map/ppermute | solution.py:836
  10.6 5.1 %collective-permute-start.2 = (f32[224,128]{1,0:T(8,128)S(1)}, f32[224,128]{1,0:T(8,128)S(1)}, u32[]{:S(2)}, u32[]{:S(2)}) collective-permute-start(f32[224,128]{1,0:T(8,128)S(1)} %slice.14), channel_id=1, source_target_pairs={{0,3},{1,17},{2,18},{3,0},{4,7},{5,21},{6,22},{7,4},{8,11},{9,25},... | collective-permute-start | bytes 344072 | tf_op jit(solution)/shard_map/ppermute | solution.py:836
  10.7 5.0 %collective-permute-start.3 = (f32[144,128]{1,0:T(8,128)S(1)}, f32[144,128]{1,0:T(8,128)S(1)}, u32[]{:S(2)}, u32[]{:S(2)}) collective-permute-start(f32[144,128]{1,0:T(8,128)S(1)} %slice.15), channel_id=1, source_target_pairs={{0,3},{1,17},{2,18},{3,0},{4,7},{5,21},{6,22},{7,4},{8,11},{9,25},... | collective-permute-start | bytes 221192 | tf_op jit(solution)/shard_map/ppermute | solution.py:836
  15.9 1.6 %collective-permute-start.4 = (f32[544,128]{1,0:T(8,128)S(1)}, f32[544,128]{1,0:T(8,128)S(1)}, u32[]{:S(2)}, u32[]{:S(2)}) collective-permute-start(f32[544,128]{1,0:T(8,128)S(1)} %get-tuple-element.27.ours), channel_id=1, source_target_pairs={{0,1},{1,0},{2,3},{3,2},{4,5},{5,4},{6,7},{7,6},{8,9},{9,8},{10,11... | collective-permute-start | bytes 835592 | tf_op jit(solution)/shard_map/ppermute | solution.py:836
  19.1 11.8 %collective-permute-start.5 = (f32[136,128]{1,0:T(8,128)S(1)}, f32[136,128]{1,0:T(8,128)S(1)}, u32[]{:S(2)}, u32[]{:S(2)}) collective-permute-start(f32[136,128]{1,0:T(8,128)S(1)} %get-tuple-element.33), channel_id=1, source_target_pairs={{0,4},{1,5},{2,6},{3,7},{4,0},{5,1},{6,2},{7,3},{8,12},{9,13},{10,... | collective-permute-start | bytes 208904 | tf_op jit(solution)/shard_map/ppermute | solution.py:836
  20.7 10.2 %collective-permute-start.6 = (f32[88,128]{1,0:T(8,128)S(1)}, f32[88,128]{1,0:T(8,128)S(1)}, u32[]{:S(2)}, u32[]{:S(2)}) collective-permute-start(f32[88,128]{1,0:T(8,128)S(1)} %get-tuple-element.34), channel_id=1, source_target_pairs={{4,8},{5,9},{6,10},{7,11},{8,4},{9,5},{10,6},{11,7},{20,24},{21,25... | collective-permute-start | bytes 135176 | tf_op jit(solution)/shard_map/ppermute | solution.py:836
  21.4 6.8 %collective-permute-start.8 = (f32[48,128]{1,0:T(8,128)S(1)}, f32[48,128]{1,0:T(8,128)S(1)}, u32[]{:S(2)}, u32[]{:S(2)}) collective-permute-start(f32[48,128]{1,0:T(8,128)S(1)} %get-tuple-element.32.ours), channel_id=1, source_target_pairs={{0,8},{1,9},{2,10},{3,11},{4,12},{5,13},{6,14},{7,15},{8,0},{9,1},... | collective-permute-start | bytes 73736 | tf_op jit(solution)/shard_map/ppermute | solution.py:836
  25.3 5.6 %collective-permute-start.7 = (f32[48,128]{1,0:T(8,128)S(1)}, f32[48,128]{1,0:T(8,128)S(1)}, u32[]{:S(2)}, u32[]{:S(2)}) collective-permute-start(f32[48,128]{1,0:T(8,128)S(1)} %get-tuple-element.32.ours), channel_id=1, source_target_pairs={{0,12},{1,13},{2,14},{3,15},{4,8},{5,9},{6,10},{7,11},{8,4},{9,5},... | collective-permute-start | bytes 73736 | tf_op jit(solution)/shard_map/ppermute | solution.py:836

commit v6 on v5

--- a/solution.py
+++ b/solution.py
@@ -208,38 +208,95 @@
 
 
 def side_pack(tile, slot):
-    return moved(tile, LANES - 3, 6, 8 * slot)
+    return moved(tile, LANES - 3, 6, 6 * slot)
 
 
 def side_unpack(packed, slot):
-    return moved(packed, 8 * slot, 6, LANES - 3)
-
-
-SLOTS = LANES // 8
-
-
-def slab_emit(r_ref, x_ref, out, at, up):
-    ez, ex, _ = r_ref.shape
-    start = jnp.where(up, ez - 5, 0)
-    start_x = jnp.where(up, ez - 3, 1)
+    return moved(packed, 6 * slot, 6, LANES - 3)
+
+
+def slab_layers(r_ref, x_ref, up, low, high):
+    start = jnp.where(up, high[0], low[0])
+    start_x = jnp.where(up, high[1], low[1])
+    return [(r_ref, start + j) for j in range(5)] + [(x_ref, start_x + j) for j in range(2)]
+
+
+def slab_own(r_ref, x_ref, up):
+    ez = r_ref.shape[0]
+    return slab_layers(r_ref, x_ref, up, (0, 1), (ez - 5, ez - 3))
+
+
+def slab_there(r_ref, x_ref, up):
+    ez = r_ref.shape[0]
+    return slab_layers(r_ref, x_ref, up, (1, 3), (ez - 6, ez - 5))
+
+
+def slab_emit(r_ref, x_ref, out, up):
+    ex = r_ref.shape[1]
     lat = None
-    for j in range(7):
-        v = r_ref[start + j] if j < 5 else x_ref[start_x + j - 5]
-        out[at + j * ex:at + (j + 1) * ex, :] = v[:, 0:LANES]
+    for j, (ref, k) in enumerate(slab_own(r_ref, x_ref, up)):
+        v = ref[k]
+        out[j * ex:(j + 1) * ex, :] = v[:, 0:LANES]
         part = side_pack(v[:, LANES:], j)
         lat = part if lat is None else lat + part
-    out[at + 7 * ex:at + 8 * ex, :] = lat
-
-
-def slab_add(r_ref, x_ref, slab, at, up):
-    ez, ex, _ = r_ref.shape
-    start = jnp.where(up, ez - 6, 1)
-    start_x = jnp.where(up, ez - 5, 3)
-    lat = slab[at + 7 * ex:at + 8 * ex, :]
-    for j in range(7):
-        ref, k = (r_ref, start + j) if j < 5 else (x_ref, start_x + j - 5)
-        ref[k, :, 0:LANES] += slab[at + j * ex:at + (j + 1) * ex, :]
+    out[7 * ex:8 * ex, :] = lat
+
+
+def slab_add(r_ref, x_ref, slab, up):
+    ex = r_ref.shape[1]
+    lat = slab[7 * ex:8 * ex, :]
+    for j, (ref, k) in enumerate(slab_there(r_ref, x_ref, up)):
+        ref[k, :, 0:LANES] += slab[j * ex:(j + 1) * ex, :]
         ref[k, :, LANES:] += side_unpack(lat, j)
+
+
+BESIDE = ((2, 2, 0, 0), (1, 1, 0, 3), (3, 1, 0, 5), (5, 1, 1, 0), (6, 1, 1, 3))
+
+
+def beside(tile, count):
+    row = iota(tile.shape, 0)
+    return only((row < count) | (row >= 8 - count), tile)
+
+
+def thin_emit(r_ref, x_ref, out, up):
+    bx = r_ref.shape[1] - 8
+    layers = slab_own(r_ref, x_ref, up)
+    lat = None
+    for j, (ref, k) in enumerate(layers):
+        out[j * bx:(j + 1) * bx, :] = ref[k, 0:bx, 0:LANES]
+        part = side_pack(ref[k, 0:bx, LANES:], j)
+        lat = part if lat is None else lat + part
+    tiles = [None, None]
+    for j, count, which, turn in BESIDE:
+        ref, k = layers[j]
+        part = beside(ref[k, bx:, 0:LANES], count)
+        part = pltpu.roll(part, turn, 0) if turn else part
+        tiles[which] = part if tiles[which] is None else tiles[which] + part
+    at = 7 * bx
+    out[at:at + 8, :] = tiles[0]
+    out[at + 8:at + 16, :] = tiles[1]
+    out[at + 16:at + 16 + bx, :] = lat
+    for j in (1, 2, 3):
+        ref, k = layers[j]
+        out[at + 16:at + 24, :] += side_pack(ref[k, bx:, LANES:], 6 + j)
+
+
+def thin_add(r_ref, x_ref, slab, up):
+    bx = r_ref.shape[1] - 8
+    layers = slab_there(r_ref, x_ref, up)
+    at = 7 * bx
+    lat = slab[at + 16:at + 16 + bx, :]
+    for j, (ref, k) in enumerate(layers):
+        ref[k, 0:bx, 0:LANES] += slab[j * bx:(j + 1) * bx, :]
+        ref[k, 0:bx, LANES:] += side_unpack(lat, j)
+    for j, count, which, turn in BESIDE:
+        ref, k = layers[j]
+        tile = slab[at + 8 * which:at + 8 * which + 8, :]
+        tile = pltpu.roll(tile, 8 - turn, 0) if turn else tile
+        ref[k, bx:, 0:LANES] += beside(tile, count)
+    for j in (1, 2, 3):
+        ref, k = layers[j]
+        ref[k, bx:, LANES:] += side_unpack(lat[0:8], 6 + j)
 
 
 def rows_out(r, x, up):
@@ -270,34 +327,55 @@
 
 def rows_emit(r_ref, x_ref, out, up):
     ez = r_ref.shape[0]
-    for group in range(-(-ez // SLOTS)):
-        lat = jnp.zeros((8, LANES), F32)
-        for k in range(group * SLOTS, min(ez, (group + 1) * SLOTS)):
-            rows = rows_out(r_ref[k], x_ref[k], up)
-            out[8 * k:8 * k + 8, :] = rows[:, 0:LANES]
-            lat = lat + side_pack(rows[:, LANES:], k - group * SLOTS)
-        out[8 * (ez + group):8 * (ez + group) + 8, :] = lat
+    row = iota((8, LANES), 0)
+    lat = jnp.zeros((8, LANES), F32)
+    for t, k in enumerate(range(1, ez - 1)):
+        far = {1: 0, ez - 2: ez - 1}.get(k)
+        rows = rows_out(r_ref[k], None if far is not None else x_ref[k], up)
+        tile = rows[:, 0:LANES]
+        if far is not None:
+            more = rows_out(r_ref[far, :, 0:LANES], None, up)
+            more = jnp.where(up, pltpu.roll(more, 5, 0), pltpu.roll(more, 2, 0))
+            tile = jnp.where((row == 5) | (row == 6), more, tile)
+        out[8 * t:8 * t + 8, :] = tile
+        lat = lat + side_pack(rows[:, LANES:], t)
+    at = 8 * (ez - 2)
+    out[at:at + 8, :] = lat
 
 
 def rows_add(r_ref, x_ref, slab, up):
     ez = r_ref.shape[0]
-    for k in range(ez):
-        at = 8 * (ez + k // SLOTS)
-        lat = side_unpack(slab[at:at + 8, :], k % SLOTS)
-        rows = jnp.concatenate([slab[8 * k:8 * k + 8, :], lat], axis=1)
-        rows_in(r_ref, x_ref, k, rows, up)
+    at = 8 * (ez - 2)
+    lat = slab[at:at + 8, :]
+    row = iota((8, LANES), 0)
+    for t, k in enumerate(range(1, ez - 1)):
+        far = {1: 0, ez - 2: ez - 1}.get(k)
+        tile = slab[8 * t:8 * t + 8, :]
+        rows = jnp.concatenate([tile, side_unpack(lat, t)], axis=1)
+        rows_in(r_ref, None if far is not None else x_ref, k, rows, up)
+        if far is not None:
+            tile = only((row == 5) | (row == 6), tile)
+            tile = jnp.where(up, pltpu.roll(tile, 6, 0), pltpu.roll(tile, 3, 0))
+            rows = jnp.concatenate([tile, jnp.zeros((8, LANES), F32)], axis=1)
+            rows_in(r_ref, None, far, rows, up)
 
 
 class Plan:
+    def first_layer(self, iz):
+        start = iz * (self.block[0] // 2) - 4
+        return jnp.clip(start, 0, self.level1[0] - self.window[0])
+
     def __init__(self, shape, peers):
         self.peers = peers
         self.block = bz, bx, by = shape
         self.ext = self.ez, self.ex, self.ey = bz + 6, bx + 8, by + LANES
         self.rows, self.pairs = bx // 2, bz // 4 + 2
         self.lat_at = self.pairs * (self.rows + 4)
-        self.coarse = self.lat_at + 16
-        self.x_groups = -(-self.ez // SLOTS)
-        self.slab = max(8 * self.ex, (self.ez + self.x_groups) * 8)
+        self.coarse = self.lat_at + 8
+        self.slab = 8 * self.ex
+        self.slab_z = 8 * bx + 16
+        self.slab_x = 8 * (bz + 5)
+        self.corner = 6 * 8
         self.layers = bz + 4
         self.level1 = (peers[0] * bz // 2, peers[1] * bx // 2, LANES)
         self.level2 = (peers[0] * bz // 4, peers[1] * bx // 4, peers[2] * by // 4)
@@ -308,14 +386,15 @@
             at += 3 + count + (2 if count == 2 else 0)
         assert at <= LANES
         self.fine_rows = self.ex
-        self.edge = self.fine_rows + self.level1[0] * self.level1[1] // 8
+        self.window = (bz // 2 + 8, self.level1[1], LANES)
+        self.edge = self.fine_rows + self.window[0] * self.window[1] // 8
         self.wide2 = by // 4 + 4
         self.fold = LANES // self.wide2
         self.lines2 = -(-self.level2[0] // self.fold)
         self.share = self.lines2 * self.level2[1]
 
 
-def first_kernel(plan, both, r_ref, x_ref, pay, d_one, d_two, pairs, lines):
+def first_kernel(plan, both, r_ref, x_ref, pay_z, pay_x, pay_d, d_one, d_two, pairs, lines):
     p_ext, b_ext = both.at[0], both.at[1]
     bz, bx, by = plan.block
     ez, ex, ey = plan.ext
@@ -385,8 +464,7 @@
     table = as_table((fine >> 1) == coarse, 0.5)
     even, odd = right_dot(lines[0], table), right_dot(lines[1], table)
     lane = iota(even.shape, 1)
-    at = plan.slab
-    pay[at:at + plan.lat_at, :] = jnp.where(lane < LANES // 2, even, shifted(odd, LANES // 2))
+    main = jnp.where(lane < LANES // 2, even, shifted(odd, LANES // 2))
     own_lat = spill_lat = None
     row = iota((8, LANES), 0)
     for zc in range(coarse_z):
@@ -400,67 +478,52 @@
         if zc // 2 % 2:
             tile = pltpu.roll(tile, 4, 0)
         tile = only(row < 4, tile)
-        part = moved(tile, by // 2, 2, 4 * zc) + moved(tile, LANES - 2, 2, 4 * zc + 2)
+        slot = LANES // 2 + 4 * zc
+        part = moved(tile, by // 2, 2, slot) + moved(tile, LANES - 2, 2, slot + 2)
         spill_lat = part if spill_lat is None else spill_lat + part
-    at = plan.slab + plan.lat_at
-    pay[at:at + 8, :] = own_lat
-    pay[at + 8:at + 16, :] = spill_lat
-    inner = (iz == 1) | (iz == 2)
-
-    @pl.when(inner)
-    def _():
-        slab_emit(r_ref, x_ref, pay, 0, side(iz, 3)[0])
-
-    @pl.when(jnp.logical_not(inner))
-    def _():
-        rows_emit(r_ref, x_ref, pay, side(ix, 1)[0])
-
-
-def step_kernel(plan, r_in, x_in, ours, got, r_ref, x_ref, pay):
+    for pay, at in ((pay_z, plan.slab_z), (pay_x, plan.slab_x), (pay_d, plan.corner)):
+        pay[at:at + plan.lat_at, :] = main
+        pay[at + plan.lat_at:at + plan.coarse, :] = own_lat + spill_lat
+
+    up_z, _ = side(iz, 3)
+    up_x, _ = side(ix, 1)
+    thin_emit(r_ref, x_ref, pay_z, up_z)
+    rows_emit(r_ref, x_ref, pay_x, up_x)
+    lat = jnp.zeros((8, LANES), F32)
+    start = jnp.where(up_z, ez - 5, 0)
+    for j in range(5):
+        out = rows_out(r_ref[start + j], x_ref[start + j] if j == 2 else None, up_x)
+        pay_d[8 * j:8 * j + 8, :] = out[:, 0:LANES]
+        lat = lat + side_pack(out[:, LANES:], j)
+    pay_d[40:48, :] = lat
+
+
+def chip_kernel(plan, r_in, x_in, from_z, from_x, from_d, r_ref, x_ref, pay):
+    ez, ex, ey = plan.ext
     iz, _, _ = place("gz", plan.peers[0])
     ix, _, _ = place("gx", plan.peers[1])
-    up_z, inner = side(iz, 3)
+    up_z, near = side(iz, 3)
     up_x, _ = side(ix, 1)
-    for k in range(plan.ez):
+    for k in range(ez):
         r_ref[k] = r_in[k]
         x_ref[k] = x_in[k]
-
-    @pl.when(inner)
+    rows_add(r_ref, x_ref, from_x, up_x)
+
+    @pl.when(near)
     def _():
-        slab_add(r_ref, x_ref, got, 0, up_z)
-        rows_emit(r_ref, x_ref, pay, up_x)
-
-    @pl.when(jnp.logical_not(inner))
-    def _():
-        rows_add(r_ref, x_ref, got, up_x)
-        pay[0:plan.slab, :] = jnp.zeros((plan.slab, LANES), F32)
-
-    for j, ref in enumerate((ours, got)):
-        here = plan.slab + j * plan.coarse
-        pay[here:here + plan.coarse, :] = ref[plan.slab:plan.slab + plan.coarse, :]
-
-
-def core_kernel(plan, r_in, x_in, ours, got, r_ref, x_ref, pay):
-    iz, _, _ = place("gz", plan.peers[0])
-    ix, _, _ = place("gx", plan.peers[1])
-    _, inner = side(iz, 3)
-    up_x, _ = side(ix, 1)
-    for k in range(plan.ez):
-        r_ref[k] = r_in[k]
-        x_ref[k] = x_in[k]
-
-    @pl.when(inner)
-    def _():
-        rows_add(r_ref, x_ref, got, up_x)
-
-    slab_emit(r_ref, x_ref, pay, 0, side(iz, 1)[0])
-    for j, ref in enumerate((ours, got)):
-        here = plan.slab + 2 * j * plan.coarse
-        pay[here:here + 2 * plan.coarse, :] = ref[plan.slab:plan.slab + 2 * plan.coarse, :]
+        thin_add(r_ref, x_ref, from_z, up_z)
+        start = jnp.where(up_z, ez - 6, 1)
+        lat = from_d[40:48, :]
+        for j in range(5):
+            rows = from_d[8 * j:8 * j + 8, :]
+            rows = jnp.concatenate([rows, side_unpack(lat, j)], axis=1)
+            rows_in(r_ref, x_ref if j == 2 else None, start + j, rows, up_x)
+
+    slab_emit(r_ref, x_ref, pay, side(iz, 1)[0])
 
 
 def plane_kernel(plan, r_in, x_in, ours, theirs, r_ref, x_ref, r1_ref, x1_ref, pay, later, share,
-                 r_all, x_all, b1, d1, d2, pairs, lines):
+                 r_all, x_all, b1, d1, d2, r1, x1, pairs, lines):
     bz, bx, by = plan.block
     ez, ex, ey = plan.ext
     layers = plan.layers
@@ -471,7 +534,7 @@
     for k in range(ez):
         r_all[k] = r_in[k]
         x_all[k] = x_in[k]
-    slab_add(r_all, x_all, theirs, 0, up_z)
+    slab_add(r_all, x_all, theirs, up_z)
     for k in range(layers):
         r_ref[k] = r_all[k + 1]
     for k in range(bz):
@@ -503,17 +566,14 @@
         for i in range(plan.peers[1]):
             flip = iz ^ j
             other = ((flip ^ (flip >> 1)) & 1) == 1
-            along_z, along_x = flip >> 1, ix ^ i
-            met_z = ((iz == 1) | (iz == 2)) ^ other
-            chip = jnp.where(met_z, along_z + 2 * along_x, along_x + 2 * along_z)
+            chip = (flip >> 1) + 2 * (ix ^ i)
             at = pl.multiple_of(plan.slab + chip * plan.coarse, 8)
 
             def rows_at(offset, count):
                 here = pl.ds(pl.multiple_of(at + offset, 8), count)
                 return jnp.where(other, theirs[here, :], ours[here, :])
 
-            own_lat = rows_at(plan.lat_at, 8)
-            spill_lat = rows_at(plan.lat_at + 8, 8)
+            lat = rows_at(plan.lat_at, 8)
             for zp in range(plan.pairs):
                 own = rows_at(zp * rows, rows)
                 if zp % 2 == 0:
@@ -525,14 +585,14 @@
                     if not 0 <= k < nz1:
                         continue
 
-                    def wide(main, lat):
+                    def wide(main, slot):
                         return (
                             moved(main, part * half, half, 0)
-                            + moved(lat, 4 * zc, 2, half) + moved(lat, 4 * zc + 2, 2, LANES - 2)
+                            + moved(lat, slot, 2, half) + moved(lat, slot + 2, 2, LANES - 2)
                         )
 
-                    b1[k, i * rows:(i + 1) * rows, :] += wide(own, own_lat)
-                    v = wide(spill, spill_lat)
+                    b1[k, i * rows:(i + 1) * rows, :] += wide(own, 4 * zc)
+                    v = wide(spill, LANES // 2 + 4 * zc)
                     if i + 1 < plan.peers[1]:
                         at_row = (i + 1) * rows
                         b1[k, at_row:at_row + 8, :] += only(row < 2, v)
@@ -546,15 +606,15 @@
         d1[k] = b1[k] * first_scale
     for k in range(nz1):
         r = b1[k] - apply_at(d1, k, lateral1)
-        r1_ref[k] = r
+        r1[k] = r
         d2[k] = keep * (carry_coef * d1[k] + fresh_coef * r)
     for k in range(nz1):
-        r1_ref[k] = keep * (r1_ref[k] - apply_at(d2, k, lateral1))
-        x1_ref[k] = d1[k] + d2[k]
+        r1[k] = keep * (r1[k] - apply_at(d2, k, lateral1))
+        x1[k] = d1[k] + d2[k]
 
     nz2, nx2, _ = plan.level2
     for zc in range(nz2):
-        pairs[zc * nx1:(zc + 1) * nx1, :] = r1_ref[2 * zc] + r1_ref[2 * zc + 1]
+        pairs[zc * nx1:(zc + 1) * nx1, :] = r1[2 * zc] + r1[2 * zc + 1]
         part, at = divmod(zc, plan.lines2)
         lines[part, at * nx2:(at + 1) * nx2, :] = (
             pairs[pl.ds(zc * nx1, nx2, 2), :] + pairs[pl.ds(zc * nx1 + 1, nx2, 2), :]
@@ -571,9 +631,14 @@
         total = term if total is None else total + term
     share[...] = total
     pay[plan.edge:plan.edge + plan.share, :] = total
-
+    later[plan.edge:plan.edge + plan.share, :] = total
+
+    start = plan.first_layer(iz)
+    for k in range(plan.window[0]):
+        r1_ref[k] = r1[start + k]
+        x1_ref[k] = x1[start + k]
     per_tile = LANES // 16
-    for group in range(nz1 // per_tile):
+    for group in range(plan.window[0] // per_tile):
         tiles = []
         for which in range(2):
             total = jnp.zeros((nx1, LANES), F32)
@@ -652,12 +717,12 @@
     return x, (x if level == LEVELS - 1 else coarsest)
 
 
-def last_kernel(plan, r_in, x_in, r1_in, x1_in, ours, from_a, from_b, from_3, from_2, p_out, res_out, last_ref, *scratch):
+def last_kernel(plan, r_in, x_in, r1_in, x1_in, ours, from_a, from_b, from_c, p_out, res_out, last_ref, *scratch):
     shares, p_ref, res_ref, r, q1, e1, e0, d0, d1, r1, lines, wide, sem = scratch
     bz, bx, by = plan.block
     ez, ex, ey = plan.ext
-    nz1, nx1, _ = plan.level1
-    nz2, nx2, ny2 = plan.level2
+    nz1, nx1, _ = plan.window
+    nz2, nx2, _ = plan.level2
     layers, half = plan.layers, by // 2
     iz, z_low, z_high = place("gz", plan.peers[0])
     ix, x_low, x_high = place("gx", plan.peers[1])
@@ -665,8 +730,8 @@
 
     shares[0] = ours[...]
     shares[1] = from_a[plan.edge:plan.edge + plan.share, :]
-    shares[2] = from_2[...]
-    shares[3] = from_3[...]
+    shares[3] = from_b[plan.edge:plan.edge + plan.share, :]
+    shares[2] = from_c[...]
     own2 = half // 2
     source = []
     for part in range(plan.fold):
@@ -692,8 +757,10 @@
 
     fine = signed(iota((LANES, LANES), 1), half, LANES)
     coarse = iota((LANES, LANES), 0) - iy * own2
-    e2 = right_dot(lines[...], as_table((fine >> 1) == coarse))
-    for zc in range(nz2):
+    start = plan.first_layer(iz)
+    here = pl.ds(pl.multiple_of(start // 2 * nx2, 8), nz1 // 2 * nx2)
+    e2 = right_dot(lines[here, :], as_table((fine >> 1) == coarse))
+    for zc in range(nz1 // 2):
         v = e2[zc * nx2:(zc + 1) * nx2]
         for part in range(2):
             q1.at[2 * zc + part][pl.ds(0, nx2, 2), :] = v
@@ -732,8 +799,8 @@
     double = as_table((fine >> 1) == coarse)
     half_z, half_x = bz // 2, bx // 2
     for zc in range(half_z + 4):
-        start = pl.multiple_of(ix * half_x, 8)
-        v = e1[iz * half_z + zc, pl.ds(start, half_x + 16), :]
+        here = pl.ds(pl.multiple_of(ix * half_x, 8), half_x + 16)
+        v = e1[iz * half_z - start + zc, here, :]
         own, low, high = v[8:8 + half_x], v[0:8], v[8 + half_x:16 + half_x]
         at = zc * ex
         wide[pl.ds(at, half_x, 2), :] = own
@@ -836,48 +903,48 @@
     return lax.ppermute(values, axes, pairs)
 
 
-def swap_parts(values, partner):
-    cut = values.shape[0] * 5 // 64 * 8
-    parts = [swap(values[:cut], partner), swap(values[cut:], partner)]
-    return jnp.concatenate(parts, axis=0)
-
-
 def body_fast(divergence, pressure_prev):
     plan = Plan(divergence.shape, tuple(lax.axis_size(a) for a in ("gz", "gx", "gy")))
     ext, level1 = plan.ext, plan.level1
-    payload = [(plan.slab + n * plan.coarse, LANES) for n in (1, 2, 4)]
+    window, layers = plan.window, (plan.layers, plan.ex, plan.ey)
+    payload = [(n + plan.coarse, LANES) for n in (plan.slab_z, plan.slab_x, plan.corner)]
     both = jnp.stack([pressure_prev, divergence])
     both = jnp.pad(both, ((0, 0), (3, 3), (0, plan.ex - plan.block[1]), (0, plan.ey - plan.block[2])))
-    r, x, ours = run(
-        first_kernel, plan, [ext, ext, payload[0]],
+    r, x, pay_z, pay_x, pay_d = run(
+        first_kernel, plan, [ext, ext] + payload,
         [ext, ext, (2, 2 * plan.pairs * plan.ex, LANES), (2, plan.lat_at, plan.ey)],
         both,
     )
-    got = swap_parts(ours, lambda x, y, z: (x, y, z ^ 3) if z in (1, 2) else (x ^ 1, y, z))
-    r, x, ours = run(step_kernel, plan, [ext, ext, payload[1]], [], r, x, ours, got)
-    got = swap_parts(ours, lambda x, y, z: (x ^ 1, y, z) if z in (1, 2) else (x, y, z ^ 3))
-    r, x, ours = run(core_kernel, plan, [ext, ext, payload[2]], [], r, x, ours, got)
+    from_z = swap(pay_z, lambda x, y, z: (x, y, z ^ 3))
+    from_x = swap(pay_x, lambda x, y, z: (x ^ 1, y, z))
+    from_d = swap(pay_d, lambda x, y, z: (x ^ 1, y, z ^ 3))
+    r, x, slab = run(
+        chip_kernel, plan, [ext, ext, (plan.slab, LANES)], [], r, x, from_z, from_x, from_d
+    )
+    ours = jnp.concatenate([
+        slab, pay_z[plan.slab_z:], from_z[plan.slab_z:], from_x[plan.slab_x:], from_d[plan.corner:]
+    ], axis=0)
     got = swap(ours, lambda x, y, z: (x, y, z ^ 1))
     nz2, nx2, _ = plan.level2
-    layers = (plan.layers, plan.ex, plan.ey)
     share = (plan.share, LANES)
     r, x, r1, x1, now, later, ours = run(
         plane_kernel, plan,
-        [layers, plan.block, level1, level1, (plan.edge + plan.share, LANES), (plan.edge, LANES), share],
-        [ext, ext, level1, level1, level1, (nz2 * level1[1], LANES), (plan.fold,) + share],
+        [layers, plan.block, window, window, (plan.edge + plan.share, LANES),
+         (plan.edge + plan.share, LANES), share],
+        [ext, ext, level1, level1, level1, level1, level1, (nz2 * level1[1], LANES),
+         (plan.fold,) + share],
         r, x, ours, got,
     )
     from_a = swap(now, lambda x, y, z: (x, y ^ 1, z))
-    from_b = swap(later, lambda x, y, z: (x, y ^ 3, z) if y in (1, 2) else None)
-    from_3 = swap(ours, lambda x, y, z: (x, y ^ 3, z))
-    from_2 = swap(ours, lambda x, y, z: (x, y ^ 2, z))
+    from_b = swap(later, lambda x, y, z: (x, y ^ 3, z))
+    from_c = swap(ours, lambda x, y, z: (x, y ^ 2, z))
     return run(
         last_kernel, plan,
         [plan.block, plan.block, tuple(n >> 3 for n in plan.level2)],
-        [(4,) + share, plan.block, plan.block, layers, level1,
-         (level1[0] + 4, level1[1] + 16, LANES), ext, layers, level1, level1,
+        [(4,) + share, plan.block, plan.block, layers, window,
+         (window[0] + 4, window[1] + 16, LANES), ext, layers, window, window,
          (nz2 * nx2, LANES), (2 * plan.pairs * plan.ex, LANES)],
-        r, x, r1, x1, ours, from_a, from_b, from_3, from_2,
+        r, x, r1, x1, ours, from_a, from_b, from_c,
         out_specs=[ANY, ANY, VMEM], semaphores=3,
     )
 

time: 35.6 us -> 29.6 us (0.83)
  starting transfers between devices: 14.1 us -> 9.74 us
  waiting for transfers between devices: 11.6 us -> 10.4 us
  Pallas kernels: 7.91 us -> 7.48 us
    ppermute x9 -> x7, starting transfers between devices: 14.1 us -> 9.74 us  [swap(): return lax.ppermute(values, axes, pairs)]
    ppermute x9 -> x7, waiting for transfers between devices: 11.6 us -> 10.4 us  [swap(): return lax.ppermute(values, axes, pairs)]
    pallas_call x5 -> x4, Pallas kernels: 7.91 us -> 7.48 us  [run(): pl.pallas_call(functools.partial(kernel, plan), out_shape=[whole(s) for s...]
  transfers between devices with their start and end apart: 9 -> 7, of which waited for: 4 -> 3; matrix products, arithmetic and copies ran while one was open for 0% -> 0% of each run, Pallas kernels for 0% -> 0%
where the time goes in v6:
time: 29.6 us; the launch traced here: 29.4 us
  waiting for transfers between devices  10.4 us (35%)
  starting transfers between devices  9.74 us (33%)
  Pallas kernels  7.48 us (25%)
  other arithmetic  1.04 us (4%)
  between operations  0.7 us (2%)
    ppermute x7, waiting for transfers between devices, swap(): return lax.ppermute(values, axes, pairs)  10.4 us
    ppermute x7, starting transfers between devices, swap(): return lax.ppermute(values, axes, pairs)  9.74 us
    pallas_call x4, Pallas kernels, run(): pl.pallas_call(functools.partial(kernel, plan), out_shape=[whole(s) for s...  7.48 us
    another operation x1, other arithmetic, body_fast(): both = jnp.stack([pressure_prev, divergence])  1.04 us
  transfers between devices with their start and end apart: 7, of which 3 were waited for; matrix products, arithmetic and copies ran while one was open for 0% of the time, Pallas kernels for 0%

profile of v6, /device:TPU:0, one launch (start us, length us, event | category | flops | bytes accessed | tf_op | source)
XLA Modules:
  0.0 29.4 jit_solution(9874318242960552945)
XLA Ops:
  0.6 1.0 %select_maximum_fusion.both = f32[2,22,24,256]{3,2,1,0:T(8,128)S(1)} fusion(f32[1,16,16,128]{3,2,1,0:T(8,128)} %bitcast.2, f32[1,16,16,128]{3,2,1,0:T(8,128)} %bitcast.3), kind=kLoop, calls=%fused_computation.2 | loop fusion | flops 3784704 | bytes 1343488 | tf_op jit(solution)/shard_map/stack | solution.py:911
  1.7 1.4 %shard_map.49 = (f32[22,24,256]{2,1,0:T(8,128)S(1)}, f32[22,24,256]{2,1,0:T(8,128)S(1)}, f32[224,128]{1,0:T(8,128)S(1)}, f32[248,128]{1,0:T(8,128)S(1)}, f32[128,128]{1,0:T(8,128)S(1)}) custom-call(f32[2,22,24,256]{3,2,1,0:T(8,128)S(1)} %select_maximum_fusion.both), custom_call_target="tpu_custom_call" | custom-call | tf_op jit(solution)/shard_map/pallas_call | solution.py:885
  3.1 3.0 %collective-permute-start.1 = (f32[248,128]{1,0:T(8,128)S(1)}, f32[248,128]{1,0:T(8,128)S(1)}, u32[]{:S(2)}, u32[]{:S(2)}) collective-permute-start(f32[248,128]{1,0:T(8,128)S(1)} %get-tuple-element.21), channel_id=1, source_target_pairs={{0,16},{1,17},{2,18},{3,19},{4,20},{5,21},{6,22},{7,23},{8,24},{9,... | collective-permute-start | bytes 380936 | tf_op jit(solution)/shard_map/ppermute | solution.py:903
  6.1 0.6 %collective-permute-start = (f32[224,128]{1,0:T(8,128)S(1)}, f32[224,128]{1,0:T(8,128)S(1)}, u32[]{:S(2)}, u32[]{:S(2)}) collective-permute-start(f32[224,128]{1,0:T(8,128)S(1)} %get-tuple-element.20), channel_id=1, source_target_pairs={{0,3},{1,2},{2,1},{3,0},{4,7},{5,6},{6,5},{7,4},{8,11},{9,10},{10,... | collective-permute-start | bytes 344072 | tf_op jit(solution)/shard_map/ppermute | solution.py:903
  6.8 0.6 %collective-permute-start.2 = (f32[128,128]{1,0:T(8,128)S(1)}, f32[128,128]{1,0:T(8,128)S(1)}, u32[]{:S(2)}, u32[]{:S(2)}) collective-permute-start(f32[128,128]{1,0:T(8,128)S(1)} %get-tuple-element.22), channel_id=1, source_target_pairs={{0,19},{1,18},{2,17},{3,16},{4,23},{5,22},{6,21},{7,20},{8,27},{9,... | collective-permute-start | bytes 196616 | tf_op jit(solution)/shard_map/ppermute | solution.py:903
  7.4 4.4 %collective-permute-done.2.from_d = f32[128,128]{1,0:T(8,128)S(1)} collective-permute-done((f32[128,128]{1,0:T(8,128)S(1)}, f32[128,128]{1,0:T(8,128)S(1)}, u32[]{:S(2)}, u32[]{:S(2)}) %collective-permute-start.2) | collective-permute-done | bytes 65568 | tf_op jit(solution)/shard_map/ppermute | solution.py:903
  11.8 0.0 collective-permute-done.from_z
  11.8 0.0 collective-permute-done.1.from_x
  11.8 0.3 shard_map.50
  12.1 0.7 %collective-permute-start.3 = (f32[512,128]{1,0:T(8,128)S(1)}, f32[512,128]{1,0:T(8,128)S(1)}, u32[]{:S(2)}, u32[]{:S(2)}) collective-permute-start(f32[512,128]{1,0:T(8,128)S(1)} %slice_dynamic-update-slice_fusion.ours), channel_id=1, source_target_pairs={{0,1},{1,0},{2,3},{3,2},{4,5},{5,4},{6,7},{7,6},{8,9},{9,8},{10,11... | collective-permute-start | bytes 786440 | tf_op jit(solution)/shard_map/ppermute | solution.py:903
  12.8 1.2 %collective-permute-done.3.theirs = f32[512,128]{1,0:T(8,128)S(1)} collective-permute-done((f32[512,128]{1,0:T(8,128)S(1)}, f32[512,128]{1,0:T(8,128)S(1)}, u32[]{:S(2)}, u32[]{:S(2)}) %collective-permute-start.3) | collective-permute-done | bytes 262176 | tf_op jit(solution)/shard_map/ppermute | solution.py:903
  14.0 1.5 %shard_map.51 = (f32[20,24,256]{2,1,0:T(8,128)S(1)}, f32[16,16,128]{2,1,0:T(8,128)S(1)}, f32[16,16,128]{2,1,0:T(8,128)S(1)}, f32[16,16,128]{2,1,0:T(8,128)S(1)},...) custom-call(f32[22,24,256]{2,1,0:T(8,128)S(1)} %get-tuple-element.23.r_in, ...), custom_call_target="tpu_custom_call" | custom-call | tf_op jit(solution)/shard_map/pallas_call | solution.py:885
  15.5 2.2 %collective-permute-start.4 = (f32[104,128]{1,0:T(8,128)S(1)}, f32[104,128]{1,0:T(8,128)S(1)}, u32[]{:S(2)}, u32[]{:S(2)}) collective-permute-start(f32[104,128]{1,0:T(8,128)S(1)} %get-tuple-element.31), channel_id=1, source_target_pairs={{0,4},{1,5},{2,6},{3,7},{4,0},{5,1},{6,2},{7,3},{8,12},{9,13},{10,... | collective-permute-start | bytes 159752 | tf_op jit(solution)/shard_map/ppermute | solution.py:903
  17.6 2.5 %collective-permute-start.5 = (f32[104,128]{1,0:T(8,128)S(1)}, f32[104,128]{1,0:T(8,128)S(1)}, u32[]{:S(2)}, u32[]{:S(2)}) collective-permute-start(f32[104,128]{1,0:T(8,128)S(1)} %get-tuple-element.32), channel_id=1, source_target_pairs={{0,12},{1,13},{2,14},{3,15},{4,8},{5,9},{6,10},{7,11},{8,4},{9,5},... | collective-permute-start | bytes 159752 | tf_op jit(solution)/shard_map/ppermute | solution.py:903
  20.1 0.1 collective-permute-start.6
  20.2 4.9 %collective-permute-done.6.from_c = f32[48,128]{1,0:T(8,128)S(1)} collective-permute-done((f32[48,128]{1,0:T(8,128)S(1)}, f32[48,128]{1,0:T(8,128)S(1)}, u32[]{:S(2)}, u32[]{:S(2)}) %collective-permute-start.6) | collective-permute-done | bytes 24608 | tf_op jit(solution)/shard_map/ppermute | solution.py:903
  25.1 0.0 collective-permute-done.4.from_a
  25.1 0.0 collective-permute-done.5.from_b
  25.1 4.3 %shard_map.52 = (f32[16,16,128]{2,1,0:T(8,128)}, f32[16,16,128]{2,1,0:T(8,128)}, f32[2,1,16]{2,1,0:T(1,128)}) custom-call(f32[20,24,256]{2,1,0:T(8,128)S(1)} %get-tuple-element.26.r_in, f32[16,16,128]{2,1,0:T(8,128)S(1)} %get-tuple-element.27.x_in, f32[16,16,128]{2,1,0:T(8,128)S(1)} %get-tuple-element.28.r1_in, f32[16,16,128]{2,1,0:T(8,128)S(1)} %get-tuple-element.29.x1_in, ...), custom_call_target="tpu_custom_call" | custom-call | tf_op jit(solution)/shard_map/pallas_call | solution.py:885
  (5 shorter events, 0.0 us)
Async XLA Ops:
  3.1 8.7 %collective-permute-start.1 = (f32[248,128]{1,0:T(8,128)S(1)}, f32[248,128]{1,0:T(8,128)S(1)}, u32[]{:S(2)}, u32[]{:S(2)}) collective-permute-start(f32[248,128]{1,0:T(8,128)S(1)} %get-tuple-element.21), channel_id=1, source_target_pairs={{0,16},{1,17},{2,18},{3,19},{4,20},{5,21},{6,22},{7,23},{8,24},{9,... | collective-permute-start | bytes 380936 | tf_op jit(solution)/shard_map/ppermute | solution.py:903
  6.1 5.7 %collective-permute-start = (f32[224,128]{1,0:T(8,128)S(1)}, f32[224,128]{1,0:T(8,128)S(1)}, u32[]{:S(2)}, u32[]{:S(2)}) collective-permute-start(f32[224,128]{1,0:T(8,128)S(1)} %get-tuple-element.20), channel_id=1, source_target_pairs={{0,3},{1,2},{2,1},{3,0},{4,7},{5,6},{6,5},{7,4},{8,11},{9,10},{10,... | collective-permute-start | bytes 344072 | tf_op jit(solution)/shard_map/ppermute | solution.py:903
  6.8 5.0 %collective-permute-start.2 = (f32[128,128]{1,0:T(8,128)S(1)}, f32[128,128]{1,0:T(8,128)S(1)}, u32[]{:S(2)}, u32[]{:S(2)}) collective-permute-start(f32[128,128]{1,0:T(8,128)S(1)} %get-tuple-element.22), channel_id=1, source_target_pairs={{0,19},{1,18},{2,17},{3,16},{4,23},{5,22},{6,21},{7,20},{8,27},{9,... | collective-permute-start | bytes 196616 | tf_op jit(solution)/shard_map/ppermute | solution.py:903
  12.1 1.9 %collective-permute-start.3 = (f32[512,128]{1,0:T(8,128)S(1)}, f32[512,128]{1,0:T(8,128)S(1)}, u32[]{:S(2)}, u32[]{:S(2)}) collective-permute-start(f32[512,128]{1,0:T(8,128)S(1)} %slice_dynamic-update-slice_fusion.ours), channel_id=1, source_target_pairs={{0,1},{1,0},{2,3},{3,2},{4,5},{5,4},{6,7},{7,6},{8,9},{9,8},{10,11... | collective-permute-start | bytes 786440 | tf_op jit(solution)/shard_map/ppermute | solution.py:903
  15.5 9.6 %collective-permute-start.4 = (f32[104,128]{1,0:T(8,128)S(1)}, f32[104,128]{1,0:T(8,128)S(1)}, u32[]{:S(2)}, u32[]{:S(2)}) collective-permute-start(f32[104,128]{1,0:T(8,128)S(1)} %get-tuple-element.31), channel_id=1, source_target_pairs={{0,4},{1,5},{2,6},{3,7},{4,0},{5,1},{6,2},{7,3},{8,12},{9,13},{10,... | collective-permute-start | bytes 159752 | tf_op jit(solution)/shard_map/ppermute | solution.py:903
  17.6 7.5 %collective-permute-start.5 = (f32[104,128]{1,0:T(8,128)S(1)}, f32[104,128]{1,0:T(8,128)S(1)}, u32[]{:S(2)}, u32[]{:S(2)}) collective-permute-start(f32[104,128]{1,0:T(8,128)S(1)} %get-tuple-element.32), channel_id=1, source_target_pairs={{0,12},{1,13},{2,14},{3,15},{4,8},{5,9},{6,10},{7,11},{8,4},{9,5},... | collective-permute-start | bytes 159752 | tf_op jit(solution)/shard_map/ppermute | solution.py:903
  20.1 5.0 %collective-permute-start.6 = (f32[48,128]{1,0:T(8,128)S(1)}, f32[48,128]{1,0:T(8,128)S(1)}, u32[]{:S(2)}, u32[]{:S(2)}) collective-permute-start(f32[48,128]{1,0:T(8,128)S(1)} %get-tuple-element.30.ours), channel_id=1, source_target_pairs={{0,8},{1,9},{2,10},{3,11},{4,12},{5,13},{6,14},{7,15},{8,0},{9,1},... | collective-permute-start | bytes 73736 | tf_op jit(solution)/shard_map/ppermute | solution.py:903

commit v7 on v6

--- a/solution.py
+++ b/solution.py
@@ -1,4 +1,5 @@
 import functools
+import math
 
 import jax
 import jax.numpy as jnp
@@ -522,40 +523,11 @@
     slab_emit(r_ref, x_ref, pay, side(iz, 1)[0])
 
 
-def plane_kernel(plan, r_in, x_in, ours, theirs, r_ref, x_ref, r1_ref, x1_ref, pay, later, share,
-                 r_all, x_all, b1, d1, d2, r1, x1, pairs, lines):
+def plane_kernel(plan, ours, theirs, r1_ref, x1_ref, share, b1, d1, d2, r1, x1, pairs, lines):
     bz, bx, by = plan.block
-    ez, ex, ey = plan.ext
-    layers = plan.layers
     iz, _, _ = place("gz", plan.peers[0])
     ix, _, _ = place("gx", plan.peers[1])
     iy, y_low, y_high = place("gy", plan.peers[2])
-    up_z, _ = side(iz, 1)
-    for k in range(ez):
-        r_all[k] = r_in[k]
-        x_all[k] = x_in[k]
-    slab_add(r_all, x_all, theirs, up_z)
-    for k in range(layers):
-        r_ref[k] = r_all[k + 1]
-    for k in range(bz):
-        x_ref[k] = x_all[k + 3, 0:bx, 0:by]
-
-    up, _ = side(iy, 1)
-    up_inner, _ = side(iy, 3)
-    high, low = jnp.zeros((ex, LANES), F32), jnp.zeros((ex, LANES), F32)
-    for k in range(layers):
-        slot, inner = plan.slots[k], plan.inner[k]
-        count = 3 + inner
-        v, spill = r_all[k + 1, :, 0:by], r_all[k + 1, :, by:ey]
-        high = high + moved(jnp.where(lanes_of(v, 0, 3), spill, v), LANES - inner, count, slot)
-        mixed = jnp.where(lanes_of(v, 0, 2), v, spill)
-        low = low + moved(mixed, LANES - 3, count, slot)
-        if inner == 2:
-            spill = x_all[k + 1, :, by:ey]
-            high = high + moved(spill, 0, 2, slot + count)
-            low = low + moved(spill, LANES - 2, 2, slot + count)
-    pay[0:ex, :] = jnp.where(up, high, low)
-    later[0:ex, :] = jnp.where(up_inner, high, low)
 
     nz1, nx1, _ = plan.level1
     rows, half = plan.rows, by // 2
@@ -630,13 +602,47 @@
         term = right_dot(lines[part], as_table(near & ((fine >> 1) == coarse), 0.5))
         total = term if total is None else total + term
     share[...] = total
-    pay[plan.edge:plan.edge + plan.share, :] = total
-    later[plan.edge:plan.edge + plan.share, :] = total
 
     start = plan.first_layer(iz)
     for k in range(plan.window[0]):
         r1_ref[k] = r1[start + k]
         x1_ref[k] = x1[start + k]
+
+
+def border_kernel(plan, r_in, x_in, theirs, r1_ref, x1_ref, r_ref, x_ref, pay, later, r_all, x_all):
+    bz, bx, by = plan.block
+    ez, ex, ey = plan.ext
+    layers, half = plan.layers, by // 2
+    iz, _, _ = place("gz", plan.peers[0])
+    iy, _, _ = place("gy", plan.peers[2])
+    nx1 = plan.window[1]
+    up_z, _ = side(iz, 1)
+    for k in range(ez):
+        r_all[k] = r_in[k]
+        x_all[k] = x_in[k]
+    slab_add(r_all, x_all, theirs, up_z)
+    for k in range(layers):
+        r_ref[k] = r_all[k + 1]
+    for k in range(bz):
+        x_ref[k] = x_all[k + 3, 0:bx, 0:by]
+
+    up, _ = side(iy, 1)
+    up_inner, _ = side(iy, 3)
+    high, low = jnp.zeros((ex, LANES), F32), jnp.zeros((ex, LANES), F32)
+    for k in range(layers):
+        slot, inner = plan.slots[k], plan.inner[k]
+        count = 3 + inner
+        v, spill = r_all[k + 1, :, 0:by], r_all[k + 1, :, by:ey]
+        high = high + moved(jnp.where(lanes_of(v, 0, 3), spill, v), LANES - inner, count, slot)
+        mixed = jnp.where(lanes_of(v, 0, 2), v, spill)
+        low = low + moved(mixed, LANES - 3, count, slot)
+        if inner == 2:
+            spill = x_all[k + 1, :, by:ey]
+            high = high + moved(spill, 0, 2, slot + count)
+            low = low + moved(spill, LANES - 2, 2, slot + count)
+    pay[0:ex, :] = jnp.where(up, high, low)
+    later[0:ex, :] = jnp.where(up_inner, high, low)
+
     per_tile = LANES // 16
     for group in range(plan.window[0] // per_tile):
         tiles = []
@@ -717,7 +723,7 @@
     return x, (x if level == LEVELS - 1 else coarsest)
 
 
-def last_kernel(plan, r_in, x_in, r1_in, x1_in, ours, from_a, from_b, from_c, p_out, res_out, last_ref, *scratch):
+def last_kernel(plan, r_in, x_in, r1_in, x1_in, ours, from_a, from_b, p_out, res_out, last_ref, *scratch):
     shares, p_ref, res_ref, r, q1, e1, e0, d0, d1, r1, lines, wide, sem = scratch
     bz, bx, by = plan.block
     ez, ex, ey = plan.ext
@@ -728,10 +734,10 @@
     ix, x_low, x_high = place("gx", plan.peers[1])
     iy, y_low, y_high = place("gy", plan.peers[2])
 
-    shares[0] = ours[...]
-    shares[1] = from_a[plan.edge:plan.edge + plan.share, :]
-    shares[3] = from_b[plan.edge:plan.edge + plan.share, :]
-    shares[2] = from_c[...]
+    for j, ref in enumerate((ours, from_a)):
+        for k in range(2):
+            here = plan.edge + k * plan.share
+            shares[j + 2 * k] = ref[here:here + plan.share, :]
     own2 = half // 2
     source = []
     for part in range(plan.fold):
@@ -882,6 +888,7 @@
     scratch = [pltpu.VMEM(s, F32) for s in scratch]
     if semaphores:
         scratch.append(pltpu.SemaphoreType.DMA((semaphores,)))
+    moved_bytes = 4 * sum(math.prod(s) for s in [v.shape for v in operands] + list(outs))
     return pl.pallas_call(
         functools.partial(kernel, plan),
         out_shape=[whole(s) for s in outs],
@@ -889,6 +896,9 @@
         out_specs=out_specs or [VMEM] * len(outs),
         scratch_shapes=scratch,
         compiler_params=pltpu.CompilerParams(vmem_limit_bytes=VMEM_BYTES),
+        cost_estimate=pl.CostEstimate(
+            flops=8 * moved_bytes, bytes_accessed=moved_bytes, transcendentals=0
+        ),
     )(*operands)
 
 
@@ -927,24 +937,26 @@
     got = swap(ours, lambda x, y, z: (x, y, z ^ 1))
     nz2, nx2, _ = plan.level2
     share = (plan.share, LANES)
-    r, x, r1, x1, now, later, ours = run(
-        plane_kernel, plan,
-        [layers, plan.block, window, window, (plan.edge + plan.share, LANES),
-         (plan.edge + plan.share, LANES), share],
-        [ext, ext, level1, level1, level1, level1, level1, (nz2 * level1[1], LANES),
-         (plan.fold,) + share],
-        r, x, ours, got,
+    r1, x1, ours = run(
+        plane_kernel, plan, [window, window, share],
+        [level1, level1, level1, level1, level1, (nz2 * level1[1], LANES), (plan.fold,) + share],
+        ours, got,
     )
-    from_a = swap(now, lambda x, y, z: (x, y ^ 1, z))
-    from_b = swap(later, lambda x, y, z: (x, y ^ 3, z))
-    from_c = swap(ours, lambda x, y, z: (x, y ^ 2, z))
+    there = swap(ours, lambda x, y, z: (x, y ^ 2, z))
+    edge = (plan.edge, LANES)
+    r, x, now, later = run(
+        border_kernel, plan, [layers, plan.block, edge, edge], [ext, ext], r, x, got, r1, x1
+    )
+    ours = jnp.concatenate([now, ours, there], axis=0)
+    from_a = swap(ours, lambda x, y, z: (x, y ^ 1, z))
+    from_b = swap(later, lambda x, y, z: (x, y ^ 3, z) if y in (1, 2) else None)
     return run(
         last_kernel, plan,
         [plan.block, plan.block, tuple(n >> 3 for n in plan.level2)],
         [(4,) + share, plan.block, plan.block, layers, window,
          (window[0] + 4, window[1] + 16, LANES), ext, layers, window, window,
          (nz2 * nx2, LANES), (2 * plan.pairs * plan.ex, LANES)],
-        r, x, r1, x1, ours, from_a, from_b, from_c,
+        r, x, r1, x1, ours, from_a, from_b,
         out_specs=[ANY, ANY, VMEM], semaphores=3,
     )
 

time: 29.6 us -> 31.3 us (1.057)
  the two profiles are of different devices: /device:TPU:0 before, /device:TPU:20 now
where the time goes in v7:
time: 31.3 us; the launch traced here: 31.2 us
  waiting for transfers between devices  14.1 us (45%)
  Pallas kernels  7.69 us (25%)
  starting transfers between devices  7.57 us (24%)
  other arithmetic  1.04 us (3%)
  between operations  0.72 us (2%)
    ppermute x7, waiting for transfers between devices, swap(): return lax.ppermute(values, axes, pairs)  14.1 us
    pallas_call x5, Pallas kernels, run(): pl.pallas_call(functools.partial(kernel, plan), out_shape=[whole(s) for s...  7.69 us
    ppermute x7, starting transfers between devices, swap(): return lax.ppermute(values, axes, pairs)  7.57 us
    another operation x1, other arithmetic, body_fast(): both = jnp.stack([pressure_prev, divergence])  1.04 us
  transfers between devices with their start and end apart: 7, of which 4 were waited for; matrix products, arithmetic and copies ran while one was open for 0% of the time, Pallas kernels for 2%

profile of v7, /device:TPU:20, one launch (start us, length us, event | category | flops | bytes accessed | tf_op | source)
XLA Modules:
  0.0 31.2 jit_solution(9498521399793908555)
XLA Ops:
  0.6 1.0 %select_maximum_fusion.both = f32[2,22,24,256]{3,2,1,0:T(8,128)S(1)} fusion(f32[1,16,16,128]{3,2,1,0:T(8,128)} %bitcast.2, f32[1,16,16,128]{3,2,1,0:T(8,128)} %bitcast.3), kind=kLoop, calls=%fused_computation.2 | loop fusion | flops 3784704 | bytes 1343488 | tf_op jit(solution)/shard_map/stack | solution.py:921
  1.7 1.4 %shard_map.49 = (f32[22,24,256]{2,1,0:T(8,128)S(1)}, f32[22,24,256]{2,1,0:T(8,128)S(1)}, f32[224,128]{1,0:T(8,128)S(1)}, f32[248,128]{1,0:T(8,128)S(1)}, f32[128,128]{1,0:T(8,128)S(1)}) custom-call(f32[2,22,24,256]{3,2,1,0:T(8,128)S(1)} %select_maximum_fusion.both), custom_call_target="tpu_custom_call" | custom-call | flops 19759104 | bytes 2469888 | tf_op jit(solution)/shard_map/pallas_call | solution.py:892
  3.1 0.6 %collective-permute-start.1 = (f32[248,128]{1,0:T(8,128)S(1)}, f32[248,128]{1,0:T(8,128)S(1)}, u32[]{:S(2)}, u32[]{:S(2)}) collective-permute-start(f32[248,128]{1,0:T(8,128)S(1)} %get-tuple-element.21), channel_id=1, source_target_pairs={{0,16},{1,17},{2,18},{3,19},{4,20},{5,21},{6,22},{7,23},{8,24},{9,... | collective-permute-start | bytes 380936 | tf_op jit(solution)/shard_map/ppermute | solution.py:913
  3.7 0.6 %collective-permute-start = (f32[224,128]{1,0:T(8,128)S(1)}, f32[224,128]{1,0:T(8,128)S(1)}, u32[]{:S(2)}, u32[]{:S(2)}) collective-permute-start(f32[224,128]{1,0:T(8,128)S(1)} %get-tuple-element.20), channel_id=1, source_target_pairs={{0,3},{1,2},{2,1},{3,0},{4,7},{5,6},{6,5},{7,4},{8,11},{9,10},{10,... | collective-permute-start | bytes 344072 | tf_op jit(solution)/shard_map/ppermute | solution.py:913
  4.3 2.1 %collective-permute-start.2 = (f32[128,128]{1,0:T(8,128)S(1)}, f32[128,128]{1,0:T(8,128)S(1)}, u32[]{:S(2)}, u32[]{:S(2)}) collective-permute-start(f32[128,128]{1,0:T(8,128)S(1)} %get-tuple-element.22), channel_id=1, source_target_pairs={{0,19},{1,18},{2,17},{3,16},{4,23},{5,22},{6,21},{7,20},{8,27},{9,... | collective-permute-start | bytes 196616 | tf_op jit(solution)/shard_map/ppermute | solution.py:913
  6.4 5.1 %collective-permute-done.2.from_d = f32[128,128]{1,0:T(8,128)S(1)} collective-permute-done((f32[128,128]{1,0:T(8,128)S(1)}, f32[128,128]{1,0:T(8,128)S(1)}, u32[]{:S(2)}, u32[]{:S(2)}) %collective-permute-start.2) | collective-permute-done | bytes 65568 | tf_op jit(solution)/shard_map/ppermute | solution.py:913
  11.4 0.0 collective-permute-done.from_z
  11.4 0.0 collective-permute-done.1.from_x
  11.4 0.3 shard_map.50
  11.8 0.3 collective-permute-start.3
  12.1 1.3 %collective-permute-done.3.theirs = f32[512,128]{1,0:T(8,128)S(1)} collective-permute-done((f32[512,128]{1,0:T(8,128)S(1)}, f32[512,128]{1,0:T(8,128)S(1)}, u32[]{:S(2)}, u32[]{:S(2)}) %collective-permute-start.3) | collective-permute-done | bytes 262176 | tf_op jit(solution)/shard_map/ppermute | solution.py:913
  13.4 1.1 %shard_map.51 = (f32[16,16,128]{2,1,0:T(8,128)S(1)}, f32[16,16,128]{2,1,0:T(8,128)S(1)}, f32[48,128]{1,0:T(8,128)S(1)}) custom-call(f32[512,128]{1,0:T(8,128)S(1)} %slice_dynamic-update-slice_fusion.ours, f32[512,128]{1,0:T(8,128)S(1)} %collective-permute-done.3.theirs), custom_call_target="tpu_custom_call" | custom-call | flops 6488064 | bytes 811008 | tf_op jit(solution)/shard_map/pallas_call | solution.py:892
  14.5 0.4 %collective-permute-start.4 = (f32[48,128]{1,0:T(8,128)S(1)}, f32[48,128]{1,0:T(8,128)S(1)}, u32[]{:S(2)}, u32[]{:S(2)}) collective-permute-start(f32[48,128]{1,0:T(8,128)S(1)} %get-tuple-element.31), channel_id=1, source_target_pairs={{0,8},{1,9},{2,10},{3,11},{4,12},{5,13},{6,14},{7,15},{8,0},{9,1},... | collective-permute-start | bytes 73736 | tf_op jit(solution)/shard_map/ppermute | solution.py:913
  14.9 0.5 %shard_map.52 = (f32[20,24,256]{2,1,0:T(8,128)S(1)}, f32[16,16,128]{2,1,0:T(8,128)S(1)}, f32[56,128]{1,0:T(8,128)S(1)}, f32[56,128]{1,0:T(8,128)S(1)}) custom-call(f32[22,24,256]{2,1,0:T(8,128)S(1)} %get-tuple-element.23.r_in, f32[22,24,256]{2,1,0:T(8,128)S(1)} %get-tuple-element.24.x_in, f32[512,128]{1,0:T(8,128)S(1)} %collective-permute-done.3.theirs, ...), custom_call_target="tpu_custom_call" | custom-call | flops 18284544 | bytes 2285568 | tf_op jit(solution)/shard_map/pallas_call | solution.py:892
  15.5 3.8 %collective-permute-done.4 = f32[48,128]{1,0:T(8,128)S(1)} collective-permute-done((f32[48,128]{1,0:T(8,128)S(1)}, f32[48,128]{1,0:T(8,128)S(1)}, u32[]{:S(2)}, u32[]{:S(2)}) %collective-permute-start.4) | collective-permute-done | bytes 24608 | tf_op jit(solution)/shard_map/ppermute | solution.py:913
  19.3 1.7 %collective-permute-start.5 = (f32[152,128]{1,0:T(8,128)S(1)}, f32[152,128]{1,0:T(8,128)S(1)}, u32[]{:S(2)}, u32[]{:S(2)}) collective-permute-start(f32[152,128]{1,0:T(8,128)S(1)} %constant_dynamic-update-slice_fusion.1.ours), channel_id=1, source_target_pairs={{0,4},{1,5},{2,6},{3,7},{4,0},{5,1},{6,2},{7,3},{8,12},{9,13},{10,... | collective-permute-start | bytes 233480 | tf_op jit(solution)/shard_map/ppermute | solution.py:913
  21.0 1.9 %collective-permute-start.6 = (f32[56,128]{1,0:T(8,128)S(1)}, f32[56,128]{1,0:T(8,128)S(1)}, u32[]{:S(2)}, u32[]{:S(2)}) collective-permute-start(f32[56,128]{1,0:T(8,128)S(1)} %get-tuple-element.32), channel_id=1, source_target_pairs={{4,8},{5,9},{6,10},{7,11},{8,4},{9,5},{10,6},{11,7},{20,24},{21,25... | collective-permute-start | bytes 86024 | tf_op jit(solution)/shard_map/ppermute | solution.py:913
  23.0 3.8 %collective-permute-done.6.from_b = f32[56,128]{1,0:T(8,128)S(1)} collective-permute-done((f32[56,128]{1,0:T(8,128)S(1)}, f32[56,128]{1,0:T(8,128)S(1)}, u32[]{:S(2)}, u32[]{:S(2)}) %collective-permute-start.6) | collective-permute-done | bytes 28704 | tf_op jit(solution)/shard_map/ppermute | solution.py:913
  26.8 0.0 collective-permute-done.5.from_a
  26.8 4.4 %shard_map.53 = (f32[16,16,128]{2,1,0:T(8,128)}, f32[16,16,128]{2,1,0:T(8,128)}, f32[2,1,16]{2,1,0:T(1,128)}) custom-call(f32[20,24,256]{2,1,0:T(8,128)S(1)} %get-tuple-element.28.r_in, f32[16,16,128]{2,1,0:T(8,128)S(1)} %get-tuple-element.29.x_in, f32[16,16,128]{2,1,0:T(8,128)S(1)} %get-tuple-element.26.r1_ref.r1_in, ...), custom_call_target="tpu_custom_call" | custom-call | flops 10650624 | bytes 1331328 | tf_op jit(solution)/shard_map/pallas_call | solution.py:892
  (8 shorter events, 0.0 us)
Async XLA Ops:
  3.1 8.3 %collective-permute-start.1 = (f32[248,128]{1,0:T(8,128)S(1)}, f32[248,128]{1,0:T(8,128)S(1)}, u32[]{:S(2)}, u32[]{:S(2)}) collective-permute-start(f32[248,128]{1,0:T(8,128)S(1)} %get-tuple-element.21), channel_id=1, source_target_pairs={{0,16},{1,17},{2,18},{3,19},{4,20},{5,21},{6,22},{7,23},{8,24},{9,... | collective-permute-start | bytes 380936 | tf_op jit(solution)/shard_map/ppermute | solution.py:913
  3.7 7.8 %collective-permute-start = (f32[224,128]{1,0:T(8,128)S(1)}, f32[224,128]{1,0:T(8,128)S(1)}, u32[]{:S(2)}, u32[]{:S(2)}) collective-permute-start(f32[224,128]{1,0:T(8,128)S(1)} %get-tuple-element.20), channel_id=1, source_target_pairs={{0,3},{1,2},{2,1},{3,0},{4,7},{5,6},{6,5},{7,4},{8,11},{9,10},{10,... | collective-permute-start | bytes 344072 | tf_op jit(solution)/shard_map/ppermute | solution.py:913
  4.3 7.1 %collective-permute-start.2 = (f32[128,128]{1,0:T(8,128)S(1)}, f32[128,128]{1,0:T(8,128)S(1)}, u32[]{:S(2)}, u32[]{:S(2)}) collective-permute-start(f32[128,128]{1,0:T(8,128)S(1)} %get-tuple-element.22), channel_id=1, source_target_pairs={{0,19},{1,18},{2,17},{3,16},{4,23},{5,22},{6,21},{7,20},{8,27},{9,... | collective-permute-start | bytes 196616 | tf_op jit(solution)/shard_map/ppermute | solution.py:913
  11.8 1.6 %collective-permute-start.3 = (f32[512,128]{1,0:T(8,128)S(1)}, f32[512,128]{1,0:T(8,128)S(1)}, u32[]{:S(2)}, u32[]{:S(2)}) collective-permute-start(f32[512,128]{1,0:T(8,128)S(1)} %slice_dynamic-update-slice_fusion.ours), channel_id=1, source_target_pairs={{0,1},{1,0},{2,3},{3,2},{4,5},{5,4},{6,7},{7,6},{8,9},{9,8},{10,11... | collective-permute-start | bytes 786440 | tf_op jit(solution)/shard_map/ppermute | solution.py:913
  14.5 4.8 %collective-permute-start.4 = (f32[48,128]{1,0:T(8,128)S(1)}, f32[48,128]{1,0:T(8,128)S(1)}, u32[]{:S(2)}, u32[]{:S(2)}) collective-permute-start(f32[48,128]{1,0:T(8,128)S(1)} %get-tuple-element.31), channel_id=1, source_target_pairs={{0,8},{1,9},{2,10},{3,11},{4,12},{5,13},{6,14},{7,15},{8,0},{9,1},... | collective-permute-start | bytes 73736 | tf_op jit(solution)/shard_map/ppermute | solution.py:913
  19.3 7.5 %collective-permute-start.5 = (f32[152,128]{1,0:T(8,128)S(1)}, f32[152,128]{1,0:T(8,128)S(1)}, u32[]{:S(2)}, u32[]{:S(2)}) collective-permute-start(f32[152,128]{1,0:T(8,128)S(1)} %constant_dynamic-update-slice_fusion.1.ours), channel_id=1, source_target_pairs={{0,4},{1,5},{2,6},{3,7},{4,0},{5,1},{6,2},{7,3},{8,12},{9,13},{10,... | collective-permute-start | bytes 233480 | tf_op jit(solution)/shard_map/ppermute | solution.py:913
  21.0 5.8 %collective-permute-start.6 = (f32[56,128]{1,0:T(8,128)S(1)}, f32[56,128]{1,0:T(8,128)S(1)}, u32[]{:S(2)}, u32[]{:S(2)}) collective-permute-start(f32[56,128]{1,0:T(8,128)S(1)} %get-tuple-element.32), channel_id=1, source_target_pairs={{4,8},{5,9},{6,10},{7,11},{8,4},{9,5},{10,6},{11,7},{20,24},{21,25... | collective-permute-start | bytes 86024 | tf_op jit(solution)/shard_map/ppermute | solution.py:913

commit v8 on v6

--- a/solution.py
+++ b/solution.py
@@ -124,23 +124,15 @@
     return jnp.where(index >= (size + extent) // 2, index - extent, index)
 
 
-def split(values):
+def right_dot(values, table):
+    rows = values.shape[0]
     terms = []
     for _ in range(3):
         term = values.astype(jnp.bfloat16)
         terms.append(term)
         values = values - term.astype(F32)
-    return terms
-
-
-def right_dot(values, table):
-    parts = [jnp.dot(t, table, preferred_element_type=F32) for t in split(values)]
-    return parts[0] + parts[1] + parts[2]
-
-
-def left_dot(table, values):
-    parts = [jnp.dot(table, t, preferred_element_type=F32) for t in split(values)]
-    return parts[0] + parts[1] + parts[2]
+    out = jnp.dot(jnp.concatenate(terms, axis=0), table, preferred_element_type=F32)
+    return out[0:rows] + out[rows:2 * rows] + out[2 * rows:3 * rows]
 
 
 def as_table(keep, value=1.0):
@@ -207,12 +199,18 @@
     return shifted(only(lanes_of(v, first, count), v), to - first)
 
 
+def landed(v, first, count, to):
+    to = to % LANES
+    v = shifted(v, to - first)
+    return only(lanes_of(v, to, count), v)
+
+
 def side_pack(tile, slot):
     return moved(tile, LANES - 3, 6, 6 * slot)
 
 
 def side_unpack(packed, slot):
-    return moved(packed, 6 * slot, 6, LANES - 3)
+    return landed(packed, 6 * slot, 6, LANES - 3)
 
 
 def slab_layers(r_ref, x_ref, up, low, high):
@@ -456,13 +454,15 @@
             odd = pairs.at[tile][pl.ds(base + 1, ex // 2, 2), :]
             sums = even + odd
             at = zc // 2 * rows
-            lines[zc % 2, at:at + rows, here] = sums[0:rows]
-            at = plan.pairs * rows + zc // 2 * 4
-            lines[zc % 2, at:at + 4, here] = sums[rows:rows + 4]
+            at += zc % 2 * plan.lat_at
+            lines[at:at + rows, here] = sums[0:rows]
+            at = plan.pairs * rows + zc // 2 * 4 + zc % 2 * plan.lat_at
+            lines[at:at + 4, here] = sums[rows:rows + 4]
     fine = signed(iota((ey, LANES), 0), by, ey)
     coarse = signed(iota((ey, LANES), 1), by // 2, LANES)
     table = as_table((fine >> 1) == coarse, 0.5)
-    even, odd = right_dot(lines[0], table), right_dot(lines[1], table)
+    out = right_dot(lines[...], table)
+    even, odd = out[0:plan.lat_at], out[plan.lat_at:]
     lane = iota(even.shape, 1)
     main = jnp.where(lane < LANES // 2, even, shifted(odd, LANES // 2))
     own_lat = spill_lat = None
@@ -587,8 +587,8 @@
 
                     def wide(main, slot):
                         return (
-                            moved(main, part * half, half, 0)
-                            + moved(lat, slot, 2, half) + moved(lat, slot + 2, 2, LANES - 2)
+                            landed(main, part * half, half, 0)
+                            + landed(lat, slot, 2, half) + landed(lat, slot + 2, 2, LANES - 2)
                         )
 
                     b1[k, i * rows:(i + 1) * rows, :] += wide(own, 4 * zc)
@@ -616,19 +616,20 @@
     for zc in range(nz2):
         pairs[zc * nx1:(zc + 1) * nx1, :] = r1[2 * zc] + r1[2 * zc + 1]
         part, at = divmod(zc, plan.lines2)
-        lines[part, at * nx2:(at + 1) * nx2, :] = (
+        lines[at * nx2:(at + 1) * nx2, part * LANES:(part + 1) * LANES] = (
             pairs[pl.ds(zc * nx1, nx2, 2), :] + pairs[pl.ds(zc * nx1 + 1, nx2, 2), :]
         )
-    fine = signed(iota((LANES, LANES), 0), half, LANES)
-    total = None
+    shape = (plan.fold * LANES, LANES)
+    fine, coarse = iota(shape, 0), iota(shape, 1)
+    part, fine = fine // LANES, signed(fine % LANES, half, LANES)
+    coarse = coarse - part * plan.wide2 - 2
+    near = (coarse >= -2) & (coarse < plan.wide2 - 2)
     for part in range(plan.fold):
         count = min(plan.lines2, nz2 - part * plan.lines2) * nx2
         if count < plan.share:
-            lines[part, count:, :] = jnp.zeros((plan.share - count, LANES), F32)
-        coarse = iota((LANES, LANES), 1) - part * plan.wide2 - 2
-        near = (coarse >= -2) & (coarse < plan.wide2 - 2)
-        term = right_dot(lines[part], as_table(near & ((fine >> 1) == coarse), 0.5))
-        total = term if total is None else total + term
+            here = slice(part * LANES, (part + 1) * LANES)
+            lines[count:, here] = jnp.zeros((plan.share - count, LANES), F32)
+    total = right_dot(lines[...], as_table(near & ((fine >> 1) == coarse), 0.5))
     share[...] = total
     pay[plan.edge:plan.edge + plan.share, :] = total
     later[plan.edge:plan.edge + plan.share, :] = total
@@ -775,12 +776,12 @@
             k = group * per_tile + j
             s = 16 * j
             r1[k] = (
-                r1_in[k] + moved(high, s, 7, half - 4) + moved(low, s, 7, LANES - 3)
+                r1_in[k] + landed(high, s, 7, half - 4) + landed(low, s, 7, LANES - 3)
                 - apply_at(q1, k, lateral1)
             )
             e1[k + 2, 8:8 + nx1, :] = (
                 x1_in[k] + q1[k]
-                + moved(high, s + 7, 5, half - 3) + moved(low, s + 7, 5, LANES - 2)
+                + landed(high, s + 7, 5, half - 3) + landed(low, s + 7, 5, LANES - 2)
             )
     for k in range(nz1):
         d1[k] = keep * (r1[k] * first_scale)
@@ -811,11 +812,11 @@
                 wide[row:row + 1, :] = high[j:j + 1]
                 row = at + ex - 4 + 2 * j + twin
                 wide[row:row + 1, :] = low[6 + j:7 + j]
+    out = right_dot(wide[...], double)
     for zc in range(half_z + 4):
-        v = right_dot(wide[zc * ex:(zc + 1) * ex, :], double)
         for k in (2 * zc - 1, 2 * zc):
             if 0 <= k < ez:
-                e0[k] = v
+                e0[k] = out[zc * ex:(zc + 1) * ex]
     flat = wrapped_mask((ex, ey), {0: bx, 1: by}, (x_low, y_low), (x_high, y_high))
     below = jnp.where(z_low, 1.0, 0.0).astype(F32)
     above = jnp.where(z_high, 1.0, 0.0).astype(F32)
@@ -832,10 +833,10 @@
     for k in range(layers):
         s, inner = plan.slots[k], plan.inner[k]
         v = r_in[k] - apply_at(e0, k + 1)
-        own = v[:, 0:by] + moved(high, s, 3, LANES - 3) + moved(low, s + inner, 3, 0)
+        own = v[:, 0:by] + landed(high, s, 3, LANES - 3) + landed(low, s + inner, 3, 0)
         spill = v[:, by:ey]
         if inner:
-            spill = spill + moved(high, s + 3, inner, 0) + moved(low, s, inner, LANES - inner)
+            spill = spill + landed(high, s + 3, inner, 0) + landed(low, s, inner, LANES - inner)
         r[k, :, 0:by] = own
         r[k, :, by:ey] = spill
         d0[k] = masked(k + 1, r[k] * first_scale)
@@ -843,7 +844,7 @@
             s = s + 3 + inner
             p_ref[k - 2] = (
                 x_in[k - 2] + e0[k + 1, 0:bx, 0:by]
-                + (moved(high, s, 2, LANES - 2) + moved(low, s, 2, 0))[0:bx]
+                + (landed(high, s, 2, LANES - 2) + landed(low, s, 2, 0))[0:bx]
             )
     for k in range(1, layers - 1):
         v = r[k] - apply_at(d0, k)
@@ -912,7 +913,7 @@
     both = jnp.pad(both, ((0, 0), (3, 3), (0, plan.ex - plan.block[1]), (0, plan.ey - plan.block[2])))
     r, x, pay_z, pay_x, pay_d = run(
         first_kernel, plan, [ext, ext] + payload,
-        [ext, ext, (2, 2 * plan.pairs * plan.ex, LANES), (2, plan.lat_at, plan.ey)],
+        [ext, ext, (2, 2 * plan.pairs * plan.ex, LANES), (2 * plan.lat_at, plan.ey)],
         both,
     )
     from_z = swap(pay_z, lambda x, y, z: (x, y, z ^ 3))
@@ -932,7 +933,7 @@
         [layers, plan.block, window, window, (plan.edge + plan.share, LANES),
          (plan.edge + plan.share, LANES), share],
         [ext, ext, level1, level1, level1, level1, level1, (nz2 * level1[1], LANES),
-         (plan.fold,) + share],
+         (plan.share, plan.fold * LANES)],
         r, x, ours, got,
     )
     from_a = swap(now, lambda x, y, z: (x, y ^ 1, z))

time: 29.6 us -> 29.5 us (level)
  no operation moved by 1% of the time
where the time goes in v8:
time: 29.5 us; the launch traced here: 29.3 us
  waiting for transfers between devices  10.4 us (35%)
  starting transfers between devices  9.75 us (33%)
  Pallas kernels  7.38 us (25%)
  other arithmetic  1.04 us (4%)
  between operations  0.7 us (2%)
    ppermute x7, waiting for transfers between devices, swap(): return lax.ppermute(values, axes, pairs)  10.4 us
    ppermute x7, starting transfers between devices, swap(): return lax.ppermute(values, axes, pairs)  9.75 us
    pallas_call x4, Pallas kernels, run(): pl.pallas_call(functools.partial(kernel, plan), out_shape=[whole(s) for s...  7.38 us
    another operation x1, other arithmetic, body_fast(): both = jnp.stack([pressure_prev, divergence])  1.04 us
  transfers between devices with their start and end apart: 7, of which 3 were waited for; matrix products, arithmetic and copies ran while one was open for 0% of the time, Pallas kernels for 0%

profile of v8, /device:TPU:0, one launch (start us, length us, event | category | flops | bytes accessed | tf_op | source)
XLA Modules:
  0.0 29.3 jit_solution(15967083069356130761)
XLA Ops:
  0.6 1.0 %select_maximum_fusion.both = f32[2,22,24,256]{3,2,1,0:T(8,128)S(1)} fusion(f32[1,16,16,128]{3,2,1,0:T(8,128)} %bitcast.2, f32[1,16,16,128]{3,2,1,0:T(8,128)} %bitcast.3), kind=kLoop, calls=%fused_computation.2 | loop fusion | flops 3784704 | bytes 1343488 | tf_op jit(solution)/shard_map/stack | solution.py:912
  1.7 1.4 %shard_map.49 = (f32[22,24,256]{2,1,0:T(8,128)S(1)}, f32[22,24,256]{2,1,0:T(8,128)S(1)}, f32[224,128]{1,0:T(8,128)S(1)}, f32[248,128]{1,0:T(8,128)S(1)}, f32[128,128]{1,0:T(8,128)S(1)}) custom-call(f32[2,22,24,256]{3,2,1,0:T(8,128)S(1)} %select_maximum_fusion.both), custom_call_target="tpu_custom_call" | custom-call | tf_op jit(solution)/shard_map/pallas_call | solution.py:886
  3.1 3.0 %collective-permute-start.1 = (f32[248,128]{1,0:T(8,128)S(1)}, f32[248,128]{1,0:T(8,128)S(1)}, u32[]{:S(2)}, u32[]{:S(2)}) collective-permute-start(f32[248,128]{1,0:T(8,128)S(1)} %get-tuple-element.21), channel_id=1, source_target_pairs={{0,16},{1,17},{2,18},{3,19},{4,20},{5,21},{6,22},{7,23},{8,24},{9,... | collective-permute-start | bytes 380936 | tf_op jit(solution)/shard_map/ppermute | solution.py:904
  6.1 0.6 %collective-permute-start = (f32[224,128]{1,0:T(8,128)S(1)}, f32[224,128]{1,0:T(8,128)S(1)}, u32[]{:S(2)}, u32[]{:S(2)}) collective-permute-start(f32[224,128]{1,0:T(8,128)S(1)} %get-tuple-element.20), channel_id=1, source_target_pairs={{0,3},{1,2},{2,1},{3,0},{4,7},{5,6},{6,5},{7,4},{8,11},{9,10},{10,... | collective-permute-start | bytes 344072 | tf_op jit(solution)/shard_map/ppermute | solution.py:904
  6.7 0.6 %collective-permute-start.2 = (f32[128,128]{1,0:T(8,128)S(1)}, f32[128,128]{1,0:T(8,128)S(1)}, u32[]{:S(2)}, u32[]{:S(2)}) collective-permute-start(f32[128,128]{1,0:T(8,128)S(1)} %get-tuple-element.22), channel_id=1, source_target_pairs={{0,19},{1,18},{2,17},{3,16},{4,23},{5,22},{6,21},{7,20},{8,27},{9,... | collective-permute-start | bytes 196616 | tf_op jit(solution)/shard_map/ppermute | solution.py:904
  7.3 4.4 %collective-permute-done.2.from_d = f32[128,128]{1,0:T(8,128)S(1)} collective-permute-done((f32[128,128]{1,0:T(8,128)S(1)}, f32[128,128]{1,0:T(8,128)S(1)}, u32[]{:S(2)}, u32[]{:S(2)}) %collective-permute-start.2) | collective-permute-done | bytes 65568 | tf_op jit(solution)/shard_map/ppermute | solution.py:904
  11.8 0.0 collective-permute-done.from_z
  11.8 0.0 collective-permute-done.1.from_x
  11.8 0.2 shard_map.50
  12.1 0.7 %collective-permute-start.3 = (f32[512,128]{1,0:T(8,128)S(1)}, f32[512,128]{1,0:T(8,128)S(1)}, u32[]{:S(2)}, u32[]{:S(2)}) collective-permute-start(f32[512,128]{1,0:T(8,128)S(1)} %slice_dynamic-update-slice_fusion.ours), channel_id=1, source_target_pairs={{0,1},{1,0},{2,3},{3,2},{4,5},{5,4},{6,7},{7,6},{8,9},{9,8},{10,11... | collective-permute-start | bytes 786440 | tf_op jit(solution)/shard_map/ppermute | solution.py:904
  12.8 1.2 %collective-permute-done.3.theirs = f32[512,128]{1,0:T(8,128)S(1)} collective-permute-done((f32[512,128]{1,0:T(8,128)S(1)}, f32[512,128]{1,0:T(8,128)S(1)}, u32[]{:S(2)}, u32[]{:S(2)}) %collective-permute-start.3) | collective-permute-done | bytes 262176 | tf_op jit(solution)/shard_map/ppermute | solution.py:904
  13.9 1.3 %shard_map.51 = (f32[20,24,256]{2,1,0:T(8,128)S(1)}, f32[16,16,128]{2,1,0:T(8,128)S(1)}, f32[16,16,128]{2,1,0:T(8,128)S(1)}, f32[16,16,128]{2,1,0:T(8,128)S(1)},...) custom-call(f32[22,24,256]{2,1,0:T(8,128)S(1)} %get-tuple-element.23.r_in, ...), custom_call_target="tpu_custom_call" | custom-call | tf_op jit(solution)/shard_map/pallas_call | solution.py:886
  15.2 2.2 %collective-permute-start.4 = (f32[104,128]{1,0:T(8,128)S(1)}, f32[104,128]{1,0:T(8,128)S(1)}, u32[]{:S(2)}, u32[]{:S(2)}) collective-permute-start(f32[104,128]{1,0:T(8,128)S(1)} %get-tuple-element.31), channel_id=1, source_target_pairs={{0,4},{1,5},{2,6},{3,7},{4,0},{5,1},{6,2},{7,3},{8,12},{9,13},{10,... | collective-permute-start | bytes 159752 | tf_op jit(solution)/shard_map/ppermute | solution.py:904
  17.4 2.5 %collective-permute-start.5 = (f32[104,128]{1,0:T(8,128)S(1)}, f32[104,128]{1,0:T(8,128)S(1)}, u32[]{:S(2)}, u32[]{:S(2)}) collective-permute-start(f32[104,128]{1,0:T(8,128)S(1)} %get-tuple-element.32), channel_id=1, source_target_pairs={{0,12},{1,13},{2,14},{3,15},{4,8},{5,9},{6,10},{7,11},{8,4},{9,5},... | collective-permute-start | bytes 159752 | tf_op jit(solution)/shard_map/ppermute | solution.py:904
  19.9 0.1 collective-permute-start.6
  20.0 4.9 %collective-permute-done.6.from_c = f32[48,128]{1,0:T(8,128)S(1)} collective-permute-done((f32[48,128]{1,0:T(8,128)S(1)}, f32[48,128]{1,0:T(8,128)S(1)}, u32[]{:S(2)}, u32[]{:S(2)}) %collective-permute-start.6) | collective-permute-done | bytes 24608 | tf_op jit(solution)/shard_map/ppermute | solution.py:904
  24.9 0.0 collective-permute-done.4.from_a
  24.9 0.0 collective-permute-done.5.from_b
  24.9 4.4 %shard_map.52 = (f32[16,16,128]{2,1,0:T(8,128)}, f32[16,16,128]{2,1,0:T(8,128)}, f32[2,1,16]{2,1,0:T(1,128)}) custom-call(f32[20,24,256]{2,1,0:T(8,128)S(1)} %get-tuple-element.26.r_in, f32[16,16,128]{2,1,0:T(8,128)S(1)} %get-tuple-element.27.x_in, f32[16,16,128]{2,1,0:T(8,128)S(1)} %get-tuple-element.28.r1_in, f32[16,16,128]{2,1,0:T(8,128)S(1)} %get-tuple-element.29.x1_in, ...), custom_call_target="tpu_custom_call" | custom-call | tf_op jit(solution)/shard_map/pallas_call | solution.py:886
  (5 shorter events, 0.0 us)
Async XLA Ops:
  3.1 8.7 %collective-permute-start.1 = (f32[248,128]{1,0:T(8,128)S(1)}, f32[248,128]{1,0:T(8,128)S(1)}, u32[]{:S(2)}, u32[]{:S(2)}) collective-permute-start(f32[248,128]{1,0:T(8,128)S(1)} %get-tuple-element.21), channel_id=1, source_target_pairs={{0,16},{1,17},{2,18},{3,19},{4,20},{5,21},{6,22},{7,23},{8,24},{9,... | collective-permute-start | bytes 380936 | tf_op jit(solution)/shard_map/ppermute | solution.py:904
  6.1 5.7 %collective-permute-start = (f32[224,128]{1,0:T(8,128)S(1)}, f32[224,128]{1,0:T(8,128)S(1)}, u32[]{:S(2)}, u32[]{:S(2)}) collective-permute-start(f32[224,128]{1,0:T(8,128)S(1)} %get-tuple-element.20), channel_id=1, source_target_pairs={{0,3},{1,2},{2,1},{3,0},{4,7},{5,6},{6,5},{7,4},{8,11},{9,10},{10,... | collective-permute-start | bytes 344072 | tf_op jit(solution)/shard_map/ppermute | solution.py:904
  6.7 5.0 %collective-permute-start.2 = (f32[128,128]{1,0:T(8,128)S(1)}, f32[128,128]{1,0:T(8,128)S(1)}, u32[]{:S(2)}, u32[]{:S(2)}) collective-permute-start(f32[128,128]{1,0:T(8,128)S(1)} %get-tuple-element.22), channel_id=1, source_target_pairs={{0,19},{1,18},{2,17},{3,16},{4,23},{5,22},{6,21},{7,20},{8,27},{9,... | collective-permute-start | bytes 196616 | tf_op jit(solution)/shard_map/ppermute | solution.py:904
  12.1 1.8 %collective-permute-start.3 = (f32[512,128]{1,0:T(8,128)S(1)}, f32[512,128]{1,0:T(8,128)S(1)}, u32[]{:S(2)}, u32[]{:S(2)}) collective-permute-start(f32[512,128]{1,0:T(8,128)S(1)} %slice_dynamic-update-slice_fusion.ours), channel_id=1, source_target_pairs={{0,1},{1,0},{2,3},{3,2},{4,5},{5,4},{6,7},{7,6},{8,9},{9,8},{10,11... | collective-permute-start | bytes 786440 | tf_op jit(solution)/shard_map/ppermute | solution.py:904
  15.2 9.7 %collective-permute-start.4 = (f32[104,128]{1,0:T(8,128)S(1)}, f32[104,128]{1,0:T(8,128)S(1)}, u32[]{:S(2)}, u32[]{:S(2)}) collective-permute-start(f32[104,128]{1,0:T(8,128)S(1)} %get-tuple-element.31), channel_id=1, source_target_pairs={{0,4},{1,5},{2,6},{3,7},{4,0},{5,1},{6,2},{7,3},{8,12},{9,13},{10,... | collective-permute-start | bytes 159752 | tf_op jit(solution)/shard_map/ppermute | solution.py:904
  17.4 7.5 %collective-permute-start.5 = (f32[104,128]{1,0:T(8,128)S(1)}, f32[104,128]{1,0:T(8,128)S(1)}, u32[]{:S(2)}, u32[]{:S(2)}) collective-permute-start(f32[104,128]{1,0:T(8,128)S(1)} %get-tuple-element.32), channel_id=1, source_target_pairs={{0,12},{1,13},{2,14},{3,15},{4,8},{5,9},{6,10},{7,11},{8,4},{9,5},... | collective-permute-start | bytes 159752 | tf_op jit(solution)/shard_map/ppermute | solution.py:904
  19.9 5.0 %collective-permute-start.6 = (f32[48,128]{1,0:T(8,128)S(1)}, f32[48,128]{1,0:T(8,128)S(1)}, u32[]{:S(2)}, u32[]{:S(2)}) collective-permute-start(f32[48,128]{1,0:T(8,128)S(1)} %get-tuple-element.30.ours), channel_id=1, source_target_pairs={{0,8},{1,9},{2,10},{3,11},{4,12},{5,13},{6,14},{7,15},{8,0},{9,1},... | collective-permute-start | bytes 73736 | tf_op jit(solution)/shard_map/ppermute | solution.py:904

commit v9 on v8

--- a/solution.py
+++ b/solution.py
@@ -135,6 +135,16 @@
     return out[0:rows] + out[rows:2 * rows] + out[2 * rows:3 * rows]
 
 
+def right_dots(values, table):
+    total = None
+    for _ in range(3):
+        term = values.astype(jnp.bfloat16)
+        part = jnp.dot(term, table, preferred_element_type=F32)
+        total = part if total is None else total + part
+        values = values - term.astype(F32)
+    return total
+
+
 def as_table(keep, value=1.0):
     return jnp.where(keep, value, 0.0).astype(jnp.bfloat16)
 
@@ -154,6 +164,36 @@
         beside = beside + ref[k - 1]
     if k < ref.shape[0] - 1:
         beside = beside + ref[k + 1]
+    return 6.0 * centre - beside
+
+
+def padded(plan):
+    return (plan.ey // LANES, plan.ez, plan.ex + 16, LANES)
+
+
+def put(ref, k, v):
+    rows = v.shape[0]
+    for tile in range(ref.shape[0]):
+        part = v[:, tile * LANES:(tile + 1) * LANES]
+        ref[tile, k, 8:8 + rows, :] = part
+        ref[tile, k, 7:8, :] = part[rows - 1:rows]
+        ref[tile, k, 8 + rows:9 + rows, :] = part[0:1]
+
+
+def rows_of(ref, k, first):
+    here = pl.ds(first, ref.shape[2] - 16)
+    return jnp.concatenate([ref[tile, k, here, :] for tile in range(ref.shape[0])], axis=1)
+
+
+def apply_padded(ref, k, origin):
+    centre = rows_of(ref, k, 8)
+    lanes = centre.shape[1]
+    beside = rows_of(ref, k, origin - 1) + rows_of(ref, k, origin + 1)
+    beside = beside + (pltpu.roll(centre, 1, 1) + pltpu.roll(centre, lanes - 1, 1))
+    if k > 0:
+        beside = beside + rows_of(ref, k - 1, 8)
+    if k < ref.shape[1] - 1:
+        beside = beside + rows_of(ref, k + 1, 8)
     return 6.0 * centre - beside
 
 
@@ -413,29 +453,39 @@
         return v
 
     zero = jnp.zeros((ex, ey), F32)
+    origin = 8 + (iz >> 8)
     for k in range(ez):
         if 2 <= k < ez - 2:
             r = b_ext[k] - apply_at(p_ext, k)
             r_ref[k] = r
-            d_one[k] = masked(k, r * first_scale)
-        else:
-            d_one[k] = zero
+            put(d_one, k, masked(k, r * first_scale))
+        elif 1 <= k < ez - 1:
+            put(d_one, k, zero)
     for k in range(ez):
         if 1 <= k < ez - 1:
-            r = -apply_at(d_one, k)
             if 2 <= k < ez - 2:
-                r = r + r_ref[k]
+                r = r_ref[k] - apply_padded(d_one, k, origin)
+                d = carry_coef * rows_of(d_one, k, 8) + fresh_coef * r
+            else:
+                inward = k + 1 if k == 1 else k - 1
+                r = rows_of(d_one, inward, 8)
+                d = fresh_coef * r
             r_ref[k] = r
-            d_two[k] = masked(k, carry_coef * d_one[k] + fresh_coef * r)
+            put(d_two, k, masked(k, d))
+    for k in range(ez):
+        if 1 <= k < ez - 1:
+            part = rows_of(d_two, k, 8)
+            beside = rows_of(d_two, k, origin - 1) + rows_of(d_two, k, origin + 1)
+            beside = beside + (pltpu.roll(part, 1, 1) + pltpu.roll(part, ey - 1, 1))
+            if k > 1:
+                beside = beside + rows_of(d_two, k - 1, 8)
+            if k < ez - 2:
+                beside = beside + rows_of(d_two, k + 1, 8)
+            r_ref[k] = masked(k, r_ref[k] - (6.0 * part - beside))
+            x_ref[k] = p_ext[k] + (rows_of(d_one, k, 8) + part)
         else:
-            d_two[k] = zero
-    for k in range(ez):
-        r = -apply_at(d_two, k)
-        if 1 <= k < ez - 1:
-            r = r + r_ref[k]
-        r_ref[k] = masked(k, r)
-        x_ref[k] = p_ext[k] + d_one[k] + d_two[k]
-
+            r_ref[k] = masked(k, rows_of(d_two, 1 if k == 0 else ez - 2, 8))
+            x_ref[k] = zero
 
     coarse_z, rows = 2 * plan.pairs, plan.rows
     for zc in range(coarse_z):
@@ -812,11 +862,12 @@
                 wide[row:row + 1, :] = high[j:j + 1]
                 row = at + ex - 4 + 2 * j + twin
                 wide[row:row + 1, :] = low[6 + j:7 + j]
-    out = right_dot(wide[...], double)
+    origin = 8 + (iz >> 8)
     for zc in range(half_z + 4):
+        v = right_dots(wide[zc * ex:(zc + 1) * ex, :], double)
         for k in (2 * zc - 1, 2 * zc):
             if 0 <= k < ez:
-                e0[k] = out[zc * ex:(zc + 1) * ex]
+                put(e0, k, v)
     flat = wrapped_mask((ex, ey), {0: bx, 1: by}, (x_low, y_low), (x_high, y_high))
     below = jnp.where(z_low, 1.0, 0.0).astype(F32)
     above = jnp.where(z_high, 1.0, 0.0).astype(F32)
@@ -832,27 +883,28 @@
     high, low = sent((0, ex))
     for k in range(layers):
         s, inner = plan.slots[k], plan.inner[k]
-        v = r_in[k] - apply_at(e0, k + 1)
+        v = r_in[k] - apply_padded(e0, k + 1, origin)
         own = v[:, 0:by] + landed(high, s, 3, LANES - 3) + landed(low, s + inner, 3, 0)
         spill = v[:, by:ey]
         if inner:
             spill = spill + landed(high, s + 3, inner, 0) + landed(low, s, inner, LANES - inner)
         r[k, :, 0:by] = own
         r[k, :, by:ey] = spill
-        d0[k] = masked(k + 1, r[k] * first_scale)
+        put(d0, k, masked(k + 1, r[k] * first_scale))
         if inner == 2:
             s = s + 3 + inner
             p_ref[k - 2] = (
-                x_in[k - 2] + e0[k + 1, 0:bx, 0:by]
+                x_in[k - 2] + e0[0, k + 1, 8:8 + bx, :]
                 + (landed(high, s, 2, LANES - 2) + landed(low, s, 2, 0))[0:bx]
             )
     for k in range(1, layers - 1):
-        v = r[k] - apply_at(d0, k)
+        v = r[k] - apply_padded(d0, k, origin)
         r[k] = v
-        v = masked(k + 1, carry_coef * d0[k] + fresh_coef * v)
-        e0[k] = v
+        d = rows_of(d0, k, 8)
+        v = masked(k + 1, carry_coef * d + fresh_coef * v)
+        put(e0, k, v)
         if 2 <= k < 2 + bz:
-            p_ref[k - 2] += d0[k, 0:bx, 0:by] + v[0:bx, 0:by]
+            p_ref[k - 2] += d[0:bx, 0:by] + v[0:bx, 0:by]
     copy = pltpu.make_async_copy(p_ref, p_out, sem.at[0])
     copy.start()
     copies = [copy]
@@ -860,7 +912,7 @@
     for part in range(parts):
         here = range(part * bz // parts, (part + 1) * bz // parts)
         for j in here:
-            v = r[j + 2] - apply_at(e0, j + 2)
+            v = r[j + 2] - apply_padded(e0, j + 2, origin)
             res_ref[j] = v[0:bx, 0:by]
         here = pl.ds(here[0], bz // parts)
         copy = pltpu.make_async_copy(res_ref.at[here], res_out.at[here], sem.at[1 + part])
@@ -913,7 +965,8 @@
     both = jnp.pad(both, ((0, 0), (3, 3), (0, plan.ex - plan.block[1]), (0, plan.ey - plan.block[2])))
     r, x, pay_z, pay_x, pay_d = run(
         first_kernel, plan, [ext, ext] + payload,
-        [ext, ext, (2, 2 * plan.pairs * plan.ex, LANES), (2 * plan.lat_at, plan.ey)],
+        [padded(plan), padded(plan), (2, 2 * plan.pairs * plan.ex, LANES),
+         (2 * plan.lat_at, plan.ey)],
         both,
     )
     from_z = swap(pay_z, lambda x, y, z: (x, y, z ^ 3))
@@ -943,7 +996,7 @@
         last_kernel, plan,
         [plan.block, plan.block, tuple(n >> 3 for n in plan.level2)],
         [(4,) + share, plan.block, plan.block, layers, window,
-         (window[0] + 4, window[1] + 16, LANES), ext, layers, window, window,
+         (window[0] + 4, window[1] + 16, LANES), padded(plan), padded(plan), window, window,
          (nz2 * nx2, LANES), (2 * plan.pairs * plan.ex, LANES)],
         r, x, r1, x1, ours, from_a, from_b, from_c,
         out_specs=[ANY, ANY, VMEM], semaphores=3,

time: 29.5 us -> 29.3 us (level)
  no operation moved by 1% of the time
where the time goes in v9:
time: 29.3 us; the launch traced here: 29.2 us
  waiting for transfers between devices  10.4 us (35%)
  starting transfers between devices  9.75 us (33%)
  Pallas kernels  7.22 us (25%)
  other arithmetic  1.04 us (4%)
  between operations  0.7 us (2%)
    ppermute x7, waiting for transfers between devices, swap(): return lax.ppermute(values, axes, pairs)  10.4 us
    ppermute x7, starting transfers between devices, swap(): return lax.ppermute(values, axes, pairs)  9.75 us
    pallas_call x4, Pallas kernels, run(): pl.pallas_call(functools.partial(kernel, plan), out_shape=[whole(s) for s...  7.22 us
    another operation x1, other arithmetic, body_fast(): both = jnp.stack([pressure_prev, divergence])  1.04 us
  transfers between devices with their start and end apart: 7, of which 3 were waited for; matrix products, arithmetic and copies ran while one was open for 0% of the time, Pallas kernels for 0%

profile of v9, /device:TPU:0, one launch (start us, length us, event | category | flops | bytes accessed | tf_op | source)
XLA Modules:
  0.0 29.2 jit_solution(13415674464531311919)
XLA Ops:
  0.6 1.0 %select_maximum_fusion.both = f32[2,22,24,256]{3,2,1,0:T(8,128)S(1)} fusion(f32[1,16,16,128]{3,2,1,0:T(8,128)} %bitcast.2, f32[1,16,16,128]{3,2,1,0:T(8,128)} %bitcast.3), kind=kLoop, calls=%fused_computation.2 | loop fusion | flops 3784704 | bytes 1343488 | tf_op jit(solution)/shard_map/stack | solution.py:964
  1.7 1.3 %shard_map.49 = (f32[22,24,256]{2,1,0:T(8,128)S(1)}, f32[22,24,256]{2,1,0:T(8,128)S(1)}, f32[224,128]{1,0:T(8,128)S(1)}, f32[248,128]{1,0:T(8,128)S(1)}, f32[128,128]{1,0:T(8,128)S(1)}) custom-call(f32[2,22,24,256]{3,2,1,0:T(8,128)S(1)} %select_maximum_fusion.both), custom_call_target="tpu_custom_call" | custom-call | tf_op jit(solution)/shard_map/pallas_call | solution.py:938
  2.9 3.0 %collective-permute-start.1 = (f32[248,128]{1,0:T(8,128)S(1)}, f32[248,128]{1,0:T(8,128)S(1)}, u32[]{:S(2)}, u32[]{:S(2)}) collective-permute-start(f32[248,128]{1,0:T(8,128)S(1)} %get-tuple-element.21), channel_id=1, source_target_pairs={{0,16},{1,17},{2,18},{3,19},{4,20},{5,21},{6,22},{7,23},{8,24},{9,... | collective-permute-start | bytes 380936 | tf_op jit(solution)/shard_map/ppermute | solution.py:956
  6.0 0.6 %collective-permute-start = (f32[224,128]{1,0:T(8,128)S(1)}, f32[224,128]{1,0:T(8,128)S(1)}, u32[]{:S(2)}, u32[]{:S(2)}) collective-permute-start(f32[224,128]{1,0:T(8,128)S(1)} %get-tuple-element.20), channel_id=1, source_target_pairs={{0,3},{1,2},{2,1},{3,0},{4,7},{5,6},{6,5},{7,4},{8,11},{9,10},{10,... | collective-permute-start | bytes 344072 | tf_op jit(solution)/shard_map/ppermute | solution.py:956
  6.6 0.6 %collective-permute-start.2 = (f32[128,128]{1,0:T(8,128)S(1)}, f32[128,128]{1,0:T(8,128)S(1)}, u32[]{:S(2)}, u32[]{:S(2)}) collective-permute-start(f32[128,128]{1,0:T(8,128)S(1)} %get-tuple-element.22), channel_id=1, source_target_pairs={{0,19},{1,18},{2,17},{3,16},{4,23},{5,22},{6,21},{7,20},{8,27},{9,... | collective-permute-start | bytes 196616 | tf_op jit(solution)/shard_map/ppermute | solution.py:956
  7.2 4.4 %collective-permute-done.2.from_d = f32[128,128]{1,0:T(8,128)S(1)} collective-permute-done((f32[128,128]{1,0:T(8,128)S(1)}, f32[128,128]{1,0:T(8,128)S(1)}, u32[]{:S(2)}, u32[]{:S(2)}) %collective-permute-start.2) | collective-permute-done | bytes 65568 | tf_op jit(solution)/shard_map/ppermute | solution.py:956
  11.6 0.0 collective-permute-done.from_z
  11.6 0.0 collective-permute-done.1.from_x
  11.6 0.2 shard_map.50
  12.0 0.7 %collective-permute-start.3 = (f32[512,128]{1,0:T(8,128)S(1)}, f32[512,128]{1,0:T(8,128)S(1)}, u32[]{:S(2)}, u32[]{:S(2)}) collective-permute-start(f32[512,128]{1,0:T(8,128)S(1)} %slice_dynamic-update-slice_fusion.ours), channel_id=1, source_target_pairs={{0,1},{1,0},{2,3},{3,2},{4,5},{5,4},{6,7},{7,6},{8,9},{9,8},{10,11... | collective-permute-start | bytes 786440 | tf_op jit(solution)/shard_map/ppermute | solution.py:956
  12.6 1.2 %collective-permute-done.3.theirs = f32[512,128]{1,0:T(8,128)S(1)} collective-permute-done((f32[512,128]{1,0:T(8,128)S(1)}, f32[512,128]{1,0:T(8,128)S(1)}, u32[]{:S(2)}, u32[]{:S(2)}) %collective-permute-start.3) | collective-permute-done | bytes 262176 | tf_op jit(solution)/shard_map/ppermute | solution.py:956
  13.8 1.3 %shard_map.51 = (f32[20,24,256]{2,1,0:T(8,128)S(1)}, f32[16,16,128]{2,1,0:T(8,128)S(1)}, f32[16,16,128]{2,1,0:T(8,128)S(1)}, f32[16,16,128]{2,1,0:T(8,128)S(1)},...) custom-call(f32[22,24,256]{2,1,0:T(8,128)S(1)} %get-tuple-element.23.r_in, ...), custom_call_target="tpu_custom_call" | custom-call | tf_op jit(solution)/shard_map/pallas_call | solution.py:938
  15.1 2.2 %collective-permute-start.4 = (f32[104,128]{1,0:T(8,128)S(1)}, f32[104,128]{1,0:T(8,128)S(1)}, u32[]{:S(2)}, u32[]{:S(2)}) collective-permute-start(f32[104,128]{1,0:T(8,128)S(1)} %get-tuple-element.31), channel_id=1, source_target_pairs={{0,4},{1,5},{2,6},{3,7},{4,0},{5,1},{6,2},{7,3},{8,12},{9,13},{10,... | collective-permute-start | bytes 159752 | tf_op jit(solution)/shard_map/ppermute | solution.py:956
  17.3 2.5 %collective-permute-start.5 = (f32[104,128]{1,0:T(8,128)S(1)}, f32[104,128]{1,0:T(8,128)S(1)}, u32[]{:S(2)}, u32[]{:S(2)}) collective-permute-start(f32[104,128]{1,0:T(8,128)S(1)} %get-tuple-element.32), channel_id=1, source_target_pairs={{0,12},{1,13},{2,14},{3,15},{4,8},{5,9},{6,10},{7,11},{8,4},{9,5},... | collective-permute-start | bytes 159752 | tf_op jit(solution)/shard_map/ppermute | solution.py:956
  19.8 0.1 collective-permute-start.6
  19.9 4.9 %collective-permute-done.6.from_c = f32[48,128]{1,0:T(8,128)S(1)} collective-permute-done((f32[48,128]{1,0:T(8,128)S(1)}, f32[48,128]{1,0:T(8,128)S(1)}, u32[]{:S(2)}, u32[]{:S(2)}) %collective-permute-start.6) | collective-permute-done | bytes 24608 | tf_op jit(solution)/shard_map/ppermute | solution.py:956
  24.8 0.0 collective-permute-done.4.from_a
  24.8 0.0 collective-permute-done.5.from_b
  24.8 4.4 %shard_map.52 = (f32[16,16,128]{2,1,0:T(8,128)}, f32[16,16,128]{2,1,0:T(8,128)}, f32[2,1,16]{2,1,0:T(1,128)}) custom-call(f32[20,24,256]{2,1,0:T(8,128)S(1)} %get-tuple-element.26.r_in, f32[16,16,128]{2,1,0:T(8,128)S(1)} %get-tuple-element.27.x_in, f32[16,16,128]{2,1,0:T(8,128)S(1)} %get-tuple-element.28.r1_in, f32[16,16,128]{2,1,0:T(8,128)S(1)} %get-tuple-element.29.x1_in, ...), custom_call_target="tpu_custom_call" | custom-call | tf_op jit(solution)/shard_map/pallas_call | solution.py:938
  (5 shorter events, 0.0 us)
Async XLA Ops:
  2.9 8.7 %collective-permute-start.1 = (f32[248,128]{1,0:T(8,128)S(1)}, f32[248,128]{1,0:T(8,128)S(1)}, u32[]{:S(2)}, u32[]{:S(2)}) collective-permute-start(f32[248,128]{1,0:T(8,128)S(1)} %get-tuple-element.21), channel_id=1, source_target_pairs={{0,16},{1,17},{2,18},{3,19},{4,20},{5,21},{6,22},{7,23},{8,24},{9,... | collective-permute-start | bytes 380936 | tf_op jit(solution)/shard_map/ppermute | solution.py:956
  6.0 5.7 %collective-permute-start = (f32[224,128]{1,0:T(8,128)S(1)}, f32[224,128]{1,0:T(8,128)S(1)}, u32[]{:S(2)}, u32[]{:S(2)}) collective-permute-start(f32[224,128]{1,0:T(8,128)S(1)} %get-tuple-element.20), channel_id=1, source_target_pairs={{0,3},{1,2},{2,1},{3,0},{4,7},{5,6},{6,5},{7,4},{8,11},{9,10},{10,... | collective-permute-start | bytes 344072 | tf_op jit(solution)/shard_map/ppermute | solution.py:956
  6.6 5.0 %collective-permute-start.2 = (f32[128,128]{1,0:T(8,128)S(1)}, f32[128,128]{1,0:T(8,128)S(1)}, u32[]{:S(2)}, u32[]{:S(2)}) collective-permute-start(f32[128,128]{1,0:T(8,128)S(1)} %get-tuple-element.22), channel_id=1, source_target_pairs={{0,19},{1,18},{2,17},{3,16},{4,23},{5,22},{6,21},{7,20},{8,27},{9,... | collective-permute-start | bytes 196616 | tf_op jit(solution)/shard_map/ppermute | solution.py:956
  12.0 1.8 %collective-permute-start.3 = (f32[512,128]{1,0:T(8,128)S(1)}, f32[512,128]{1,0:T(8,128)S(1)}, u32[]{:S(2)}, u32[]{:S(2)}) collective-permute-start(f32[512,128]{1,0:T(8,128)S(1)} %slice_dynamic-update-slice_fusion.ours), channel_id=1, source_target_pairs={{0,1},{1,0},{2,3},{3,2},{4,5},{5,4},{6,7},{7,6},{8,9},{9,8},{10,11... | collective-permute-start | bytes 786440 | tf_op jit(solution)/shard_map/ppermute | solution.py:956
  15.1 9.7 %collective-permute-start.4 = (f32[104,128]{1,0:T(8,128)S(1)}, f32[104,128]{1,0:T(8,128)S(1)}, u32[]{:S(2)}, u32[]{:S(2)}) collective-permute-start(f32[104,128]{1,0:T(8,128)S(1)} %get-tuple-element.31), channel_id=1, source_target_pairs={{0,4},{1,5},{2,6},{3,7},{4,0},{5,1},{6,2},{7,3},{8,12},{9,13},{10,... | collective-permute-start | bytes 159752 | tf_op jit(solution)/shard_map/ppermute | solution.py:956
  17.3 7.5 %collective-permute-start.5 = (f32[104,128]{1,0:T(8,128)S(1)}, f32[104,128]{1,0:T(8,128)S(1)}, u32[]{:S(2)}, u32[]{:S(2)}) collective-permute-start(f32[104,128]{1,0:T(8,128)S(1)} %get-tuple-element.32), channel_id=1, source_target_pairs={{0,12},{1,13},{2,14},{3,15},{4,8},{5,9},{6,10},{7,11},{8,4},{9,5},... | collective-permute-start | bytes 159752 | tf_op jit(solution)/shard_map/ppermute | solution.py:956
  19.8 5.0 %collective-permute-start.6 = (f32[48,128]{1,0:T(8,128)S(1)}, f32[48,128]{1,0:T(8,128)S(1)}, u32[]{:S(2)}, u32[]{:S(2)}) collective-permute-start(f32[48,128]{1,0:T(8,128)S(1)} %get-tuple-element.30.ours), channel_id=1, source_target_pairs={{0,8},{1,9},{2,10},{3,11},{4,12},{5,13},{6,14},{7,15},{8,0},{9,1},... | collective-permute-start | bytes 73736 | tf_op jit(solution)/shard_map/ppermute | solution.py:956

commit v10 on v9

--- a/solution.py
+++ b/solution.py
@@ -768,7 +768,7 @@
     return x, (x if level == LEVELS - 1 else coarsest)
 
 
-def last_kernel(plan, r_in, x_in, r1_in, x1_in, ours, from_a, from_b, from_c, p_out, res_out, last_ref, *scratch):
+def last_kernel(plan, r_in, x_in, r1_in, x1_in, ours, from_a, from_b, from_2, from_3, p_out, res_out, last_ref, *scratch):
     shares, p_ref, res_ref, r, q1, e1, e0, d0, d1, r1, lines, wide, sem = scratch
     bz, bx, by = plan.block
     ez, ex, ey = plan.ext
@@ -781,8 +781,9 @@
 
     shares[0] = ours[...]
     shares[1] = from_a[plan.edge:plan.edge + plan.share, :]
-    shares[3] = from_b[plan.edge:plan.edge + plan.share, :]
-    shares[2] = from_c[...]
+    inner = side(iy, 3)[1]
+    shares[3] = jnp.where(inner, from_b[plan.edge:plan.edge + plan.share, :], from_3[...])
+    shares[2] = from_2[...]
     own2 = half // 2
     source = []
     for part in range(plan.fold):
@@ -990,15 +991,16 @@
         r, x, ours, got,
     )
     from_a = swap(now, lambda x, y, z: (x, y ^ 1, z))
-    from_b = swap(later, lambda x, y, z: (x, y ^ 3, z))
-    from_c = swap(ours, lambda x, y, z: (x, y ^ 2, z))
+    from_b = swap(later, lambda x, y, z: (x, y ^ 3, z) if y in (1, 2) else None)
+    from_3 = swap(ours, lambda x, y, z: (x, y ^ 3, z) if y in (0, 3) else None)
+    from_2 = swap(ours, lambda x, y, z: (x, y ^ 2, z))
     return run(
         last_kernel, plan,
         [plan.block, plan.block, tuple(n >> 3 for n in plan.level2)],
         [(4,) + share, plan.block, plan.block, layers, window,
          (window[0] + 4, window[1] + 16, LANES), padded(plan), padded(plan), window, window,
          (nz2 * nx2, LANES), (2 * plan.pairs * plan.ex, LANES)],
-        r, x, r1, x1, ours, from_a, from_b, from_c,
+        r, x, r1, x1, ours, from_a, from_b, from_2, from_3,
         out_specs=[ANY, ANY, VMEM], semaphores=3,
     )
 

time: 29.3 us -> 32 us (1.092)
  starting transfers between devices: 9.75 us -> 12.4 us
    ppermute x7 -> x8, starting transfers between devices: 9.75 us -> 12.4 us  [swap(): return lax.ppermute(values, axes, pairs)]
    ppermute x7 -> x8, waiting for transfers between devices: 10.4 us -> 10.4 us  [swap(): return lax.ppermute(values, axes, pairs)]
  transfers between devices with their start and end apart: 7 -> 8, of which waited for: 3 -> 4; matrix products, arithmetic and copies ran while one was open for 0% -> 0% of each run, Pallas kernels for 0% -> 0%
where the time goes in v10:
time: 32 us; the launch traced here: 31.8 us
  starting transfers between devices  12.4 us (39%)
  waiting for transfers between devices  10.4 us (32%)
  Pallas kernels  7.23 us (23%)
  other arithmetic  1.04 us (3%)
  between operations  0.72 us (2%)
    ppermute x8, starting transfers between devices, swap(): return lax.ppermute(values, axes, pairs)  12.4 us
    ppermute x8, waiting for transfers between devices, swap(): return lax.ppermute(values, axes, pairs)  10.4 us
    pallas_call x4, Pallas kernels, run(): pl.pallas_call(functools.partial(kernel, plan), out_shape=[whole(s) for s...  7.23 us
    another operation x1, other arithmetic, body_fast(): both = jnp.stack([pressure_prev, divergence])  1.04 us
  transfers between devices with their start and end apart: 8, of which 4 were waited for; matrix products, arithmetic and copies ran while one was open for 0% of the time, Pallas kernels for 0%

profile of v10, /device:TPU:0, one launch (start us, length us, event | category | flops | bytes accessed | tf_op | source)
XLA Modules:
  0.0 31.8 jit_solution(735776338508393538)
XLA Ops:
  0.6 1.0 %select_maximum_fusion.both = f32[2,22,24,256]{3,2,1,0:T(8,128)S(1)} fusion(f32[1,16,16,128]{3,2,1,0:T(8,128)} %bitcast.2, f32[1,16,16,128]{3,2,1,0:T(8,128)} %bitcast.3), kind=kLoop, calls=%fused_computation.2 | loop fusion | flops 3784704 | bytes 1343488 | tf_op jit(solution)/shard_map/stack | solution.py:965
  1.7 1.3 %shard_map.49 = (f32[22,24,256]{2,1,0:T(8,128)S(1)}, f32[22,24,256]{2,1,0:T(8,128)S(1)}, f32[224,128]{1,0:T(8,128)S(1)}, f32[248,128]{1,0:T(8,128)S(1)}, f32[128,128]{1,0:T(8,128)S(1)}) custom-call(f32[2,22,24,256]{3,2,1,0:T(8,128)S(1)} %select_maximum_fusion.both), custom_call_target="tpu_custom_call" | custom-call | tf_op jit(solution)/shard_map/pallas_call | solution.py:939
  2.9 3.0 %collective-permute-start.1 = (f32[248,128]{1,0:T(8,128)S(1)}, f32[248,128]{1,0:T(8,128)S(1)}, u32[]{:S(2)}, u32[]{:S(2)}) collective-permute-start(f32[248,128]{1,0:T(8,128)S(1)} %get-tuple-element.21), channel_id=1, source_target_pairs={{0,16},{1,17},{2,18},{3,19},{4,20},{5,21},{6,22},{7,23},{8,24},{9,... | collective-permute-start | bytes 380936 | tf_op jit(solution)/shard_map/ppermute | solution.py:957
  6.0 0.6 %collective-permute-start = (f32[224,128]{1,0:T(8,128)S(1)}, f32[224,128]{1,0:T(8,128)S(1)}, u32[]{:S(2)}, u32[]{:S(2)}) collective-permute-start(f32[224,128]{1,0:T(8,128)S(1)} %get-tuple-element.20), channel_id=1, source_target_pairs={{0,3},{1,2},{2,1},{3,0},{4,7},{5,6},{6,5},{7,4},{8,11},{9,10},{10,... | collective-permute-start | bytes 344072 | tf_op jit(solution)/shard_map/ppermute | solution.py:957
  6.6 0.6 %collective-permute-start.2 = (f32[128,128]{1,0:T(8,128)S(1)}, f32[128,128]{1,0:T(8,128)S(1)}, u32[]{:S(2)}, u32[]{:S(2)}) collective-permute-start(f32[128,128]{1,0:T(8,128)S(1)} %get-tuple-element.22), channel_id=1, source_target_pairs={{0,19},{1,18},{2,17},{3,16},{4,23},{5,22},{6,21},{7,20},{8,27},{9,... | collective-permute-start | bytes 196616 | tf_op jit(solution)/shard_map/ppermute | solution.py:957
  7.2 4.4 %collective-permute-done.2.from_d = f32[128,128]{1,0:T(8,128)S(1)} collective-permute-done((f32[128,128]{1,0:T(8,128)S(1)}, f32[128,128]{1,0:T(8,128)S(1)}, u32[]{:S(2)}, u32[]{:S(2)}) %collective-permute-start.2) | collective-permute-done | bytes 65568 | tf_op jit(solution)/shard_map/ppermute | solution.py:957
  11.6 0.0 collective-permute-done.from_z
  11.6 0.0 collective-permute-done.1.from_x
  11.6 0.2 shard_map.50
  12.0 0.7 %collective-permute-start.3 = (f32[512,128]{1,0:T(8,128)S(1)}, f32[512,128]{1,0:T(8,128)S(1)}, u32[]{:S(2)}, u32[]{:S(2)}) collective-permute-start(f32[512,128]{1,0:T(8,128)S(1)} %slice_dynamic-update-slice_fusion.ours), channel_id=1, source_target_pairs={{0,1},{1,0},{2,3},{3,2},{4,5},{5,4},{6,7},{7,6},{8,9},{9,8},{10,11... | collective-permute-start | bytes 786440 | tf_op jit(solution)/shard_map/ppermute | solution.py:957
  12.6 1.2 %collective-permute-done.3.theirs = f32[512,128]{1,0:T(8,128)S(1)} collective-permute-done((f32[512,128]{1,0:T(8,128)S(1)}, f32[512,128]{1,0:T(8,128)S(1)}, u32[]{:S(2)}, u32[]{:S(2)}) %collective-permute-start.3) | collective-permute-done | bytes 262176 | tf_op jit(solution)/shard_map/ppermute | solution.py:957
  13.8 1.3 %shard_map.51 = (f32[20,24,256]{2,1,0:T(8,128)S(1)}, f32[16,16,128]{2,1,0:T(8,128)S(1)}, f32[16,16,128]{2,1,0:T(8,128)S(1)}, f32[16,16,128]{2,1,0:T(8,128)S(1)},...) custom-call(f32[22,24,256]{2,1,0:T(8,128)S(1)} %get-tuple-element.23.r_in, ...), custom_call_target="tpu_custom_call" | custom-call | tf_op jit(solution)/shard_map/pallas_call | solution.py:939
  15.1 2.2 %collective-permute-start.4 = (f32[104,128]{1,0:T(8,128)S(1)}, f32[104,128]{1,0:T(8,128)S(1)}, u32[]{:S(2)}, u32[]{:S(2)}) collective-permute-start(f32[104,128]{1,0:T(8,128)S(1)} %get-tuple-element.31), channel_id=1, source_target_pairs={{0,4},{1,5},{2,6},{3,7},{4,0},{5,1},{6,2},{7,3},{8,12},{9,13},{10,... | collective-permute-start | bytes 159752 | tf_op jit(solution)/shard_map/ppermute | solution.py:957
  17.3 0.7 %collective-permute-start.5 = (f32[104,128]{1,0:T(8,128)S(1)}, f32[104,128]{1,0:T(8,128)S(1)}, u32[]{:S(2)}, u32[]{:S(2)}) collective-permute-start(f32[104,128]{1,0:T(8,128)S(1)} %get-tuple-element.32), channel_id=1, source_target_pairs={{4,8},{5,9},{6,10},{7,11},{8,4},{9,5},{10,6},{11,7},{20,24},{21,25... | collective-permute-start | bytes 159752 | tf_op jit(solution)/shard_map/ppermute | solution.py:957
  18.0 4.4 %collective-permute-start.7 = (f32[48,128]{1,0:T(8,128)S(1)}, f32[48,128]{1,0:T(8,128)S(1)}, u32[]{:S(2)}, u32[]{:S(2)}) collective-permute-start(f32[48,128]{1,0:T(8,128)S(1)} %get-tuple-element.30.ours), channel_id=1, source_target_pairs={{0,12},{1,13},{2,14},{3,15},{12,0},{13,1},{14,2},{15,3},{16,28},{1... | collective-permute-start | bytes 73736 | tf_op jit(solution)/shard_map/ppermute | solution.py:957
  22.4 0.2 collective-permute-start.6
  22.6 2.9 %collective-permute-done.7.from_3 = f32[48,128]{1,0:T(8,128)S(1)} collective-permute-done((f32[48,128]{1,0:T(8,128)S(1)}, f32[48,128]{1,0:T(8,128)S(1)}, u32[]{:S(2)}, u32[]{:S(2)}) %collective-permute-start.7) | collective-permute-done | bytes 24608 | tf_op jit(solution)/shard_map/ppermute | solution.py:957
  25.5 1.9 %collective-permute-done.6.from_2 = f32[48,128]{1,0:T(8,128)S(1)} collective-permute-done((f32[48,128]{1,0:T(8,128)S(1)}, f32[48,128]{1,0:T(8,128)S(1)}, u32[]{:S(2)}, u32[]{:S(2)}) %collective-permute-start.6) | collective-permute-done | bytes 24608 | tf_op jit(solution)/shard_map/ppermute | solution.py:957
  27.4 0.0 collective-permute-done.4.from_a
  27.4 0.0 collective-permute-done.5.from_b
  27.4 4.4 %shard_map.52 = (f32[16,16,128]{2,1,0:T(8,128)}, f32[16,16,128]{2,1,0:T(8,128)}, f32[2,1,16]{2,1,0:T(1,128)}) custom-call(f32[20,24,256]{2,1,0:T(8,128)S(1)} %get-tuple-element.26.r_in, f32[16,16,128]{2,1,0:T(8,128)S(1)} %get-tuple-element.27.x_in, f32[16,16,128]{2,1,0:T(8,128)S(1)} %get-tuple-element.28.r1_in, f32[16,16,128]{2,1,0:T(8,128)S(1)} %get-tuple-element.29.x1_in, ...), custom_call_target="tpu_custom_call" | custom-call | tf_op jit(solution)/shard_map/pallas_call | solution.py:939
  (5 shorter events, 0.0 us)
Async XLA Ops:
  2.9 8.7 %collective-permute-start.1 = (f32[248,128]{1,0:T(8,128)S(1)}, f32[248,128]{1,0:T(8,128)S(1)}, u32[]{:S(2)}, u32[]{:S(2)}) collective-permute-start(f32[248,128]{1,0:T(8,128)S(1)} %get-tuple-element.21), channel_id=1, source_target_pairs={{0,16},{1,17},{2,18},{3,19},{4,20},{5,21},{6,22},{7,23},{8,24},{9,... | collective-permute-start | bytes 380936 | tf_op jit(solution)/shard_map/ppermute | solution.py:957
  6.0 5.7 %collective-permute-start = (f32[224,128]{1,0:T(8,128)S(1)}, f32[224,128]{1,0:T(8,128)S(1)}, u32[]{:S(2)}, u32[]{:S(2)}) collective-permute-start(f32[224,128]{1,0:T(8,128)S(1)} %get-tuple-element.20), channel_id=1, source_target_pairs={{0,3},{1,2},{2,1},{3,0},{4,7},{5,6},{6,5},{7,4},{8,11},{9,10},{10,... | collective-permute-start | bytes 344072 | tf_op jit(solution)/shard_map/ppermute | solution.py:957
  6.6 5.0 %collective-permute-start.2 = (f32[128,128]{1,0:T(8,128)S(1)}, f32[128,128]{1,0:T(8,128)S(1)}, u32[]{:S(2)}, u32[]{:S(2)}) collective-permute-start(f32[128,128]{1,0:T(8,128)S(1)} %get-tuple-element.22), channel_id=1, source_target_pairs={{0,19},{1,18},{2,17},{3,16},{4,23},{5,22},{6,21},{7,20},{8,27},{9,... | collective-permute-start | bytes 196616 | tf_op jit(solution)/shard_map/ppermute | solution.py:957
  12.0 1.8 %collective-permute-start.3 = (f32[512,128]{1,0:T(8,128)S(1)}, f32[512,128]{1,0:T(8,128)S(1)}, u32[]{:S(2)}, u32[]{:S(2)}) collective-permute-start(f32[512,128]{1,0:T(8,128)S(1)} %slice_dynamic-update-slice_fusion.ours), channel_id=1, source_target_pairs={{0,1},{1,0},{2,3},{3,2},{4,5},{5,4},{6,7},{7,6},{8,9},{9,8},{10,11... | collective-permute-start | bytes 786440 | tf_op jit(solution)/shard_map/ppermute | solution.py:957
  15.1 12.3 %collective-permute-start.4 = (f32[104,128]{1,0:T(8,128)S(1)}, f32[104,128]{1,0:T(8,128)S(1)}, u32[]{:S(2)}, u32[]{:S(2)}) collective-permute-start(f32[104,128]{1,0:T(8,128)S(1)} %get-tuple-element.31), channel_id=1, source_target_pairs={{0,4},{1,5},{2,6},{3,7},{4,0},{5,1},{6,2},{7,3},{8,12},{9,13},{10,... | collective-permute-start | bytes 159752 | tf_op jit(solution)/shard_map/ppermute | solution.py:957
  17.3 10.1 %collective-permute-start.5 = (f32[104,128]{1,0:T(8,128)S(1)}, f32[104,128]{1,0:T(8,128)S(1)}, u32[]{:S(2)}, u32[]{:S(2)}) collective-permute-start(f32[104,128]{1,0:T(8,128)S(1)} %get-tuple-element.32), channel_id=1, source_target_pairs={{4,8},{5,9},{6,10},{7,11},{8,4},{9,5},{10,6},{11,7},{20,24},{21,25... | collective-permute-start | bytes 159752 | tf_op jit(solution)/shard_map/ppermute | solution.py:957
  18.0 7.5 %collective-permute-start.7 = (f32[48,128]{1,0:T(8,128)S(1)}, f32[48,128]{1,0:T(8,128)S(1)}, u32[]{:S(2)}, u32[]{:S(2)}) collective-permute-start(f32[48,128]{1,0:T(8,128)S(1)} %get-tuple-element.30.ours), channel_id=1, source_target_pairs={{0,12},{1,13},{2,14},{3,15},{12,0},{13,1},{14,2},{15,3},{16,28},{1... | collective-permute-start | bytes 73736 | tf_op jit(solution)/shard_map/ppermute | solution.py:957
  22.4 5.1 %collective-permute-start.6 = (f32[48,128]{1,0:T(8,128)S(1)}, f32[48,128]{1,0:T(8,128)S(1)}, u32[]{:S(2)}, u32[]{:S(2)}) collective-permute-start(f32[48,128]{1,0:T(8,128)S(1)} %get-tuple-element.30.ours), channel_id=1, source_target_pairs={{0,8},{1,9},{2,10},{3,11},{4,12},{5,13},{6,14},{7,15},{8,0},{9,1},... | collective-permute-start | bytes 73736 | tf_op jit(solution)/shard_map/ppermute | solution.py:957

commit v11 on v9

--- a/solution.py
+++ b/solution.py
@@ -742,26 +742,65 @@
             out.append(6.0 * v[k] - beside)
         return out
 
+    def moves(v, dim, places):
+        size, shift = v.shape[dim], places * step
+        if abs(shift) >= size:
+            return jnp.zeros_like(v)
+        index = row if dim == 0 else lane
+        keep = index < size - shift if shift > 0 else index >= -shift
+        return only(keep, pltpu.roll(v, -shift % size, dim))
+
+    def at(values, k):
+        return values[k] if 0 <= k < len(values) else None
+
+    def added(*terms):
+        total = None
+        for term in terms:
+            if term is not None:
+                total = term if total is None else total + term
+        return total
+
     d = [first_scale * v for v in source]
-    r = [b - t for b, t in zip(source, op(d))]
-    d2 = [carry_coef * v + fresh_coef * t for v, t in zip(d, r)]
+    before = [b - t for b, t in zip(source, op(d))]
+    d2 = [carry_coef * v + fresh_coef * t for v, t in zip(d, before)]
     x = [v + t for v, t in zip(d, d2)]
-    r = [v - t for v, t in zip(r, op(d2))]
+    r = [v - t for v, t in zip(before, op(d2))]
     coarsest = None
     if level < LEVELS - 1:
         keep = only((row % (2 * step) == 0) & (lane % (2 * step) == 0), 0.5)
         coarse = []
         for k in range(0, count, 2):
-            v = r[k] + r[k + 1]
-            v = v + pltpu.roll(v, 8 - step, 0)
-            coarse.append(keep * (v + pltpu.roll(v, LANES - step, 1)))
+            v = d2[k] + d2[k + 1]
+            beyond = added(at(d2, k - 1), at(d2, k + 2))
+            rest = before[k] + before[k + 1] - 5.0 * v
+            rest = rest if beyond is None else rest + beyond
+            along = [
+                v + moves(v, dim, 1) + (moves(v, dim, -1) + moves(v, dim, 2)) for dim in range(2)
+            ]
+            first = rest + moves(rest, 0, 1) + along[0]
+            coarse.append(keep * (
+                first + moves(first, 1, 1) + (along[1] + moves(along[1], 0, 1))
+            ))
         coarse, coarsest = small_cycle(level + 1, coarse)
-        e = []
+        e, beside = [], []
         for v in coarse:
-            v = v + pltpu.roll(v, step, 0)
-            e += [v + pltpu.roll(v, step, 1)] * 2
-        x = [v + t for v, t in zip(x, e)]
-        r = [v - t for v, t in zip(r, op(e))]
+            back = [moves(v, dim, -1) for dim in range(2)]
+            wide = v + back[0]
+            e.append(wide + moves(wide, 1, -1))
+            along = [
+                v + back[dim] + (moves(v, dim, 1) + moves(v, dim, -2)) for dim in range(2)
+            ]
+            beside.append(
+                along[0] + moves(along[0], 1, -1) + (along[1] + moves(along[1], 0, -1))
+            )
+        for k in range(count):
+            own = e[k // 2]
+            change = 5.0 * own - beside[k // 2]
+            beyond = at(e, k // 2 + (1 if k % 2 else -1))
+            if beyond is not None:
+                change = change - beyond
+            x[k] = x[k] + own
+            r[k] = r[k] - change
     d = [first_scale * v for v in r]
     r = [v - t for v, t in zip(r, op(d))]
     x = [v + (t + (carry_coef * t + fresh_coef * u)) for v, t, u in zip(x, d, r)]

time: 29.3 us -> 29 us (0.990)
  Pallas kernels: 7.22 us -> 6.89 us
    pallas_call x4, Pallas kernels: 7.22 us -> 6.89 us  [run(): pl.pallas_call(functools.partial(kernel, plan), out_shape=[whole(s) for s...]
where the time goes in v11:
time: 29 us; the launch traced here: 28.9 us
  waiting for transfers between devices  10.4 us (36%)
  starting transfers between devices  9.75 us (34%)
  Pallas kernels  6.89 us (24%)
  other arithmetic  1.04 us (4%)
  between operations  0.7 us (2%)
    ppermute x7, waiting for transfers between devices, swap(): return lax.ppermute(values, axes, pairs)  10.4 us
    ppermute x7, starting transfers between devices, swap(): return lax.ppermute(values, axes, pairs)  9.75 us
    pallas_call x4, Pallas kernels, run(): pl.pallas_call(functools.partial(kernel, plan), out_shape=[whole(s) for s...  6.89 us
    another operation x1, other arithmetic, body_fast(): both = jnp.stack([pressure_prev, divergence])  1.04 us
  transfers between devices with their start and end apart: 7, of which 3 were waited for; matrix products, arithmetic and copies ran while one was open for 0% of the time, Pallas kernels for 0%

profile of v11, /device:TPU:0, one launch (start us, length us, event | category | flops | bytes accessed | tf_op | source)
XLA Modules:
  0.0 28.9 jit_solution(18008293373433939353)
XLA Ops:
  0.6 1.0 %select_maximum_fusion.both = f32[2,22,24,256]{3,2,1,0:T(8,128)S(1)} fusion(f32[1,16,16,128]{3,2,1,0:T(8,128)} %bitcast.2, f32[1,16,16,128]{3,2,1,0:T(8,128)} %bitcast.3), kind=kLoop, calls=%fused_computation.2 | loop fusion | flops 3784704 | bytes 1343488 | tf_op jit(solution)/shard_map/stack | solution.py:1003
  1.7 1.3 %shard_map.49 = (f32[22,24,256]{2,1,0:T(8,128)S(1)}, f32[22,24,256]{2,1,0:T(8,128)S(1)}, f32[224,128]{1,0:T(8,128)S(1)}, f32[248,128]{1,0:T(8,128)S(1)}, f32[128,128]{1,0:T(8,128)S(1)}) custom-call(f32[2,22,24,256]{3,2,1,0:T(8,128)S(1)} %select_maximum_fusion.both), custom_call_target="tpu_custom_call" | custom-call | tf_op jit(solution)/shard_map/pallas_call | solution.py:977
  2.9 3.0 %collective-permute-start.1 = (f32[248,128]{1,0:T(8,128)S(1)}, f32[248,128]{1,0:T(8,128)S(1)}, u32[]{:S(2)}, u32[]{:S(2)}) collective-permute-start(f32[248,128]{1,0:T(8,128)S(1)} %get-tuple-element.21), channel_id=1, source_target_pairs={{0,16},{1,17},{2,18},{3,19},{4,20},{5,21},{6,22},{7,23},{8,24},{9,... | collective-permute-start | bytes 380936 | tf_op jit(solution)/shard_map/ppermute | solution.py:995
  6.0 0.6 %collective-permute-start = (f32[224,128]{1,0:T(8,128)S(1)}, f32[224,128]{1,0:T(8,128)S(1)}, u32[]{:S(2)}, u32[]{:S(2)}) collective-permute-start(f32[224,128]{1,0:T(8,128)S(1)} %get-tuple-element.20), channel_id=1, source_target_pairs={{0,3},{1,2},{2,1},{3,0},{4,7},{5,6},{6,5},{7,4},{8,11},{9,10},{10,... | collective-permute-start | bytes 344072 | tf_op jit(solution)/shard_map/ppermute | solution.py:995
  6.6 0.6 %collective-permute-start.2 = (f32[128,128]{1,0:T(8,128)S(1)}, f32[128,128]{1,0:T(8,128)S(1)}, u32[]{:S(2)}, u32[]{:S(2)}) collective-permute-start(f32[128,128]{1,0:T(8,128)S(1)} %get-tuple-element.22), channel_id=1, source_target_pairs={{0,19},{1,18},{2,17},{3,16},{4,23},{5,22},{6,21},{7,20},{8,27},{9,... | collective-permute-start | bytes 196616 | tf_op jit(solution)/shard_map/ppermute | solution.py:995
  7.2 4.4 %collective-permute-done.2.from_d = f32[128,128]{1,0:T(8,128)S(1)} collective-permute-done((f32[128,128]{1,0:T(8,128)S(1)}, f32[128,128]{1,0:T(8,128)S(1)}, u32[]{:S(2)}, u32[]{:S(2)}) %collective-permute-start.2) | collective-permute-done | bytes 65568 | tf_op jit(solution)/shard_map/ppermute | solution.py:995
  11.6 0.0 collective-permute-done.from_z
  11.6 0.0 collective-permute-done.1.from_x
  11.6 0.2 shard_map.50
  12.0 0.7 %collective-permute-start.3 = (f32[512,128]{1,0:T(8,128)S(1)}, f32[512,128]{1,0:T(8,128)S(1)}, u32[]{:S(2)}, u32[]{:S(2)}) collective-permute-start(f32[512,128]{1,0:T(8,128)S(1)} %slice_dynamic-update-slice_fusion.ours), channel_id=1, source_target_pairs={{0,1},{1,0},{2,3},{3,2},{4,5},{5,4},{6,7},{7,6},{8,9},{9,8},{10,11... | collective-permute-start | bytes 786440 | tf_op jit(solution)/shard_map/ppermute | solution.py:995
  12.6 1.2 %collective-permute-done.3.theirs = f32[512,128]{1,0:T(8,128)S(1)} collective-permute-done((f32[512,128]{1,0:T(8,128)S(1)}, f32[512,128]{1,0:T(8,128)S(1)}, u32[]{:S(2)}, u32[]{:S(2)}) %collective-permute-start.3) | collective-permute-done | bytes 262176 | tf_op jit(solution)/shard_map/ppermute | solution.py:995
  13.8 1.3 %shard_map.51 = (f32[20,24,256]{2,1,0:T(8,128)S(1)}, f32[16,16,128]{2,1,0:T(8,128)S(1)}, f32[16,16,128]{2,1,0:T(8,128)S(1)}, f32[16,16,128]{2,1,0:T(8,128)S(1)},...) custom-call(f32[22,24,256]{2,1,0:T(8,128)S(1)} %get-tuple-element.23.r_in, ...), custom_call_target="tpu_custom_call" | custom-call | tf_op jit(solution)/shard_map/pallas_call | solution.py:977
  15.1 2.2 %collective-permute-start.4 = (f32[104,128]{1,0:T(8,128)S(1)}, f32[104,128]{1,0:T(8,128)S(1)}, u32[]{:S(2)}, u32[]{:S(2)}) collective-permute-start(f32[104,128]{1,0:T(8,128)S(1)} %get-tuple-element.31), channel_id=1, source_target_pairs={{0,4},{1,5},{2,6},{3,7},{4,0},{5,1},{6,2},{7,3},{8,12},{9,13},{10,... | collective-permute-start | bytes 159752 | tf_op jit(solution)/shard_map/ppermute | solution.py:995
  17.3 2.5 %collective-permute-start.5 = (f32[104,128]{1,0:T(8,128)S(1)}, f32[104,128]{1,0:T(8,128)S(1)}, u32[]{:S(2)}, u32[]{:S(2)}) collective-permute-start(f32[104,128]{1,0:T(8,128)S(1)} %get-tuple-element.32), channel_id=1, source_target_pairs={{0,12},{1,13},{2,14},{3,15},{4,8},{5,9},{6,10},{7,11},{8,4},{9,5},... | collective-permute-start | bytes 159752 | tf_op jit(solution)/shard_map/ppermute | solution.py:995
  19.8 0.1 collective-permute-start.6
  19.9 4.9 %collective-permute-done.6.from_c = f32[48,128]{1,0:T(8,128)S(1)} collective-permute-done((f32[48,128]{1,0:T(8,128)S(1)}, f32[48,128]{1,0:T(8,128)S(1)}, u32[]{:S(2)}, u32[]{:S(2)}) %collective-permute-start.6) | collective-permute-done | bytes 24608 | tf_op jit(solution)/shard_map/ppermute | solution.py:995
  24.8 0.0 collective-permute-done.4.from_a
  24.8 0.0 collective-permute-done.5.from_b
  24.8 4.1 %shard_map.52 = (f32[16,16,128]{2,1,0:T(8,128)}, f32[16,16,128]{2,1,0:T(8,128)}, f32[2,1,16]{2,1,0:T(1,128)}) custom-call(f32[20,24,256]{2,1,0:T(8,128)S(1)} %get-tuple-element.26.r_in, f32[16,16,128]{2,1,0:T(8,128)S(1)} %get-tuple-element.27.x_in, f32[16,16,128]{2,1,0:T(8,128)S(1)} %get-tuple-element.28.r1_in, f32[16,16,128]{2,1,0:T(8,128)S(1)} %get-tuple-element.29.x1_in, ...), custom_call_target="tpu_custom_call" | custom-call | tf_op jit(solution)/shard_map/pallas_call | solution.py:977
  (5 shorter events, 0.0 us)
Async XLA Ops:
  2.9 8.7 %collective-permute-start.1 = (f32[248,128]{1,0:T(8,128)S(1)}, f32[248,128]{1,0:T(8,128)S(1)}, u32[]{:S(2)}, u32[]{:S(2)}) collective-permute-start(f32[248,128]{1,0:T(8,128)S(1)} %get-tuple-element.21), channel_id=1, source_target_pairs={{0,16},{1,17},{2,18},{3,19},{4,20},{5,21},{6,22},{7,23},{8,24},{9,... | collective-permute-start | bytes 380936 | tf_op jit(solution)/shard_map/ppermute | solution.py:995
  6.0 5.7 %collective-permute-start = (f32[224,128]{1,0:T(8,128)S(1)}, f32[224,128]{1,0:T(8,128)S(1)}, u32[]{:S(2)}, u32[]{:S(2)}) collective-permute-start(f32[224,128]{1,0:T(8,128)S(1)} %get-tuple-element.20), channel_id=1, source_target_pairs={{0,3},{1,2},{2,1},{3,0},{4,7},{5,6},{6,5},{7,4},{8,11},{9,10},{10,... | collective-permute-start | bytes 344072 | tf_op jit(solution)/shard_map/ppermute | solution.py:995
  6.6 5.0 %collective-permute-start.2 = (f32[128,128]{1,0:T(8,128)S(1)}, f32[128,128]{1,0:T(8,128)S(1)}, u32[]{:S(2)}, u32[]{:S(2)}) collective-permute-start(f32[128,128]{1,0:T(8,128)S(1)} %get-tuple-element.22), channel_id=1, source_target_pairs={{0,19},{1,18},{2,17},{3,16},{4,23},{5,22},{6,21},{7,20},{8,27},{9,... | collective-permute-start | bytes 196616 | tf_op jit(solution)/shard_map/ppermute | solution.py:995
  12.0 1.8 %collective-permute-start.3 = (f32[512,128]{1,0:T(8,128)S(1)}, f32[512,128]{1,0:T(8,128)S(1)}, u32[]{:S(2)}, u32[]{:S(2)}) collective-permute-start(f32[512,128]{1,0:T(8,128)S(1)} %slice_dynamic-update-slice_fusion.ours), channel_id=1, source_target_pairs={{0,1},{1,0},{2,3},{3,2},{4,5},{5,4},{6,7},{7,6},{8,9},{9,8},{10,11... | collective-permute-start | bytes 786440 | tf_op jit(solution)/shard_map/ppermute | solution.py:995
  15.1 9.7 %collective-permute-start.4 = (f32[104,128]{1,0:T(8,128)S(1)}, f32[104,128]{1,0:T(8,128)S(1)}, u32[]{:S(2)}, u32[]{:S(2)}) collective-permute-start(f32[104,128]{1,0:T(8,128)S(1)} %get-tuple-element.31), channel_id=1, source_target_pairs={{0,4},{1,5},{2,6},{3,7},{4,0},{5,1},{6,2},{7,3},{8,12},{9,13},{10,... | collective-permute-start | bytes 159752 | tf_op jit(solution)/shard_map/ppermute | solution.py:995
  17.3 7.5 %collective-permute-start.5 = (f32[104,128]{1,0:T(8,128)S(1)}, f32[104,128]{1,0:T(8,128)S(1)}, u32[]{:S(2)}, u32[]{:S(2)}) collective-permute-start(f32[104,128]{1,0:T(8,128)S(1)} %get-tuple-element.32), channel_id=1, source_target_pairs={{0,12},{1,13},{2,14},{3,15},{4,8},{5,9},{6,10},{7,11},{8,4},{9,5},... | collective-permute-start | bytes 159752 | tf_op jit(solution)/shard_map/ppermute | solution.py:995
  19.8 5.0 %collective-permute-start.6 = (f32[48,128]{1,0:T(8,128)S(1)}, f32[48,128]{1,0:T(8,128)S(1)}, u32[]{:S(2)}, u32[]{:S(2)}) collective-permute-start(f32[48,128]{1,0:T(8,128)S(1)} %get-tuple-element.30.ours), channel_id=1, source_target_pairs={{0,8},{1,9},{2,10},{3,11},{4,12},{5,13},{6,14},{7,15},{8,0},{9,1},... | collective-permute-start | bytes 73736 | tf_op jit(solution)/shard_map/ppermute | solution.py:995

commit v12 on v11

--- a/solution.py
+++ b/solution.py
@@ -719,10 +719,52 @@
     return beside
 
 
+def line_cycle(source, step):
+    lane = iota((8, LANES), 1)
+    count = len(source)
+
+    def inside(s, v):
+        if s == 0:
+            return v
+        return only(lane < LANES - s * step if s > 0 else lane >= -s * step, v)
+
+    def op(v, width):
+        out = {}
+        for s in range(-width, width + 1):
+            out[s] = []
+            for k in range(count):
+                beside = v[s - 1][k] + v[s + 1][k]
+                if k > 0:
+                    beside = beside + v[s][k - 1]
+                if k < count - 1:
+                    beside = beside + v[s][k + 1]
+                out[s].append(inside(s, 6.0 * v[s][k] - beside))
+        return out
+
+    def mix(width, *terms):
+        return {
+            s: [sum(c * v[s][k] for c, v in terms) for k in range(count)]
+            for s in range(-width, width + 1)
+        }
+
+    b = {s: [inside(s, shifted(v, -s * step)) for v in source] for s in range(-3, 4)}
+    d = mix(3, (first_scale, b))
+    r = mix(2, (1.0, b), (-1.0, op(d, 2)))
+    d2 = mix(2, (carry_coef, d), (fresh_coef, r))
+    x = mix(0, (1.0, d), (1.0, d2))
+    r = mix(1, (1.0, r), (-1.0, op(d2, 1)))
+    d = mix(1, (first_scale, r))
+    r = mix(0, (1.0, r), (-1.0, op(d, 0)))
+    x = mix(0, (1.0, x), (1.0 + carry_coef, d), (fresh_coef, r))[0]
+    return x, x
+
+
 def small_cycle(level, source):
     step = 1 << (level - 2)
     row, lane = iota((8, LANES), 0), iota((8, LANES), 1)
     count = len(source)
+    if level == LEVELS - 1 and step >= 8:
+        return line_cycle(source, step)
     shifts = []
     if step < 8:
         shifts += [(step, 0, row >= step), (8 - step, 0, row < 8 - step)]

time: 29 us -> 28.9 us (level)
  no operation moved by 1% of the time
where the time goes in v12:
time: 28.9 us; the launch traced here: 28.8 us
  waiting for transfers between devices  10.4 us (36%)
  starting transfers between devices  9.75 us (34%)
  Pallas kernels  6.78 us (23%)
  other arithmetic  1.04 us (4%)
  between operations  0.7 us (2%)
    ppermute x7, waiting for transfers between devices, swap(): return lax.ppermute(values, axes, pairs)  10.4 us
    ppermute x7, starting transfers between devices, swap(): return lax.ppermute(values, axes, pairs)  9.75 us
    pallas_call x4, Pallas kernels, run(): pl.pallas_call(functools.partial(kernel, plan), out_shape=[whole(s) for s...  6.78 us
    another operation x1, other arithmetic, body_fast(): both = jnp.stack([pressure_prev, divergence])  1.04 us
  transfers between devices with their start and end apart: 7, of which 3 were waited for; matrix products, arithmetic and copies ran while one was open for 0% of the time, Pallas kernels for 0%

profile of v12, /device:TPU:0, one launch (start us, length us, event | category | flops | bytes accessed | tf_op | source)
XLA Modules:
  0.0 28.8 jit_solution(5493119429209258766)
XLA Ops:
  0.6 1.0 %select_maximum_fusion.both = f32[2,22,24,256]{3,2,1,0:T(8,128)S(1)} fusion(f32[1,16,16,128]{3,2,1,0:T(8,128)} %bitcast.2, f32[1,16,16,128]{3,2,1,0:T(8,128)} %bitcast.3), kind=kLoop, calls=%fused_computation.2 | loop fusion | flops 3784704 | bytes 1343488 | tf_op jit(solution)/shard_map/stack | solution.py:1045
  1.7 1.3 %shard_map.49 = (f32[22,24,256]{2,1,0:T(8,128)S(1)}, f32[22,24,256]{2,1,0:T(8,128)S(1)}, f32[224,128]{1,0:T(8,128)S(1)}, f32[248,128]{1,0:T(8,128)S(1)}, f32[128,128]{1,0:T(8,128)S(1)}) custom-call(f32[2,22,24,256]{3,2,1,0:T(8,128)S(1)} %select_maximum_fusion.both), custom_call_target="tpu_custom_call" | custom-call | tf_op jit(solution)/shard_map/pallas_call | solution.py:1019
  2.9 3.0 %collective-permute-start.1 = (f32[248,128]{1,0:T(8,128)S(1)}, f32[248,128]{1,0:T(8,128)S(1)}, u32[]{:S(2)}, u32[]{:S(2)}) collective-permute-start(f32[248,128]{1,0:T(8,128)S(1)} %get-tuple-element.21), channel_id=1, source_target_pairs={{0,16},{1,17},{2,18},{3,19},{4,20},{5,21},{6,22},{7,23},{8,24},{9,... | collective-permute-start | bytes 380936 | tf_op jit(solution)/shard_map/ppermute | solution.py:1037
  6.0 0.6 %collective-permute-start = (f32[224,128]{1,0:T(8,128)S(1)}, f32[224,128]{1,0:T(8,128)S(1)}, u32[]{:S(2)}, u32[]{:S(2)}) collective-permute-start(f32[224,128]{1,0:T(8,128)S(1)} %get-tuple-element.20), channel_id=1, source_target_pairs={{0,3},{1,2},{2,1},{3,0},{4,7},{5,6},{6,5},{7,4},{8,11},{9,10},{10,... | collective-permute-start | bytes 344072 | tf_op jit(solution)/shard_map/ppermute | solution.py:1037
  6.6 0.6 %collective-permute-start.2 = (f32[128,128]{1,0:T(8,128)S(1)}, f32[128,128]{1,0:T(8,128)S(1)}, u32[]{:S(2)}, u32[]{:S(2)}) collective-permute-start(f32[128,128]{1,0:T(8,128)S(1)} %get-tuple-element.22), channel_id=1, source_target_pairs={{0,19},{1,18},{2,17},{3,16},{4,23},{5,22},{6,21},{7,20},{8,27},{9,... | collective-permute-start | bytes 196616 | tf_op jit(solution)/shard_map/ppermute | solution.py:1037
  7.2 4.4 %collective-permute-done.2.from_d = f32[128,128]{1,0:T(8,128)S(1)} collective-permute-done((f32[128,128]{1,0:T(8,128)S(1)}, f32[128,128]{1,0:T(8,128)S(1)}, u32[]{:S(2)}, u32[]{:S(2)}) %collective-permute-start.2) | collective-permute-done | bytes 65568 | tf_op jit(solution)/shard_map/ppermute | solution.py:1037
  11.6 0.0 collective-permute-done.from_z
  11.6 0.0 collective-permute-done.1.from_x
  11.6 0.2 shard_map.50
  12.0 0.7 %collective-permute-start.3 = (f32[512,128]{1,0:T(8,128)S(1)}, f32[512,128]{1,0:T(8,128)S(1)}, u32[]{:S(2)}, u32[]{:S(2)}) collective-permute-start(f32[512,128]{1,0:T(8,128)S(1)} %slice_dynamic-update-slice_fusion.ours), channel_id=1, source_target_pairs={{0,1},{1,0},{2,3},{3,2},{4,5},{5,4},{6,7},{7,6},{8,9},{9,8},{10,11... | collective-permute-start | bytes 786440 | tf_op jit(solution)/shard_map/ppermute | solution.py:1037
  12.6 1.2 %collective-permute-done.3.theirs = f32[512,128]{1,0:T(8,128)S(1)} collective-permute-done((f32[512,128]{1,0:T(8,128)S(1)}, f32[512,128]{1,0:T(8,128)S(1)}, u32[]{:S(2)}, u32[]{:S(2)}) %collective-permute-start.3) | collective-permute-done | bytes 262176 | tf_op jit(solution)/shard_map/ppermute | solution.py:1037
  13.8 1.3 %shard_map.51 = (f32[20,24,256]{2,1,0:T(8,128)S(1)}, f32[16,16,128]{2,1,0:T(8,128)S(1)}, f32[16,16,128]{2,1,0:T(8,128)S(1)}, f32[16,16,128]{2,1,0:T(8,128)S(1)},...) custom-call(f32[22,24,256]{2,1,0:T(8,128)S(1)} %get-tuple-element.23.r_in, ...), custom_call_target="tpu_custom_call" | custom-call | tf_op jit(solution)/shard_map/pallas_call | solution.py:1019
  15.1 2.2 %collective-permute-start.4 = (f32[104,128]{1,0:T(8,128)S(1)}, f32[104,128]{1,0:T(8,128)S(1)}, u32[]{:S(2)}, u32[]{:S(2)}) collective-permute-start(f32[104,128]{1,0:T(8,128)S(1)} %get-tuple-element.31), channel_id=1, source_target_pairs={{0,4},{1,5},{2,6},{3,7},{4,0},{5,1},{6,2},{7,3},{8,12},{9,13},{10,... | collective-permute-start | bytes 159752 | tf_op jit(solution)/shard_map/ppermute | solution.py:1037
  17.3 2.5 %collective-permute-start.5 = (f32[104,128]{1,0:T(8,128)S(1)}, f32[104,128]{1,0:T(8,128)S(1)}, u32[]{:S(2)}, u32[]{:S(2)}) collective-permute-start(f32[104,128]{1,0:T(8,128)S(1)} %get-tuple-element.32), channel_id=1, source_target_pairs={{0,12},{1,13},{2,14},{3,15},{4,8},{5,9},{6,10},{7,11},{8,4},{9,5},... | collective-permute-start | bytes 159752 | tf_op jit(solution)/shard_map/ppermute | solution.py:1037
  19.8 0.1 collective-permute-start.6
  19.9 4.9 %collective-permute-done.6.from_c = f32[48,128]{1,0:T(8,128)S(1)} collective-permute-done((f32[48,128]{1,0:T(8,128)S(1)}, f32[48,128]{1,0:T(8,128)S(1)}, u32[]{:S(2)}, u32[]{:S(2)}) %collective-permute-start.6) | collective-permute-done | bytes 24608 | tf_op jit(solution)/shard_map/ppermute | solution.py:1037
  24.8 0.0 collective-permute-done.4.from_a
  24.8 0.0 collective-permute-done.5.from_b
  24.8 4.0 %shard_map.52 = (f32[16,16,128]{2,1,0:T(8,128)}, f32[16,16,128]{2,1,0:T(8,128)}, f32[2,1,16]{2,1,0:T(1,128)}) custom-call(f32[20,24,256]{2,1,0:T(8,128)S(1)} %get-tuple-element.26.r_in, f32[16,16,128]{2,1,0:T(8,128)S(1)} %get-tuple-element.27.x_in, f32[16,16,128]{2,1,0:T(8,128)S(1)} %get-tuple-element.28.r1_in, f32[16,16,128]{2,1,0:T(8,128)S(1)} %get-tuple-element.29.x1_in, ...), custom_call_target="tpu_custom_call" | custom-call | tf_op jit(solution)/shard_map/pallas_call | solution.py:1019
  (5 shorter events, 0.0 us)
Async XLA Ops:
  2.9 8.7 %collective-permute-start.1 = (f32[248,128]{1,0:T(8,128)S(1)}, f32[248,128]{1,0:T(8,128)S(1)}, u32[]{:S(2)}, u32[]{:S(2)}) collective-permute-start(f32[248,128]{1,0:T(8,128)S(1)} %get-tuple-element.21), channel_id=1, source_target_pairs={{0,16},{1,17},{2,18},{3,19},{4,20},{5,21},{6,22},{7,23},{8,24},{9,... | collective-permute-start | bytes 380936 | tf_op jit(solution)/shard_map/ppermute | solution.py:1037
  6.0 5.7 %collective-permute-start = (f32[224,128]{1,0:T(8,128)S(1)}, f32[224,128]{1,0:T(8,128)S(1)}, u32[]{:S(2)}, u32[]{:S(2)}) collective-permute-start(f32[224,128]{1,0:T(8,128)S(1)} %get-tuple-element.20), channel_id=1, source_target_pairs={{0,3},{1,2},{2,1},{3,0},{4,7},{5,6},{6,5},{7,4},{8,11},{9,10},{10,... | collective-permute-start | bytes 344072 | tf_op jit(solution)/shard_map/ppermute | solution.py:1037
  6.6 5.0 %collective-permute-start.2 = (f32[128,128]{1,0:T(8,128)S(1)}, f32[128,128]{1,0:T(8,128)S(1)}, u32[]{:S(2)}, u32[]{:S(2)}) collective-permute-start(f32[128,128]{1,0:T(8,128)S(1)} %get-tuple-element.22), channel_id=1, source_target_pairs={{0,19},{1,18},{2,17},{3,16},{4,23},{5,22},{6,21},{7,20},{8,27},{9,... | collective-permute-start | bytes 196616 | tf_op jit(solution)/shard_map/ppermute | solution.py:1037
  12.0 1.8 %collective-permute-start.3 = (f32[512,128]{1,0:T(8,128)S(1)}, f32[512,128]{1,0:T(8,128)S(1)}, u32[]{:S(2)}, u32[]{:S(2)}) collective-permute-start(f32[512,128]{1,0:T(8,128)S(1)} %slice_dynamic-update-slice_fusion.ours), channel_id=1, source_target_pairs={{0,1},{1,0},{2,3},{3,2},{4,5},{5,4},{6,7},{7,6},{8,9},{9,8},{10,11... | collective-permute-start | bytes 786440 | tf_op jit(solution)/shard_map/ppermute | solution.py:1037
  15.1 9.7 %collective-permute-start.4 = (f32[104,128]{1,0:T(8,128)S(1)}, f32[104,128]{1,0:T(8,128)S(1)}, u32[]{:S(2)}, u32[]{:S(2)}) collective-permute-start(f32[104,128]{1,0:T(8,128)S(1)} %get-tuple-element.31), channel_id=1, source_target_pairs={{0,4},{1,5},{2,6},{3,7},{4,0},{5,1},{6,2},{7,3},{8,12},{9,13},{10,... | collective-permute-start | bytes 159752 | tf_op jit(solution)/shard_map/ppermute | solution.py:1037
  17.3 7.5 %collective-permute-start.5 = (f32[104,128]{1,0:T(8,128)S(1)}, f32[104,128]{1,0:T(8,128)S(1)}, u32[]{:S(2)}, u32[]{:S(2)}) collective-permute-start(f32[104,128]{1,0:T(8,128)S(1)} %get-tuple-element.32), channel_id=1, source_target_pairs={{0,12},{1,13},{2,14},{3,15},{4,8},{5,9},{6,10},{7,11},{8,4},{9,5},... | collective-permute-start | bytes 159752 | tf_op jit(solution)/shard_map/ppermute | solution.py:1037
  19.8 5.0 %collective-permute-start.6 = (f32[48,128]{1,0:T(8,128)S(1)}, f32[48,128]{1,0:T(8,128)S(1)}, u32[]{:S(2)}, u32[]{:S(2)}) collective-permute-start(f32[48,128]{1,0:T(8,128)S(1)} %get-tuple-element.30.ours), channel_id=1, source_target_pairs={{0,8},{1,9},{2,10},{3,11},{4,12},{5,13},{6,14},{7,15},{8,0},{9,1},... | collective-permute-start | bytes 73736 | tf_op jit(solution)/shard_map/ppermute | solution.py:1037

commit v13 on v12

--- a/solution.py
+++ b/solution.py
@@ -313,7 +313,7 @@
     at = 7 * bx
     out[at:at + 8, :] = tiles[0]
     out[at + 8:at + 16, :] = tiles[1]
-    out[at + 16:at + 16 + bx, :] = lat
+    out[at + 16:at + 24, :] = lat[0:8] + shifted(lat[8:16], LANES // 2)
     for j in (1, 2, 3):
         ref, k = layers[j]
         out[at + 16:at + 24, :] += side_pack(ref[k, bx:, LANES:], 6 + j)
@@ -323,7 +323,8 @@
     bx = r_ref.shape[1] - 8
     layers = slab_there(r_ref, x_ref, up)
     at = 7 * bx
-    lat = slab[at + 16:at + 16 + bx, :]
+    lat = slab[at + 16:at + 24, :]
+    lat = jnp.concatenate([lat, shifted(lat, LANES // 2)], axis=0)
     for j, (ref, k) in enumerate(layers):
         ref[k, 0:bx, 0:LANES] += slab[j * bx:(j + 1) * bx, :]
         ref[k, 0:bx, LANES:] += side_unpack(lat, j)
@@ -411,7 +412,7 @@
         self.lat_at = self.pairs * (self.rows + 4)
         self.coarse = self.lat_at + 8
         self.slab = 8 * self.ex
-        self.slab_z = 8 * bx + 16
+        self.slab_z = 7 * bx + 24
         self.slab_x = 8 * (bz + 5)
         self.corner = 6 * 8
         self.layers = bz + 4

time: 28.9 us -> 28.8 us (level)
  no operation moved by 1% of the time
where the time goes in v13:
time: 28.8 us; the launch traced here: 28.6 us
  waiting for transfers between devices  10.4 us (36%)
  starting transfers between devices  9.68 us (34%)
  Pallas kernels  6.83 us (24%)
  other arithmetic  1.04 us (4%)
  between operations  0.7 us (2%)
    ppermute x7, waiting for transfers between devices, swap(): return lax.ppermute(values, axes, pairs)  10.4 us
    ppermute x7, starting transfers between devices, swap(): return lax.ppermute(values, axes, pairs)  9.68 us
    pallas_call x4, Pallas kernels, run(): pl.pallas_call(functools.partial(kernel, plan), out_shape=[whole(s) for s...  6.83 us
    another operation x1, other arithmetic, body_fast(): both = jnp.stack([pressure_prev, divergence])  1.04 us
  transfers between devices with their start and end apart: 7, of which 3 were waited for; matrix products, arithmetic and copies ran while one was open for 0% of the time, Pallas kernels for 0%

profile of v13, /device:TPU:0, one launch (start us, length us, event | category | flops | bytes accessed | tf_op | source)
XLA Modules:
  0.0 28.6 jit_solution(14534556885386803836)
XLA Ops:
  0.6 1.0 %select_maximum_fusion.both = f32[2,22,24,256]{3,2,1,0:T(8,128)S(1)} fusion(f32[1,16,16,128]{3,2,1,0:T(8,128)} %bitcast.2, f32[1,16,16,128]{3,2,1,0:T(8,128)} %bitcast.3), kind=kLoop, calls=%fused_computation.2 | loop fusion | flops 3784704 | bytes 1343488 | tf_op jit(solution)/shard_map/stack | solution.py:1046
  1.7 1.3 %shard_map.49 = (f32[22,24,256]{2,1,0:T(8,128)S(1)}, f32[22,24,256]{2,1,0:T(8,128)S(1)}, f32[216,128]{1,0:T(8,128)S(1)}, f32[248,128]{1,0:T(8,128)S(1)}, f32[128,128]{1,0:T(8,128)S(1)}) custom-call(f32[2,22,24,256]{3,2,1,0:T(8,128)S(1)} %select_maximum_fusion.both), custom_call_target="tpu_custom_call" | custom-call | tf_op jit(solution)/shard_map/pallas_call | solution.py:1020
  3.0 3.0 %collective-permute-start.1 = (f32[248,128]{1,0:T(8,128)S(1)}, f32[248,128]{1,0:T(8,128)S(1)}, u32[]{:S(2)}, u32[]{:S(2)}) collective-permute-start(f32[248,128]{1,0:T(8,128)S(1)} %get-tuple-element.21), channel_id=1, source_target_pairs={{0,16},{1,17},{2,18},{3,19},{4,20},{5,21},{6,22},{7,23},{8,24},{9,... | collective-permute-start | bytes 380936 | tf_op jit(solution)/shard_map/ppermute | solution.py:1038
  6.0 0.6 %collective-permute-start = (f32[216,128]{1,0:T(8,128)S(1)}, f32[216,128]{1,0:T(8,128)S(1)}, u32[]{:S(2)}, u32[]{:S(2)}) collective-permute-start(f32[216,128]{1,0:T(8,128)S(1)} %get-tuple-element.20), channel_id=1, source_target_pairs={{0,3},{1,2},{2,1},{3,0},{4,7},{5,6},{6,5},{7,4},{8,11},{9,10},{10,... | collective-permute-start | bytes 331784 | tf_op jit(solution)/shard_map/ppermute | solution.py:1038
  6.6 0.6 %collective-permute-start.2 = (f32[128,128]{1,0:T(8,128)S(1)}, f32[128,128]{1,0:T(8,128)S(1)}, u32[]{:S(2)}, u32[]{:S(2)}) collective-permute-start(f32[128,128]{1,0:T(8,128)S(1)} %get-tuple-element.22), channel_id=1, source_target_pairs={{0,19},{1,18},{2,17},{3,16},{4,23},{5,22},{6,21},{7,20},{8,27},{9,... | collective-permute-start | bytes 196616 | tf_op jit(solution)/shard_map/ppermute | solution.py:1038
  7.3 4.3 %collective-permute-done.2.from_d = f32[128,128]{1,0:T(8,128)S(1)} collective-permute-done((f32[128,128]{1,0:T(8,128)S(1)}, f32[128,128]{1,0:T(8,128)S(1)}, u32[]{:S(2)}, u32[]{:S(2)}) %collective-permute-start.2) | collective-permute-done | bytes 65568 | tf_op jit(solution)/shard_map/ppermute | solution.py:1038
  11.6 0.0 collective-permute-done.from_z
  11.6 0.0 collective-permute-done.1.from_x
  11.6 0.3 shard_map.50
  11.9 0.8 %collective-permute-start.3 = (f32[512,128]{1,0:T(8,128)S(1)}, f32[512,128]{1,0:T(8,128)S(1)}, u32[]{:S(2)}, u32[]{:S(2)}) collective-permute-start(f32[512,128]{1,0:T(8,128)S(1)} %slice_dynamic-update-slice_fusion.ours), channel_id=1, source_target_pairs={{0,1},{1,0},{2,3},{3,2},{4,5},{5,4},{6,7},{7,6},{8,9},{9,8},{10,11... | collective-permute-start | bytes 786440 | tf_op jit(solution)/shard_map/ppermute | solution.py:1038
  12.7 1.2 %collective-permute-done.3.theirs = f32[512,128]{1,0:T(8,128)S(1)} collective-permute-done((f32[512,128]{1,0:T(8,128)S(1)}, f32[512,128]{1,0:T(8,128)S(1)}, u32[]{:S(2)}, u32[]{:S(2)}) %collective-permute-start.3) | collective-permute-done | bytes 262176 | tf_op jit(solution)/shard_map/ppermute | solution.py:1038
  13.9 1.3 %shard_map.51 = (f32[20,24,256]{2,1,0:T(8,128)S(1)}, f32[16,16,128]{2,1,0:T(8,128)S(1)}, f32[16,16,128]{2,1,0:T(8,128)S(1)}, f32[16,16,128]{2,1,0:T(8,128)S(1)},...) custom-call(f32[22,24,256]{2,1,0:T(8,128)S(1)} %get-tuple-element.23.r_in, ...), custom_call_target="tpu_custom_call" | custom-call | tf_op jit(solution)/shard_map/pallas_call | solution.py:1020
  15.2 2.0 %collective-permute-start.4 = (f32[104,128]{1,0:T(8,128)S(1)}, f32[104,128]{1,0:T(8,128)S(1)}, u32[]{:S(2)}, u32[]{:S(2)}) collective-permute-start(f32[104,128]{1,0:T(8,128)S(1)} %get-tuple-element.31), channel_id=1, source_target_pairs={{0,4},{1,5},{2,6},{3,7},{4,0},{5,1},{6,2},{7,3},{8,12},{9,13},{10,... | collective-permute-start | bytes 159752 | tf_op jit(solution)/shard_map/ppermute | solution.py:1038
  17.2 2.5 %collective-permute-start.5 = (f32[104,128]{1,0:T(8,128)S(1)}, f32[104,128]{1,0:T(8,128)S(1)}, u32[]{:S(2)}, u32[]{:S(2)}) collective-permute-start(f32[104,128]{1,0:T(8,128)S(1)} %get-tuple-element.32), channel_id=1, source_target_pairs={{0,12},{1,13},{2,14},{3,15},{4,8},{5,9},{6,10},{7,11},{8,4},{9,5},... | collective-permute-start | bytes 159752 | tf_op jit(solution)/shard_map/ppermute | solution.py:1038
  19.7 0.1 collective-permute-start.6
  19.8 4.9 %collective-permute-done.6.from_c = f32[48,128]{1,0:T(8,128)S(1)} collective-permute-done((f32[48,128]{1,0:T(8,128)S(1)}, f32[48,128]{1,0:T(8,128)S(1)}, u32[]{:S(2)}, u32[]{:S(2)}) %collective-permute-start.6) | collective-permute-done | bytes 24608 | tf_op jit(solution)/shard_map/ppermute | solution.py:1038
  24.7 0.0 collective-permute-done.4.from_a
  24.7 0.0 collective-permute-done.5.from_b
  24.7 4.0 %shard_map.52 = (f32[16,16,128]{2,1,0:T(8,128)}, f32[16,16,128]{2,1,0:T(8,128)}, f32[2,1,16]{2,1,0:T(1,128)}) custom-call(f32[20,24,256]{2,1,0:T(8,128)S(1)} %get-tuple-element.26.r_in, f32[16,16,128]{2,1,0:T(8,128)S(1)} %get-tuple-element.27.x_in, f32[16,16,128]{2,1,0:T(8,128)S(1)} %get-tuple-element.28.r1_in, f32[16,16,128]{2,1,0:T(8,128)S(1)} %get-tuple-element.29.x1_in, ...), custom_call_target="tpu_custom_call" | custom-call | tf_op jit(solution)/shard_map/pallas_call | solution.py:1020
  (5 shorter events, 0.0 us)
Async XLA Ops:
  3.0 8.6 %collective-permute-start.1 = (f32[248,128]{1,0:T(8,128)S(1)}, f32[248,128]{1,0:T(8,128)S(1)}, u32[]{:S(2)}, u32[]{:S(2)}) collective-permute-start(f32[248,128]{1,0:T(8,128)S(1)} %get-tuple-element.21), channel_id=1, source_target_pairs={{0,16},{1,17},{2,18},{3,19},{4,20},{5,21},{6,22},{7,23},{8,24},{9,... | collective-permute-start | bytes 380936 | tf_op jit(solution)/shard_map/ppermute | solution.py:1038
  6.0 5.6 %collective-permute-start = (f32[216,128]{1,0:T(8,128)S(1)}, f32[216,128]{1,0:T(8,128)S(1)}, u32[]{:S(2)}, u32[]{:S(2)}) collective-permute-start(f32[216,128]{1,0:T(8,128)S(1)} %get-tuple-element.20), channel_id=1, source_target_pairs={{0,3},{1,2},{2,1},{3,0},{4,7},{5,6},{6,5},{7,4},{8,11},{9,10},{10,... | collective-permute-start | bytes 331784 | tf_op jit(solution)/shard_map/ppermute | solution.py:1038
  6.6 4.9 %collective-permute-start.2 = (f32[128,128]{1,0:T(8,128)S(1)}, f32[128,128]{1,0:T(8,128)S(1)}, u32[]{:S(2)}, u32[]{:S(2)}) collective-permute-start(f32[128,128]{1,0:T(8,128)S(1)} %get-tuple-element.22), channel_id=1, source_target_pairs={{0,19},{1,18},{2,17},{3,16},{4,23},{5,22},{6,21},{7,20},{8,27},{9,... | collective-permute-start | bytes 196616 | tf_op jit(solution)/shard_map/ppermute | solution.py:1038
  11.9 2.0 %collective-permute-start.3 = (f32[512,128]{1,0:T(8,128)S(1)}, f32[512,128]{1,0:T(8,128)S(1)}, u32[]{:S(2)}, u32[]{:S(2)}) collective-permute-start(f32[512,128]{1,0:T(8,128)S(1)} %slice_dynamic-update-slice_fusion.ours), channel_id=1, source_target_pairs={{0,1},{1,0},{2,3},{3,2},{4,5},{5,4},{6,7},{7,6},{8,9},{9,8},{10,11... | collective-permute-start | bytes 786440 | tf_op jit(solution)/shard_map/ppermute | solution.py:1038
  15.2 9.5 %collective-permute-start.4 = (f32[104,128]{1,0:T(8,128)S(1)}, f32[104,128]{1,0:T(8,128)S(1)}, u32[]{:S(2)}, u32[]{:S(2)}) collective-permute-start(f32[104,128]{1,0:T(8,128)S(1)} %get-tuple-element.31), channel_id=1, source_target_pairs={{0,4},{1,5},{2,6},{3,7},{4,0},{5,1},{6,2},{7,3},{8,12},{9,13},{10,... | collective-permute-start | bytes 159752 | tf_op jit(solution)/shard_map/ppermute | solution.py:1038
  17.2 7.5 %collective-permute-start.5 = (f32[104,128]{1,0:T(8,128)S(1)}, f32[104,128]{1,0:T(8,128)S(1)}, u32[]{:S(2)}, u32[]{:S(2)}) collective-permute-start(f32[104,128]{1,0:T(8,128)S(1)} %get-tuple-element.32), channel_id=1, source_target_pairs={{0,12},{1,13},{2,14},{3,15},{4,8},{5,9},{6,10},{7,11},{8,4},{9,5},... | collective-permute-start | bytes 159752 | tf_op jit(solution)/shard_map/ppermute | solution.py:1038
  19.7 5.0 %collective-permute-start.6 = (f32[48,128]{1,0:T(8,128)S(1)}, f32[48,128]{1,0:T(8,128)S(1)}, u32[]{:S(2)}, u32[]{:S(2)}) collective-permute-start(f32[48,128]{1,0:T(8,128)S(1)} %get-tuple-element.30.ours), channel_id=1, source_target_pairs={{0,8},{1,9},{2,10},{3,11},{4,12},{5,13},{6,14},{7,15},{8,0},{9,1},... | collective-permute-start | bytes 73736 | tf_op jit(solution)/shard_map/ppermute | solution.py:1038
